TPU v7x, 32 devices: a whole 2x2x4 slice. The times are simulated.
32 devices in a mesh: pts: 8 (over z, y), dp: 4 (over x, core).
Axes of the slice: x: 2, y: 2, z: 4, core: 2. Of those that a mesh axis runs over, the one named last changes fastest.
Arguments:
- features: bfloat16 [4, 8192, 256], P('dp', 'pts')
- hilbert_pos: int32 [4, 8192], P('dp', 'pts'), may hold values from 0 to 8191, as said below
- weight: bfloat16 [27, 256, 256], replicated, may hold values from -0.078125 to 0.078125
- neighbours: int32 [4, 16, 26], P('dp', 'pts'), may hold values from -1 to 15, as said below
- grad_out: bfloat16 [4, 8192, 256], P('dp', 'pts')
Outputs:
- conv_out: bfloat16 [4, 8192, 256], P('dp', 'pts')
- input_grad: bfloat16 [4, 8192, 256], P('dp', 'pts')
- weight_grad: bfloat16 [27, 256, 256], replicated
Inputs may be any that keep to these rules, and one draw needn't show every extreme that they name: Each crop's row is a permutation of 0 to 8191. A point at row r goes to Hilbert owner hilbert_pos // 1024, and (owner - r // 1024 + 8 / 2) mod 8 is below 8. One device sends at most 256 points to one owner, exactly 256 to some owner in every crop; within a crop every device sends the same number of points to the owner k places ahead, for each k. Entries are block numbers within the same crop or -1. The relation is symmetric: h is the neighbour of g in direction d exactly when g is the neighbour of h in direction 25 - d. A neighbour h of g satisfies 1 <= |h - g| <= 2, and some block has a neighbour exactly 2 blocks away in every crop. A neighbour h > g lies in one of the directions 13 to 25; for each block and each t, at most one of its neighbours is t blocks ahead of it and at most one t blocks behind it.
All inputs are finite; a program needn't handle non-finite values.
Results may differ from a plain program's by a relative error of at most 0.0015.
Values may be sent and summed in bfloat16 or wider, within the bound.
No kernel may reach another device: no remote copies, remote signals or barrier semaphores. Data moves between devices by JAX's collectives and lax.ppermute only.
A program may use at most 128 MiB of HBM per device.

v0:
```python
import functools

import jax
import jax.numpy as jnp
from jax import lax
from jax.experimental import pallas as pl
from jax.experimental.pallas import tpu as pltpu
from jax.sharding import PartitionSpec as P

BF = jnp.bfloat16
F32 = jnp.float32
I32 = jnp.int32
I16 = jnp.int16
C = 256
STEPS = (-2, -1, 1, 2)
HALF = 14
PART = 7
TAIL = 16
UNIT = PART * 16 + TAIL
TOP = 32760.0
MIB = 1 << 20


def dot(a, b):
    return lax.dot_general(a, b, (((1,), (0,)), ((), ())), preferred_element_type=F32)


def dot_nt(a, b):
    return lax.dot_general(a, b, (((1,), (1,)), ((), ())), preferred_element_type=F32)


def one_hot(index, key):
    return jnp.where(index == key, 1.0, 0.0).astype(BF)


def call(body, outs, args, smem=(), scratch=(), vmem=48, flops=0, moved=0):
    specs = [
        pl.BlockSpec(memory_space=pltpu.SMEM if i in smem else pltpu.VMEM)
        for i in range(len(args))
    ]
    shapes = [jax.ShapeDtypeStruct(s, d) for s, d in outs]
    return pl.pallas_call(
        body,
        out_shape=shapes,
        in_specs=specs,
        out_specs=[pl.BlockSpec(memory_space=pltpu.VMEM) for _ in shapes],
        scratch_shapes=list(scratch),
        compiler_params=pltpu.CompilerParams(vmem_limit_bytes=vmem * MIB),
        cost_estimate=pl.CostEstimate(flops=flops, bytes_accessed=moved, transcendentals=0),
    )(*args)


def pack_body(me_ref, pos_ref, x_ref, out_ref, *, count, window, cap, direct):
    rows = x_ref.shape[0]
    pos = pos_ref[...]
    owner = pos >> (rows.bit_length() - 1)
    local = pos & (rows - 1)
    if direct:
        chunk = owner
    else:
        chunk = (owner - me_ref[0] + window // 2) & (count - 1)
    member = (chunk == lax.broadcasted_iota(I32, (window, rows), 0)).astype(I32)
    lane = lax.broadcasted_iota(I32, (window, rows), 1)
    rank = member
    step = 1
    while step < rows:
        rank = rank + jnp.where(lane >= step, pltpu.roll(rank, step, 1), 0)
        step *= 2
    keys = jnp.where(member > 0, rank - 1, -1)
    line = lax.broadcasted_iota(I32, (TAIL, rows), 0)
    digits = jnp.where(line == 0, (local >> 5) + 1, jnp.where(line == 1, local & 31, 0))
    digits = digits.astype(F32).astype(BF)
    x = x_ref[...]
    slot = lax.broadcasted_iota(I32, (cap, rows), 0)
    for c in range(window):
        pick = one_hot(slot, keys[c : c + 1, :])
        out_ref[c, :cap, :] = dot(pick, x).astype(BF)
        tail = dot_nt(digits, pick)
        if cap < C:
            tail = jnp.concatenate([tail, jnp.zeros((TAIL, C - cap), F32)], axis=1)
        out_ref[c, cap : cap + TAIL, :] = tail.astype(BF)


def faces_of(rows_of, skey_ref, up_ref, down_ref, local_ref):
    slot = lax.broadcasted_iota(I32, (64, 512), 0)
    made = {}
    for g in range(2):
        rows = rows_of(g)
        pick = jnp.concatenate(
            [one_hot(slot, skey_ref[g * 4 + n : g * 4 + n + 1, :]) for n in range(4)], axis=0
        )
        face = dot(pick, rows).astype(BF)
        for n, t in enumerate(STEPS):
            made[g, t] = face[n * 64 : n * 64 + 64]
    for n, k in enumerate(((0, 2), (1, 1), (1, 2))):
        up_ref[n * 64 : n * 64 + 64, :] = made[k]
    for n, k in enumerate(((0, -1), (0, -2), (1, -2))):
        down_ref[n * 64 : n * 64 + 64, :] = made[k]
    for n, k in enumerate(((0, 1), (1, -1))):
        local_ref[n * 64 : n * 64 + 64, :] = made[k]


def faces_body(x_ref, skey_ref, up_ref, down_ref, local_ref):
    faces_of(lambda g: x_ref[g * 512 : g * 512 + 512, :], skey_ref, up_ref, down_ref, local_ref)


def order_body(got_ref, skey_ref, out_ref, up_ref, down_ref, local_ref, *, cap):
    chunks = got_ref.shape[0]
    rows = out_ref.shape[0]
    targets = []
    for c in range(chunks):
        tail = got_ref[c, cap : cap + TAIL, :].astype(F32)
        place = (tail[0:1] - 1.0) * 32.0 + tail[1:2]
        targets.append(place[:, :cap].astype(I32))
    for m in range(0, rows, 256):
        slot = lax.broadcasted_iota(I32, (256, cap), 0) + m
        total = jnp.zeros((256, C), F32)
        for c in range(chunks):
            total = total + dot(one_hot(slot, targets[c]), got_ref[c, :cap, :])
        out_ref[m : m + 256, :] = total.astype(BF)
    faces_of(lambda g: out_ref[g * 512 : g * 512 + 512, :], skey_ref, up_ref, down_ref, local_ref)


FACE_OUTS = [((192, C), BF), ((192, C), BF), ((128, C), BF)]


def fill_grid(block, x, pieces, ekey, grid_ref):
    wide = x.astype(F32)
    k_of = lax.broadcasted_iota(I32, (512, C), 0) & 7
    row = lax.broadcasted_iota(I32, (800, C), 0)
    cell = (row >> 3) * 10 + (row & 7) + 1
    for ci, c in enumerate((-1, 0, 1)):
        rim = dot(one_hot(cell, ekey - c), pieces)
        if c == 0:
            moved = wide
        elif c < 0:
            moved = jnp.where(k_of == 0, 0.0, pltpu.roll(wide, 1, 0))
        else:
            moved = jnp.where(k_of == 7, 0.0, pltpu.roll(wide, 511, 0))
        for i in range(10):
            stripe = rim[i * 80 : i * 80 + 80]
            if 1 <= i <= 8:
                inner = stripe[8:72] + moved[i * 64 - 64 : i * 64]
                stripe = jnp.concatenate([stripe[:8], inner, stripe[72:]], axis=0)
            for bi in range(3):
                grid_ref[block, bi * 3 + ci, i * 64 : i * 64 + 64, :] = stripe[
                    bi * 8 : bi * 8 + 64
                ].astype(BF)


def fill_grids(x_ref, up_ref, down_ref, local_ref, ekey_ref, grid_ref):
    def piece(ref, n):
        return ref[n * 64 : n * 64 + 64, :]

    sources = (
        (piece(up_ref, 0), piece(up_ref, 1), piece(local_ref, 1), piece(down_ref, 1)),
        (piece(up_ref, 2), piece(local_ref, 0), piece(down_ref, 0), piece(down_ref, 2)),
    )
    for g in range(2):
        fill_grid(
            g,
            x_ref[g * 512 : g * 512 + 512, :],
            jnp.concatenate(sources[g], axis=0),
            ekey_ref[g : g + 1, :],
            grid_ref,
        )


def convolve(x_ref, grid_ref, weight_ref, out_ref, acc_ref, flip):
    for g in range(2):
        acc_ref[g * 512 : g * 512 + 512, :] = x_ref[g * 512 : g * 512 + 512, :].astype(F32)

    def one(ab, carry):
        a, b = ab // 3, ab % 3
        start = pl.multiple_of(a * 64, 64)
        for g in range(2):
            total = acc_ref[g * 512 : g * 512 + 512, :]
            for c in range(3):
                rows = grid_ref[g, b * 3 + c, pl.ds(start, 512), :]
                if flip:
                    total = total + dot_nt(rows, weight_ref[26 - (ab * 3 + c)])
                else:
                    total = total + dot(rows, weight_ref[ab * 3 + c])
            acc_ref[g * 512 : g * 512 + 512, :] = total
        return carry

    lax.fori_loop(0, 9, one, 0)
    out_ref[...] = acc_ref[...].astype(BF)


def backward_body(x_ref, up, down, local, ekey, weight_ref, out_ref, turned_ref, grid_ref, acc_ref):
    fill_grids(x_ref, up, down, local, ekey, grid_ref)
    turned_ref[...] = x_ref[...].astype(F32).T.astype(BF)
    convolve(x_ref, grid_ref, weight_ref, out_ref, acc_ref, True)


def forward_body(x_ref, up, down, local, ekey, weight_ref, out_ref, grid_ref, acc_ref):
    fill_grids(x_ref, up, down, local, ekey, grid_ref)
    convolve(x_ref, grid_ref, weight_ref, out_ref, acc_ref, False)


GRID_SCRATCH = pltpu.VMEM((2, 9, 640, C), BF)


def scale_code(peak):
    peak = jnp.maximum(peak, 1e-30)
    power = jnp.floor(jnp.log2(peak))
    part = jnp.clip(jnp.ceil(peak * jnp.exp2(-power) * 64.0), 1.0, 200.0)
    return power * 256.0 + part


def scale_of(code):
    power = jnp.floor(code * (1.0 / 256.0))
    return jnp.exp2(power) * (code - power * 256.0) * (1.0 / 64.0)


def encode(values):
    code = scale_code(jnp.max(jnp.abs(values), axis=0, keepdims=True))
    return code, jnp.round(values * (TOP / scale_of(code))).astype(I32).astype(I16)


def decode(values, code):
    return values.astype(I32).astype(F32) * (scale_of(code) * (1.0 / TOP))


def tail_of(codes):
    lines = list(codes) + [jnp.zeros((1, C), F32)] * (TAIL - len(codes))
    return jnp.concatenate(lines, axis=0).astype(I32).astype(I16)


def tail_codes(ref, start):
    return ref[start : start + TAIL, :].astype(I32).astype(F32)


def kernel_grad_body(
    bits_ref, x_ref, up, down, local, ekey, turned_ref, own_ref, send_ref, grid_ref, code_ref
):
    fill_grids(x_ref, up, down, local, ekey, grid_ref)
    mine = bits_ref[0]

    def term(offset):
        at = jnp.minimum(offset, 26)
        a, bc = at // 9, at % 9
        start = pl.multiple_of(a * 64, 64)
        total = dot(turned_ref[:, :512], grid_ref[0, bc, pl.ds(start, 512), :])
        total = total + dot(turned_ref[:, 512:], grid_ref[1, bc, pl.ds(start, 512), :])
        return jnp.where(offset < 27, total, 0.0)

    code_ref[...] = jnp.zeros_like(code_ref)

    def send_one(i, carry):
        code, values = encode(term((1 - mine) * HALF + i))
        send_ref[pl.ds(pl.multiple_of(i * 256, 256), 256), :] = values
        code_ref[pl.ds(i, 1), :] = code
        return carry

    def keep_one(i, carry):
        own_ref[i] = term(mine * HALF + i)
        return carry

    lax.fori_loop(0, HALF, send_one, 0)
    send_ref[HALF * 256 :, :] = code_ref[...].astype(I32).astype(I16)
    lax.fori_loop(0, HALF, keep_one, 0)


def reduce_body(*refs, which, parts, rows):
    bits_ref, keep_ref, send_ref = refs[0], refs[-2], refs[-1]
    half = rows // 2
    mine = bits_ref[which]
    keep_at = pl.multiple_of(mine * half, half)
    send_at = pl.multiple_of((1 - mine) * half, half)
    codes = []
    for n, (first, many, total) in enumerate(parts):
        acc_ref, got_ref = refs[1 + 2 * n], refs[2 + 2 * n]
        tail = tail_codes(got_ref, total * rows)
        for i in range(first, first + many):
            at = len(codes)
            code = tail[i : i + 1]
            wide = acc_ref[i, pl.ds(send_at, half), :] + decode(
                got_ref[pl.ds(i * rows + send_at, half), :], code
            )
            new, values = encode(wide)
            codes.append(new)
            send_ref[at * half : at * half + half, :] = values
            keep_ref[at] = acc_ref[i, pl.ds(keep_at, half), :] + decode(
                got_ref[pl.ds(i * rows + keep_at, half), :], code
            )
    send_ref[len(codes) * half :, :] = tail_of(codes)


def reduce_step(bits, which, operands, parts, rows):
    many = sum(p[1] for p in parts)
    half = rows // 2
    outs = [((many, half, C), F32), ((many * half + TAIL, C), I16)]
    body = functools.partial(reduce_body, which=which, parts=parts, rows=rows)
    return call(body, outs, [bits, *operands], smem=(0,), moved=many * rows * C * 8)


def total_body(acc_ref, got_ref, out_ref):
    tail = tail_codes(got_ref, HALF * 16)
    for i in range(HALF):
        out_ref[i] = acc_ref[i] + decode(got_ref[i * 16 : i * 16 + 16, :], tail[i : i + 1])


def unit_body(total_ref, a_ref, b_ref):
    for p, out_ref in enumerate((a_ref, b_ref)):
        codes = []
        squares = jnp.zeros((1, C), F32)
        for i in range(PART):
            value = total_ref[p * PART + i]
            squares = squares + jnp.sum(value * value, axis=0, keepdims=True)
            code, coded = encode(value)
            codes.append(code)
            out_ref[i * 16 : i * 16 + 16, :] = coded
        squares = jnp.maximum(squares, 1e-30)
        power = jnp.floor(jnp.log2(squares))
        codes.append(power)
        codes.append(jnp.round(jnp.minimum(squares * jnp.exp2(-power) * 15000.0, 32000.0)))
        out_ref[PART * 16 :, :] = tail_of(codes)


def finish_body(bits_ref, own_a, own_b, far_a, far_b, out_ref, wide_ref, square_ref):
    mine = bits_ref[0]
    sides = ((mine, (own_a, own_b)), (1 - mine, (far_a, far_b)))

    def place_of(p, u):
        place = 0
        for n, which in enumerate(((1, 2, 3, 4), (2, 1, 3, 4))[p]):
            place = place * 2 + (bits_ref[which] ^ ((u >> (3 - n)) & 1))
        return place

    for half, refs in sides:
        for p in range(2):
            for u in range(16):
                tail = tail_codes(refs[p], u * UNIT + PART * 16)
                square_ref[pl.ds(half * 32 + p * 16 + place_of(p, u), 1), :] = (
                    jnp.exp2(tail[PART : PART + 1]) * tail[PART + 1 : PART + 2]
                )
    squares = jnp.sum(square_ref[...], axis=0, keepdims=True)
    mean = jnp.sum(squares, axis=1, keepdims=True) * (1.0 / (15000.0 * 27 * C * C))
    gain = 1.0 / jnp.sqrt(mean + 1e-06)
    for half, refs in sides:
        for p in range(2):
            places, scales = [], []
            for u in range(16):
                places.append(pl.multiple_of(place_of(p, u) * 16, 16))
                tail = tail_codes(refs[p], u * UNIT + PART * 16)
                scales.append(scale_of(tail[:8]) * gain * (1.0 / TOP))
            for i in range(PART):
                for u in range(16):
                    coded = refs[p][u * UNIT + i * 16 : u * UNIT + i * 16 + 16, :]
                    wide_ref[pl.ds(places[u], 16), :] = (
                        coded.astype(I32).astype(F32) * scales[u][i : i + 1]
                    )
                offset = half * HALF + p * PART + i

                @pl.when(offset < 27)
                def _():
                    out_ref[offset] = wide_ref[...].T.astype(BF)


def neighbour_keys(neighbours, first):
    blocks = neighbours.shape[0]
    own = first + lax.broadcasted_iota(I32, (blocks, 26), 0)
    lane = lax.broadcasted_iota(I32, (blocks, 26), 1)
    number = lane + (lane >= 13).astype(I32)
    found = []
    for t in STEPS:
        hit = (neighbours == own + t) & (neighbours >= 0)
        found.append(jnp.max(jnp.where(hit, number, -1), axis=1, keepdims=True))
    o = jnp.stack(found, axis=1)
    some = o >= 0
    o = jnp.maximum(o, 0)
    a, b, c = o // 9 - 1, (o // 3) % 3 - 1, o % 3 - 1
    fi, fj, fk = a == 0, b == 0, c == 0

    v = jnp.arange(512, dtype=I32)[None, None, :]
    i, j, k = v >> 6, (v >> 3) & 7, v & 7

    def at_face(step, coordinate):
        return (step == 0) | (coordinate == jnp.where(step > 0, 7, 0))

    on = some & at_face(a, i) & at_face(b, j) & at_face(c, k)
    rank = jnp.where(fi, i, 0)
    rank = rank * jnp.where(fj, 8, 1) + jnp.where(fj, j, 0)
    rank = rank * jnp.where(fk, 8, 1) + jnp.where(fk, k, 0)
    skey = jnp.where(on, rank, -1).reshape(blocks * 4, 512)

    m = jnp.arange(64, dtype=I32)[None, None, :]
    sk = jnp.where(fk, 3, 0)
    sj = jnp.where(fj, 3, 0)
    mk = m & ((1 << sk) - 1)
    mj = (m >> sk) & ((1 << sj) - 1)
    mi = m >> (sk + sj)
    inside = some & (mi < jnp.where(fi, 8, 1))

    def rim(step, free):
        return jnp.where(step == 0, free + 1, jnp.where(step > 0, 9, 0))

    cell = rim(a, mi) * 100 + rim(b, mj) * 10 + rim(c, mk)
    ekey = jnp.where(inside, cell, -100).reshape(blocks, 256)
    return skey, ekey


def swap(x, bit):
    axis, place = bit
    count = lax.axis_size(axis)
    return lax.ppermute(x, axis, [(i, i ^ (1 << place)) for i in range(count)])


def shift(x, step):
    count = lax.axis_size("pts")
    return lax.ppermute(
        x, "pts", [(i, i + step) for i in range(count) if 0 <= i + step < count]
    )


def device_bits():
    dp = lax.axis_size("dp").bit_length() - 1
    pts = lax.axis_size("pts").bit_length() - 1
    order = [("dp", n) for n in range(dp)] + [("pts", n) for n in range(pts)]
    return order[:5], order[5:]


def bit_value(bit):
    return (lax.axis_index(bit[0]) >> bit[1]) & 1


def on_device(features, hilbert_pos, weight, neighbours, grad_out):
    rows = features.shape[1]
    count = lax.axis_size("pts")
    me = lax.axis_index("pts").astype(I32)
    window = min(16, count)
    cap = 2 * rows // window
    direct = window == count
    split, extra = device_bits()
    bits = jnp.stack([bit_value(b) for b in split]).astype(I32)
    s0, s1, s2, s3, s4 = split

    body = functools.partial(pack_body, count=count, window=window, cap=cap, direct=direct)
    (packed,) = call(
        body,
        [((window, cap + TAIL, C), BF)],
        [me.reshape(1), hilbert_pos, features[0]],
        smem=(0,),
        flops=4 * rows * rows * C,
        moved=4 * rows * C * 2,
    )
    if direct:
        got = lax.all_to_all(packed, "pts", 0, 0, tiled=True)
    else:
        parts = []
        for w in range(window):
            step = w - window // 2
            turn = [(i, (i + step) % count) for i in range(count)]
            parts.append(packed[w] if step == 0 else lax.ppermute(packed[w], "pts", turn))
        got = jnp.stack(parts)

    skey, ekey = neighbour_keys(neighbours[0], me * (rows // 512))
    dy = grad_out[0]
    up, down, dy_local = call(faces_body, FACE_OUTS, [dy, skey], flops=4 * 512 * 256 * C)
    dy_up, dy_down = shift(up, 1), shift(down, -1)
    conv_flops = 2 * 27 * rows * C * C
    backward, turned = call(
        backward_body,
        [((rows, C), BF), ((C, rows), BF)],
        [dy, dy_up, dy_down, dy_local, ekey, weight],
        scratch=[GRID_SCRATCH, pltpu.VMEM((rows, C), F32)],
        flops=conv_flops,
        moved=6 * MIB,
    )

    x, up, down, x_local = call(
        functools.partial(order_body, cap=cap),
        [((rows, C), BF), *FACE_OUTS],
        [got, skey],
        flops=4 * rows * rows * C,
        moved=4 * rows * C * 2,
    )
    x_up, x_down = shift(up, 1), shift(down, -1)
    own, send = call(
        kernel_grad_body,
        [((HALF, C, C), F32), ((HALF * C + TAIL, C), I16)],
        [bits, x, x_up, x_down, x_local, ekey, turned],
        smem=(0,),
        scratch=[GRID_SCRATCH, pltpu.VMEM((TAIL, C), F32)],
        flops=conv_flops,
        moved=6 * MIB,
    )
    (forward,) = call(
        forward_body,
        [((rows, C), BF)],
        [x, x_up, x_down, x_local, ekey, weight],
        scratch=[GRID_SCRATCH, pltpu.VMEM((rows, C), F32)],
        flops=conv_flops,
        moved=6 * MIB,
    )

    came = swap(send, s0)
    keep_a, send_a = reduce_step(bits, 1, [own, came], ((0, PART, HALF),), 256)
    keep_b, send_b = reduce_step(bits, 2, [own, came], ((PART, PART, HALF),), 256)
    came_a, came_b = swap(send_a, s1), swap(send_b, s2)
    keep_a, send_a = reduce_step(bits, 2, [keep_a, came_a], ((0, PART, PART),), 128)
    keep_b, send_b = reduce_step(bits, 1, [keep_b, came_b], ((0, PART, PART),), 128)
    came_a, came_b = swap(send_a, s2), swap(send_b, s1)
    keep, send = reduce_step(
        bits, 3, [keep_a, came_a, keep_b, came_b], ((0, PART, PART), (0, PART, PART)), 64
    )
    came = swap(send, s3)
    keep, send = reduce_step(bits, 4, [keep, came], ((0, HALF, HALF),), 32)
    came = swap(send, s4)
    (total,) = call(total_body, [((HALF, 16, C), F32)], [keep, came])
    for b in extra:
        total = total + swap(total, b)
    unit_a, unit_b = call(unit_body, [((UNIT, C), I16), ((UNIT, C), I16)], [total])

    both = jnp.concatenate([unit_a, unit_b], axis=0)
    far = swap(both, s4)
    unit_a = jnp.concatenate([unit_a, far[:UNIT]], axis=0)
    unit_b = jnp.concatenate([unit_b, far[UNIT:]], axis=0)
    far = swap(jnp.concatenate([unit_a, unit_b], axis=0), s3)
    unit_a = jnp.concatenate([unit_a, far[: 2 * UNIT]], axis=0)
    unit_b = jnp.concatenate([unit_b, far[2 * UNIT :]], axis=0)
    far_a, far_b = swap(unit_a, s2), swap(unit_b, s1)
    unit_a = jnp.concatenate([unit_a, far_a], axis=0)
    unit_b = jnp.concatenate([unit_b, far_b], axis=0)
    far_a, far_b = swap(unit_a, s1), swap(unit_b, s2)
    unit_a = jnp.concatenate([unit_a, far_a], axis=0)
    unit_b = jnp.concatenate([unit_b, far_b], axis=0)
    far_a, far_b = swap(unit_a, s0), swap(unit_b, s0)
    (weight_grad,) = call(
        finish_body,
        [((27, C, C), BF)],
        [bits, unit_a, unit_b, far_a, far_b],
        smem=(0,),
        scratch=[pltpu.VMEM((C, C), F32), pltpu.VMEM((64, C), F32)],
    )
    return forward[None], backward[None], weight_grad


def solution(mesh):
    placed = (P("dp", "pts", None), P("dp", "pts"), P(), P("dp", "pts", None), P("dp", "pts", None))
    return jax.shard_map(
        on_device,
        mesh=mesh,
        in_specs=placed,
        out_specs=(P("dp", "pts", None), P("dp", "pts", None), P()),
        check_vma=False,
    )
```

profile of v0, /device:TPU:0, one launch (start us, length us, event | category | flops | bytes accessed | tf_op | source)
XLA Modules:
  0.0 164.3 jit_solution(11993221074104088140)
XLA Ops:
  0.6 1.0 copy-done.2
  1.7 0.7 copy-done.3
  2.4 3.8 %shard_map.76 = bf16[8,272,256]{2,1,0:T(8,128)(2,1)} custom-call(s32[1]{0:T(128)} %bitcast.me_ref, s32[1,1024]{1,0:T(1,128)S(1)} %copy-done.3, bf16[1024,256]{1,0:T(8,128)(2,1)S(1)} %bitcast.46), custom_call_target="tpu_custom_call" | custom-call | flops 1073741824 | bytes 2097152 | tf_op jit(solution)/shard_map/pallas_call | solution.py:42
  6.2 7.4 %all-to-all-start = ((bf16[8,272,256]{2,1,0:T(8,128)(2,1)}), bf16[8,272,256]{2,1,0:T(8,128)(2,1)S(1)}, u32[]{:S(2)}, u32[]{:S(2)}) async-start(bf16[8,272,256]{2,1,0:T(8,128)(2,1)} %shard_map.76), calls=%async_computation | async-start | bytes 2228224 | tf_op jit(solution)/shard_map/all_to_all | solution.py:450
  13.6 0.2 fusion.6
  13.8 0.1 copy.29
  13.9 0.1 copy.28
  14.0 0.1 copy.27
  14.1 0.1 copy.26
  15.0 0.3 shard_map.79
  15.3 3.9 %collective-permute-start.2 = (bf16[192,256]{1,0:T(8,128)(2,1)S(1)}, bf16[192,256]{1,0:T(8,128)(2,1)S(1)}, u32[]{:S(2)}, u32[]{:S(2)}) collective-permute-start(bf16[192,256]{1,0:T(8,128)(2,1)S(1)} %get-tuple-element.32), channel_id=1, source_target_pairs={{0,4},{4,8},{8,12},{12,16},{16,20},{20,24},{24,28},{1,5},{5,9},{9,... | collective-permute-start | bytes 294920 | tf_op jit(solution)/shard_map/ppermute | solution.py:413
  19.2 1.3 collective-permute-start.3
  20.6 0.1 copy.30
  20.9 0.1 copy.32
  21.1 0.1 copy.39
  21.3 0.1 broadcast_in_dim.149
  21.4 0.1 copy.41
  21.7 0.1 copy.40
  21.9 0.1 copy.35
  22.2 0.1 copy.38
  22.5 0.1 copy.37
  22.7 0.1 copy.36
  23.0 0.1 copy.33
  23.2 0.1 copy.34
  23.5 0.1 copy.31
  24.0 17.8 %all-to-all-done.got_ref = bf16[8,272,256]{2,1,0:T(8,128)(2,1)S(1)} async-done(((bf16[8,272,256]{2,1,0:T(8,128)(2,1)}), bf16[8,272,256]{2,1,0:T(8,128)(2,1)S(1)}, u32[]{:S(2)}, u32[]{:S(2)}) %all-to-all-start) | async-done | bytes 1114144 | tf_op jit(solution)/shard_map/all_to_all | solution.py:450
  41.8 1.5 shard_map.77
  43.3 2.3 %collective-permute-start = (bf16[192,256]{1,0:T(8,128)(2,1)S(1)}, bf16[192,256]{1,0:T(8,128)(2,1)S(1)}, u32[]{:S(2)}, u32[]{:S(2)}) collective-permute-start(bf16[192,256]{1,0:T(8,128)(2,1)S(1)} %get-tuple-element.29), channel_id=1, source_target_pairs={{0,4},{4,8},{8,12},{12,16},{16,20},{20,24},{24,28},{1,5},{5,9},{9,... | collective-permute-start | bytes 294920 | tf_op jit(solution)/shard_map/ppermute | solution.py:413
  45.6 1.5 collective-permute-start.1
  47.1 7.6 %shard_map.80 = (bf16[1024,256]{1,0:T(8,128)(2,1)}, bf16[256,1024]{1,0:T(8,128)(2,1)S(1)}) custom-call(bf16[1024,256]{1,0:T(8,128)(2,1)S(1)} %bitcast.45, bf16[192,256]{1,0:T(8,128)(2,1)S(1)} %collective-permute-done.2.up, bf16[192,256]{1,0:T(8,128)(2,1)S(1)} %collective-permute-done.3.down, bf16[128,256]{1,0:T(8,128)(2,1)S(1)} %get-tuple-element.34.local, ...), custom_call_target="tpu_custom_call" | custom-call | flops 3623878656 | bytes 6291456 | tf_op jit(solution)/shard_map/pallas_call | solution.py:42
  54.7 13.4 %shard_map.81 = (f32[14,256,256]{2,1,0:T(8,128)}, s16[3600,256]{1,0:T(8,128)(2,1)S(1)}) custom-call(s32[5]{0:T(128)S(1)} %stack.54.bits_ref.refs_0_, bf16[1024,256]{1,0:T(8,128)(2,1)S(1)} %get-tuple-element.28.x_ref, bf16[192,256]{1,0:T(8,128)(2,1)S(1)} %collective-permute-done.up, bf16[192,256]{1,0:T(8,128)(2,1)S(1)} %collective-permute-done.1.down, ...), custom_call_target="tpu_custom_call" | custom-call | flops 3623878656 | bytes 6291456 | tf_op jit(solution)/shard_map/pallas_call | solution.py:42
  68.1 3.8 %collective-permute-done.4.refs_2_ = s16[3600,256]{1,0:T(8,128)(2,1)S(1)} collective-permute-done((s16[3600,256]{1,0:T(8,128)(2,1)S(1)}, s16[3600,256]{1,0:T(8,128)(2,1)S(1)}, u32[]{:S(2)}, u32[]{:S(2)}) %collective-permute-start.4) | collective-permute-done | bytes 1843232 | tf_op jit(solution)/shard_map/ppermute | solution.py:408
  71.9 2.5 %shard_map.82 = (f32[7,128,256]{2,1,0:T(8,128)S(1)}, s16[912,256]{1,0:T(8,128)(2,1)S(1)}) custom-call(s32[5]{0:T(128)S(1)} %stack.54.bits_ref.refs_0_, f32[14,256,256]{2,1,0:T(8,128)} %get-tuple-element.37.refs_1_, s16[3600,256]{1,0:T(8,128)(2,1)S(1)} %collective-permute-done.4.refs_2_), custom_call_target="tpu_custom_call" | custom-call | bytes 3670016 | tf_op jit(solution)/shard_map/pallas_call | solution.py:42
  74.4 1.6 collective-permute-start.5
  76.0 2.5 %shard_map.84 = (f32[7,128,256]{2,1,0:T(8,128)S(1)}, s16[912,256]{1,0:T(8,128)(2,1)S(1)}) custom-call(s32[5]{0:T(128)S(1)} %stack.54.bits_ref.refs_0_, f32[14,256,256]{2,1,0:T(8,128)} %get-tuple-element.37.refs_1_, s16[3600,256]{1,0:T(8,128)(2,1)S(1)} %collective-permute-done.4.refs_2_), custom_call_target="tpu_custom_call" | custom-call | bytes 3670016 | tf_op jit(solution)/shard_map/pallas_call | solution.py:42
  78.5 2.7 %collective-permute-start.7 = (s16[912,256]{1,0:T(8,128)(2,1)S(1)}, s16[912,256]{1,0:T(8,128)(2,1)S(1)}, u32[]{:S(2)}, u32[]{:S(2)}) collective-permute-start(s16[912,256]{1,0:T(8,128)(2,1)S(1)} %get-tuple-element.44), channel_id=1, source_target_pairs={{0,4},{4,0},{8,12},{12,8},{16,20},{20,16},{24,28},{28,24},{1,5},{5... | collective-permute-start | bytes 1400840 | tf_op jit(solution)/shard_map/ppermute | solution.py:408
  81.2 6.0 %collective-permute-done.5.refs_2_ = s16[912,256]{1,0:T(8,128)(2,1)S(1)} collective-permute-done((s16[912,256]{1,0:T(8,128)(2,1)S(1)}, s16[912,256]{1,0:T(8,128)(2,1)S(1)}, u32[]{:S(2)}, u32[]{:S(2)}) %collective-permute-start.5) | collective-permute-done | bytes 466976 | tf_op jit(solution)/shard_map/ppermute | solution.py:408
  87.2 0.8 shard_map.83
  88.0 2.7 %collective-permute-start.6 = (s16[464,256]{1,0:T(8,128)(2,1)S(1)}, s16[464,256]{1,0:T(8,128)(2,1)S(1)}, u32[]{:S(2)}, u32[]{:S(2)}) collective-permute-start(s16[464,256]{1,0:T(8,128)(2,1)S(1)} %get-tuple-element.42), channel_id=1, source_target_pairs={{0,4},{4,0},{8,12},{12,8},{16,20},{20,16},{24,28},{28,24},{1,5},{5... | collective-permute-start | bytes 712712 | tf_op jit(solution)/shard_map/ppermute | solution.py:408
  90.7 2.0 %collective-permute-done.7.refs_2_ = s16[912,256]{1,0:T(8,128)(2,1)S(1)} collective-permute-done((s16[912,256]{1,0:T(8,128)(2,1)S(1)}, s16[912,256]{1,0:T(8,128)(2,1)S(1)}, u32[]{:S(2)}, u32[]{:S(2)}) %collective-permute-start.7) | collective-permute-done | bytes 466976 | tf_op jit(solution)/shard_map/ppermute | solution.py:408
  92.7 0.8 shard_map.85
  93.6 3.4 %collective-permute-done.6.refs_2_ = s16[464,256]{1,0:T(8,128)(2,1)S(1)} collective-permute-done((s16[464,256]{1,0:T(8,128)(2,1)S(1)}, s16[464,256]{1,0:T(8,128)(2,1)S(1)}, u32[]{:S(2)}, u32[]{:S(2)}) %collective-permute-start.6) | collective-permute-done | bytes 237600 | tf_op jit(solution)/shard_map/ppermute | solution.py:408
  97.0 2.8 %collective-permute-done.8.refs_4_ = s16[464,256]{1,0:T(8,128)(2,1)S(1)} collective-permute-done((s16[464,256]{1,0:T(8,128)(2,1)S(1)}, s16[464,256]{1,0:T(8,128)(2,1)S(1)}, u32[]{:S(2)}, u32[]{:S(2)}) %collective-permute-start.8) | collective-permute-done | bytes 237600 | tf_op jit(solution)/shard_map/ppermute | solution.py:408
  99.8 0.9 shard_map.86
  100.6 1.3 collective-permute-start.9
  101.9 4.9 %collective-permute-done.9.refs_2_ = s16[464,256]{1,0:T(8,128)(2,1)S(1)} collective-permute-done((s16[464,256]{1,0:T(8,128)(2,1)S(1)}, s16[464,256]{1,0:T(8,128)(2,1)S(1)}, u32[]{:S(2)}, u32[]{:S(2)}) %collective-permute-start.9) | collective-permute-done | bytes 237600 | tf_op jit(solution)/shard_map/ppermute | solution.py:408
  106.8 0.8 shard_map.87
  107.6 2.4 %collective-permute-start.10 = (s16[240,256]{1,0:T(8,128)(2,1)S(1)}, s16[240,256]{1,0:T(8,128)(2,1)S(1)}, u32[]{:S(2)}, u32[]{:S(2)}) collective-permute-start(s16[240,256]{1,0:T(8,128)(2,1)S(1)} %get-tuple-element.50), channel_id=1, source_target_pairs={{0,16},{4,20},{8,24},{12,28},{16,0},{20,4},{24,8},{28,12},{1,17},{... | collective-permute-start | bytes 368648 | tf_op jit(solution)/shard_map/ppermute | solution.py:408
  110.0 6.7 %collective-permute-done.10.got_ref = s16[240,256]{1,0:T(8,128)(2,1)S(1)} collective-permute-done((s16[240,256]{1,0:T(8,128)(2,1)S(1)}, s16[240,256]{1,0:T(8,128)(2,1)S(1)}, u32[]{:S(2)}, u32[]{:S(2)}) %collective-permute-start.10) | collective-permute-done | bytes 122912 | tf_op jit(solution)/shard_map/ppermute | solution.py:408
  116.7 0.2 shard_map.89
  116.9 0.5 collective-permute-start.11
  117.4 6.9 %collective-permute-done.11 = s16[256,256]{1,0:T(8,128)(2,1)S(1)} collective-permute-done((s16[256,256]{1,0:T(8,128)(2,1)S(1)}, s16[256,256]{1,0:T(8,128)(2,1)S(1)}, u32[]{:S(2)}, u32[]{:S(2)}) %collective-permute-start.11) | collective-permute-done | bytes 131104 | tf_op jit(solution)/shard_map/ppermute | solution.py:408
  124.3 0.4 collective-permute-start.12
  124.8 6.0 %collective-permute-done.12 = s16[512,256]{1,0:T(8,128)(2,1)S(1)} collective-permute-done((s16[512,256]{1,0:T(8,128)(2,1)S(1)}, s16[512,256]{1,0:T(8,128)(2,1)S(1)}, u32[]{:S(2)}, u32[]{:S(2)}) %collective-permute-start.12) | collective-permute-done | bytes 262176 | tf_op jit(solution)/shard_map/ppermute | solution.py:408
  130.8 1.4 collective-permute-start.13
  132.3 0.4 collective-permute-start.15
  132.7 7.4 %collective-permute-done.13 = s16[512,256]{1,0:T(8,128)(2,1)S(1)} collective-permute-done((s16[512,256]{1,0:T(8,128)(2,1)S(1)}, s16[512,256]{1,0:T(8,128)(2,1)S(1)}, u32[]{:S(2)}, u32[]{:S(2)}) %collective-permute-start.13) | collective-permute-done | bytes 262176 | tf_op jit(solution)/shard_map/ppermute | solution.py:408
  140.1 0.5 collective-permute-start.14
  140.7 0.4 collective-permute-done.15
  141.1 1.0 collective-permute-start.16
  142.1 7.3 %collective-permute-done.14 = s16[1024,256]{1,0:T(8,128)(2,1)S(1)} collective-permute-done((s16[1024,256]{1,0:T(8,128)(2,1)S(1)}, s16[1024,256]{1,0:T(8,128)(2,1)S(1)}, u32[]{:S(2)}, u32[]{:S(2)}) %collective-permute-start.14) | collective-permute-done | bytes 524320 | tf_op jit(solution)/shard_map/ppermute | solution.py:408
  149.5 0.8 collective-permute-done.16
  150.5 7.2 %shard_map.78 = bf16[1024,256]{1,0:T(8,128)(2,1)} custom-call(bf16[1024,256]{1,0:T(8,128)(2,1)S(1)} %get-tuple-element.28.x_ref, bf16[192,256]{1,0:T(8,128)(2,1)S(1)} %collective-permute-done.up, bf16[192,256]{1,0:T(8,128)(2,1)S(1)} %collective-permute-done.1.down, bf16[128,256]{1,0:T(8,128)(2,1)S(1)} %get-tuple-element.31.local, ...), custom_call_target="tpu_custom_call" | custom-call | flops 3623878656 | bytes 6291456 | tf_op jit(solution)/shard_map/pallas_call | solution.py:42
  157.7 6.5 %shard_map.90 = bf16[27,256,256]{2,1,0:T(8,128)(2,1)} custom-call(s32[5]{0:T(128)S(1)} %stack.54.bits_ref.refs_0_, s16[2048,256]{1,0:T(8,128)(2,1)S(1)} %constant_dynamic-update-slice_fusion.own_a, s16[2048,256]{1,0:T(8,128)(2,1)S(1)} %constant_dynamic-update-slice_fusion.5.own_b, s16[2048,256]{1,0:T(8,128)(2,1)S(1)} %collective-permute-done.17.far_a, ...), custom_call_target="tpu_custom_call" | custom-call | tf_op jit(solution)/shard_map/pallas_call | solution.py:42
  (85 shorter events, 3.4 us)
Async XLA Ops:
  0.6 1.0 copy-start.2
  1.7 0.7 copy-start.3
  6.2 7.5 %copy-start.4 = (s32[1,2,26]{2,1,0:T(2,128)S(1)}, s32[1,2,26]{2,1,0:T(2,128)}, u32[]{:S(2)}) copy-start(s32[1,2,26]{2,1,0:T(2,128)} %param.8) | copy-start | bytes 628
  6.2 8.8 %copy-start = (bf16[1,1024,256]{2,1,0:T(8,128)(2,1)S(1)}, bf16[1,1024,256]{2,1,0:T(8,128)(2,1)}, u32[]{:S(2)}) copy-start(bf16[1,1024,256]{2,1,0:T(8,128)(2,1)} %param.9) | copy-start | bytes 1572868
  6.2 35.6 %all-to-all-start = ((bf16[8,272,256]{2,1,0:T(8,128)(2,1)}), bf16[8,272,256]{2,1,0:T(8,128)(2,1)S(1)}, u32[]{:S(2)}, u32[]{:S(2)}) async-start(bf16[8,272,256]{2,1,0:T(8,128)(2,1)} %shard_map.76), calls=%async_computation | async-start | bytes 2228224 | tf_op jit(solution)/shard_map/all_to_all | solution.py:450
  15.3 31.8 %collective-permute-start.2 = (bf16[192,256]{1,0:T(8,128)(2,1)S(1)}, bf16[192,256]{1,0:T(8,128)(2,1)S(1)}, u32[]{:S(2)}, u32[]{:S(2)}) collective-permute-start(bf16[192,256]{1,0:T(8,128)(2,1)S(1)} %get-tuple-element.32), channel_id=1, source_target_pairs={{0,4},{4,8},{8,12},{12,16},{16,20},{20,24},{24,28},{1,5},{5,9},{9,... | collective-permute-start | bytes 294920 | tf_op jit(solution)/shard_map/ppermute | solution.py:413
  19.2 27.8 %collective-permute-start.3 = (bf16[192,256]{1,0:T(8,128)(2,1)S(1)}, bf16[192,256]{1,0:T(8,128)(2,1)S(1)}, u32[]{:S(2)}, u32[]{:S(2)}) collective-permute-start(bf16[192,256]{1,0:T(8,128)(2,1)S(1)} %get-tuple-element.33), channel_id=1, source_target_pairs={{4,0},{8,4},{12,8},{16,12},{20,16},{24,20},{28,24},{5,1},{9,5},{13... | collective-permute-start | bytes 294920 | tf_op jit(solution)/shard_map/ppermute | solution.py:413
  41.8 5.3 %copy-start.1 = (bf16[27,256,256]{2,1,0:T(8,128)(2,1)S(1)}, bf16[27,256,256]{2,1,0:T(8,128)(2,1)}, u32[]{:S(2)}) copy-start(bf16[27,256,256]{2,1,0:T(8,128)(2,1)} %weight_ref.3) | copy-start | bytes 10616836
  43.3 11.4 %collective-permute-start = (bf16[192,256]{1,0:T(8,128)(2,1)S(1)}, bf16[192,256]{1,0:T(8,128)(2,1)S(1)}, u32[]{:S(2)}, u32[]{:S(2)}) collective-permute-start(bf16[192,256]{1,0:T(8,128)(2,1)S(1)} %get-tuple-element.29), channel_id=1, source_target_pairs={{0,4},{4,8},{8,12},{12,16},{16,20},{20,24},{24,28},{1,5},{5,9},{9,... | collective-permute-start | bytes 294920 | tf_op jit(solution)/shard_map/ppermute | solution.py:413
  45.6 9.1 %collective-permute-start.1 = (bf16[192,256]{1,0:T(8,128)(2,1)S(1)}, bf16[192,256]{1,0:T(8,128)(2,1)S(1)}, u32[]{:S(2)}, u32[]{:S(2)}) collective-permute-start(bf16[192,256]{1,0:T(8,128)(2,1)S(1)} %get-tuple-element.30), channel_id=1, source_target_pairs={{4,0},{8,4},{12,8},{16,12},{20,16},{24,20},{28,24},{5,1},{9,5},{13... | collective-permute-start | bytes 294920 | tf_op jit(solution)/shard_map/ppermute | solution.py:413
  68.1 3.8 %collective-permute-start.4 = (s16[3600,256]{1,0:T(8,128)(2,1)S(1)}, s16[3600,256]{1,0:T(8,128)(2,1)S(1)}, u32[]{:S(2)}, u32[]{:S(2)}) collective-permute-start(s16[3600,256]{1,0:T(8,128)(2,1)S(1)} %get-tuple-element.38), channel_id=1, source_target_pairs={{0,1},{1,0},{2,3},{3,2},{4,5},{5,4},{6,7},{7,6},{8,9},{9,8},{10,11... | collective-permute-start | bytes 5529608 | tf_op jit(solution)/shard_map/ppermute | solution.py:408
  74.4 12.8 %collective-permute-start.5 = (s16[912,256]{1,0:T(8,128)(2,1)S(1)}, s16[912,256]{1,0:T(8,128)(2,1)S(1)}, u32[]{:S(2)}, u32[]{:S(2)}) collective-permute-start(s16[912,256]{1,0:T(8,128)(2,1)S(1)} %get-tuple-element.40), channel_id=1, source_target_pairs={{0,2},{1,3},{2,0},{3,1},{4,6},{5,7},{6,4},{7,5},{8,10},{9,11},{10,... | collective-permute-start | bytes 1400840 | tf_op jit(solution)/shard_map/ppermute | solution.py:408
  78.5 14.2 %collective-permute-start.7 = (s16[912,256]{1,0:T(8,128)(2,1)S(1)}, s16[912,256]{1,0:T(8,128)(2,1)S(1)}, u32[]{:S(2)}, u32[]{:S(2)}) collective-permute-start(s16[912,256]{1,0:T(8,128)(2,1)S(1)} %get-tuple-element.44), channel_id=1, source_target_pairs={{0,4},{4,0},{8,12},{12,8},{16,20},{20,16},{24,28},{28,24},{1,5},{5... | collective-permute-start | bytes 1400840 | tf_op jit(solution)/shard_map/ppermute | solution.py:408
  88.0 9.0 %collective-permute-start.6 = (s16[464,256]{1,0:T(8,128)(2,1)S(1)}, s16[464,256]{1,0:T(8,128)(2,1)S(1)}, u32[]{:S(2)}, u32[]{:S(2)}) collective-permute-start(s16[464,256]{1,0:T(8,128)(2,1)S(1)} %get-tuple-element.42), channel_id=1, source_target_pairs={{0,4},{4,0},{8,12},{12,8},{16,20},{20,16},{24,28},{28,24},{1,5},{5... | collective-permute-start | bytes 712712 | tf_op jit(solution)/shard_map/ppermute | solution.py:408
  93.5 6.3 %collective-permute-start.8 = (s16[464,256]{1,0:T(8,128)(2,1)S(1)}, s16[464,256]{1,0:T(8,128)(2,1)S(1)}, u32[]{:S(2)}, u32[]{:S(2)}) collective-permute-start(s16[464,256]{1,0:T(8,128)(2,1)S(1)} %get-tuple-element.46), channel_id=1, source_target_pairs={{0,2},{1,3},{2,0},{3,1},{4,6},{5,7},{6,4},{7,5},{8,10},{9,11},{10,... | collective-permute-start | bytes 712712 | tf_op jit(solution)/shard_map/ppermute | solution.py:408
  100.6 6.2 %collective-permute-start.9 = (s16[464,256]{1,0:T(8,128)(2,1)S(1)}, s16[464,256]{1,0:T(8,128)(2,1)S(1)}, u32[]{:S(2)}, u32[]{:S(2)}) collective-permute-start(s16[464,256]{1,0:T(8,128)(2,1)S(1)} %get-tuple-element.48), channel_id=1, source_target_pairs={{0,8},{4,12},{8,0},{12,4},{16,24},{20,28},{24,16},{28,20},{1,9},{5... | collective-permute-start | bytes 712712 | tf_op jit(solution)/shard_map/ppermute | solution.py:408
  107.6 9.0 %collective-permute-start.10 = (s16[240,256]{1,0:T(8,128)(2,1)S(1)}, s16[240,256]{1,0:T(8,128)(2,1)S(1)}, u32[]{:S(2)}, u32[]{:S(2)}) collective-permute-start(s16[240,256]{1,0:T(8,128)(2,1)S(1)} %get-tuple-element.50), channel_id=1, source_target_pairs={{0,16},{4,20},{8,24},{12,28},{16,0},{20,4},{24,8},{28,12},{1,17},{... | collective-permute-start | bytes 368648 | tf_op jit(solution)/shard_map/ppermute | solution.py:408
  116.9 7.4 %collective-permute-start.11 = (s16[256,256]{1,0:T(8,128)(2,1)S(1)}, s16[256,256]{1,0:T(8,128)(2,1)S(1)}, u32[]{:S(2)}, u32[]{:S(2)}) collective-permute-start(s16[256,256]{1,0:T(8,128)(2,1)S(1)} %pad_add_fusion.6), channel_id=1, source_target_pairs={{0,16},{4,20},{8,24},{12,28},{16,0},{20,4},{24,8},{28,12},{1,17},{... | collective-permute-start | bytes 393224 | tf_op jit(solution)/shard_map/ppermute | solution.py:408
  124.3 6.4 %collective-permute-start.12 = (s16[512,256]{1,0:T(8,128)(2,1)S(1)}, s16[512,256]{1,0:T(8,128)(2,1)S(1)}, u32[]{:S(2)}, u32[]{:S(2)}) collective-permute-start(s16[512,256]{1,0:T(8,128)(2,1)S(1)} %pad_add_fusion.2), channel_id=1, source_target_pairs={{0,8},{4,12},{8,0},{12,4},{16,24},{20,28},{24,16},{28,20},{1,9},{5... | collective-permute-start | bytes 786440 | tf_op jit(solution)/shard_map/ppermute | solution.py:408
  130.8 9.3 %collective-permute-start.13 = (s16[512,256]{1,0:T(8,128)(2,1)S(1)}, s16[512,256]{1,0:T(8,128)(2,1)S(1)}, u32[]{:S(2)}, u32[]{:S(2)}) collective-permute-start(s16[512,256]{1,0:T(8,128)(2,1)S(1)} %pad_add_fusion.4), channel_id=1, source_target_pairs={{0,4},{4,0},{8,12},{12,8},{16,20},{20,16},{24,28},{28,24},{1,5},{5... | collective-permute-start | bytes 786440 | tf_op jit(solution)/shard_map/ppermute | solution.py:408
  132.3 8.8 %collective-permute-start.15 = (s16[512,256]{1,0:T(8,128)(2,1)S(1)}, s16[512,256]{1,0:T(8,128)(2,1)S(1)}, u32[]{:S(2)}, u32[]{:S(2)}) collective-permute-start(s16[512,256]{1,0:T(8,128)(2,1)S(1)} %pad_add_fusion.5), channel_id=1, source_target_pairs={{0,2},{1,3},{2,0},{3,1},{4,6},{5,7},{6,4},{7,5},{8,10},{9,11},{10,... | collective-permute-start | bytes 786440 | tf_op jit(solution)/shard_map/ppermute | solution.py:408
  140.1 9.2 %collective-permute-start.14 = (s16[1024,256]{1,0:T(8,128)(2,1)S(1)}, s16[1024,256]{1,0:T(8,128)(2,1)S(1)}, u32[]{:S(2)}, u32[]{:S(2)}) collective-permute-start(s16[1024,256]{1,0:T(8,128)(2,1)S(1)} %pad_add_fusion), channel_id=1, source_target_pairs={{0,2},{1,3},{2,0},{3,1},{4,6},{5,7},{6,4},{7,5},{8,10},{9,11},{10,... | collective-permute-start | bytes 1572872 | tf_op jit(solution)/shard_map/ppermute | solution.py:408
  141.1 9.2 %collective-permute-start.16 = (s16[1024,256]{1,0:T(8,128)(2,1)S(1)}, s16[1024,256]{1,0:T(8,128)(2,1)S(1)}, u32[]{:S(2)}, u32[]{:S(2)}) collective-permute-start(s16[1024,256]{1,0:T(8,128)(2,1)S(1)} %pad_add_fusion.1), channel_id=1, source_target_pairs={{0,4},{4,0},{8,12},{12,8},{16,20},{20,16},{24,28},{28,24},{1,5},{5... | collective-permute-start | bytes 1572872 | tf_op jit(solution)/shard_map/ppermute | solution.py:408
  149.4 8.3 %collective-permute-start.17 = (s16[2048,256]{1,0:T(8,128)(2,1)S(1)}, s16[2048,256]{1,0:T(8,128)(2,1)S(1)}, u32[]{:S(2)}, u32[]{:S(2)}) collective-permute-start(s16[2048,256]{1,0:T(8,128)(2,1)S(1)} %constant_dynamic-update-slice_fusion.own_a), channel_id=1, source_target_pairs={{0,1},{1,0},{2,3},{3,2},{4,5},{5,4},{6,7},{7,6},{8,9},{9,8},{10,11... | collective-permute-start | bytes 3145736 | tf_op jit(solution)/shard_map/ppermute | solution.py:408
  150.4 7.3 %collective-permute-start.18 = (s16[2048,256]{1,0:T(8,128)(2,1)S(1)}, s16[2048,256]{1,0:T(8,128)(2,1)S(1)}, u32[]{:S(2)}, u32[]{:S(2)}) collective-permute-start(s16[2048,256]{1,0:T(8,128)(2,1)S(1)} %constant_dynamic-update-slice_fusion.5.own_b), channel_id=1, source_target_pairs={{0,1},{1,0},{2,3},{3,2},{4,5},{5,4},{6,7},{7,6},{8,9},{9,8},{10,11... | collective-permute-start | bytes 3145736 | tf_op jit(solution)/shard_map/ppermute | solution.py:408
where the time goes:
time: 165 us; the launch traced here: 164 us
  waiting for transfers between devices  76.2 us (46%)
  Pallas kernels  48.8 us (30%)
  starting transfers between devices  31.5 us (19%)
  local copies, waits for them, and re-layouts  6.03 us (4%)
    ppermute x15, waiting for transfers between devices, swap(): return lax.ppermute(x, axis, [(i, i ^ 1 << place) for i in range(count)])  58.4 us
    pallas_call x15, Pallas kernels, call(): pl.pallas_call(body, out_shape=shapes, in_specs=specs, out_specs=[pl.Bloc...  48.8 us
    all_to_all x1, waiting for transfers between devices, on_device(): got = lax.all_to_all(packed, 'pts', 0, 0, tiled=True)  17.8 us
    ppermute x15, starting transfers between devices, swap(): return lax.ppermute(x, axis, [(i, i ^ 1 << place) for i in range(count)])  15.1 us
    ppermute x4, starting transfers between devices, shift(): lax.ppermute(x, 'pts', [(i, i + step) for i in range(count) if 0 <= i + s...  8.96 us
    all_to_all x1, starting transfers between devices, on_device(): got = lax.all_to_all(packed, 'pts', 0, 0, tiled=True)  7.41 us
  transfers between devices with their start and end apart: 20, of which 14 were waited for; matrix products, arithmetic and copies ran while one was open for 3% of the time, Pallas kernels for 13%

commit v1 on v0

v1 whole, which is shorter than its diff:
```python
import functools

import jax
import jax.numpy as jnp
from jax import lax
from jax.experimental import pallas as pl
from jax.experimental.pallas import tpu as pltpu
from jax.sharding import PartitionSpec as P

BF = jnp.bfloat16
F32 = jnp.float32
I32 = jnp.int32
I16 = jnp.int16
C = 256
STEPS = (-2, -1, 1, 2)
HALF = 14
PART = 7
TAIL = 16
UNIT = PART * 16 + TAIL
TOP = 32760.0
MIB = 1 << 20


def dot(a, b):
    return lax.dot_general(a, b, (((1,), (0,)), ((), ())), preferred_element_type=F32)


def dot_nt(a, b):
    return lax.dot_general(a, b, (((1,), (1,)), ((), ())), preferred_element_type=F32)


def one_hot(index, key):
    return jnp.where(index == key, 1.0, 0.0).astype(BF)


def call(body, outs, args, smem=(), scratch=(), vmem=48, flops=0, moved=0):
    specs = [
        pl.BlockSpec(memory_space=pltpu.SMEM if i in smem else pltpu.VMEM)
        for i in range(len(args))
    ]
    shapes = [jax.ShapeDtypeStruct(s, d) for s, d in outs]
    return pl.pallas_call(
        body,
        out_shape=shapes,
        in_specs=specs,
        out_specs=[pl.BlockSpec(memory_space=pltpu.VMEM) for _ in shapes],
        scratch_shapes=list(scratch),
        compiler_params=pltpu.CompilerParams(vmem_limit_bytes=vmem * MIB),
        cost_estimate=pl.CostEstimate(flops=flops, bytes_accessed=moved, transcendentals=0),
    )(*args)


def links(near_ref, own, g):
    found = [jnp.int32(-1)] * 4
    for d in range(26):
        near = near_ref[g, d]
        for n, t in enumerate(STEPS):
            hit = jnp.logical_and(near >= 0, near == own + t)
            found[n] = jnp.where(hit, d + (d >= 13), found[n])
    return found


def key_rows(near_ref, own, g):
    v = lax.broadcasted_iota(I32, (1, 512), 1)
    i, j, k = v >> 6, (v >> 3) & 7, v & 7
    lane = lax.broadcasted_iota(I32, (1, 256), 1)
    m = lane & 63
    sends = []
    cells = jnp.full((1, 256), -100, I32)
    for n, o in enumerate(links(near_ref, own, g)):
        some = o >= 0
        o = jnp.maximum(o, 0)
        a, b, c = o // 9 - 1, (o // 3) % 3 - 1, o % 3 - 1
        sk = jnp.where(c == 0, 3, 0)
        sj = jnp.where(b == 0, 3, 0)
        rank = jnp.zeros((1, 512), I32)
        on = v >= jnp.where(some, 0, 512)
        for step, at, size in ((a, i, 3), (b, j, sj), (c, k, sk)):
            free = step == 0
            rank = (rank << jnp.where(free, 3, 0)) + at * jnp.where(free, 1, 0)
            low = jnp.where(free, 0, jnp.where(step > 0, 7, 0))
            high = jnp.where(free, 7, low)
            on = on & (at >= low) & (at <= high)
        sends.append(jnp.where(on, rank, -1))
        cell = jnp.zeros((1, 256), I32)
        for step, free_at in ((a, m >> (sk + sj)), (b, (m >> sk) & 7), (c, m & 7)):
            free = step == 0
            fixed = jnp.where(step > 0, 9, 0)
            cell = cell * 10 + (free_at + 1) * jnp.where(free, 1, 0) + jnp.where(free, 0, fixed)
        last = jnp.where(a == 0, 8, 1) << (sj + sk)
        inside = (lane >> 6 == n) & (m < jnp.where(some, last, 0))
        cells = jnp.where(inside, cell, cells)
    return sends, cells


def pack_body(me_ref, near_ref, pos_ref, x_ref, dy_ref, *refs, count, window, cap):
    *out_refs, skey_ref, ekey_ref, local_ref = refs
    rows = x_ref.shape[0]
    for g in range(2):
        sends, cells = key_rows(near_ref, me_ref[0] * 2 + g, g)
        for n in range(4):
            skey_ref[g * 4 + n : g * 4 + n + 1, :] = sends[n]
        ekey_ref[g : g + 1, :] = cells
    base = cap + TAIL
    faces_of(
        lambda g: dy_ref[g * 512 : g * 512 + 512, :],
        skey_ref,
        out_refs[window // 2 + 1].at[pl.ds(base, 192)],
        out_refs[window // 2 - 1].at[pl.ds(base, 192)],
        local_ref,
    )
    pos = pos_ref[...]
    owner = pos >> (rows.bit_length() - 1)
    local = pos & (rows - 1)
    chunk = (owner - me_ref[0] + window // 2) & (count - 1)
    member = (chunk == lax.broadcasted_iota(I32, (window, rows), 0)).astype(I32)
    lane = lax.broadcasted_iota(I32, (window, rows), 1)
    rank = member
    step = 1
    while step < rows:
        rank = rank + jnp.where(lane >= step, pltpu.roll(rank, step, 1), 0)
        step *= 2
    keys = jnp.where(member > 0, rank - 1, -1)
    line = lax.broadcasted_iota(I32, (TAIL, rows), 0)
    digits = jnp.where(line == 0, (local >> 5) + 1, jnp.where(line == 1, local & 31, 0))
    digits = digits.astype(F32).astype(BF)
    x = x_ref[...]
    slot = lax.broadcasted_iota(I32, (cap, rows), 0)
    for c in range(window):
        pick = one_hot(slot, keys[c : c + 1, :])
        out_refs[c][:cap, :] = dot(pick, x).astype(BF)
        tail = dot_nt(digits, pick)
        if cap < C:
            tail = jnp.concatenate([tail, jnp.zeros((TAIL, C - cap), F32)], axis=1)
        out_refs[c][cap : cap + TAIL, :] = tail.astype(BF)


def faces_of(rows_of, skey_ref, up_ref, down_ref, local_ref):
    slot = lax.broadcasted_iota(I32, (64, 512), 0)
    made = {}
    for g in range(2):
        rows = rows_of(g)
        pick = jnp.concatenate(
            [one_hot(slot, skey_ref[g * 4 + n : g * 4 + n + 1, :]) for n in range(4)], axis=0
        )
        face = dot(pick, rows).astype(BF)
        for n, t in enumerate(STEPS):
            made[g, t] = face[n * 64 : n * 64 + 64]
    for n, k in enumerate(((0, 2), (1, 1), (1, 2))):
        up_ref[n * 64 : n * 64 + 64, :] = made[k]
    for n, k in enumerate(((0, -1), (0, -2), (1, -2))):
        down_ref[n * 64 : n * 64 + 64, :] = made[k]
    for n, k in enumerate(((0, 1), (1, -1))):
        local_ref[n * 64 : n * 64 + 64, :] = made[k]


def order_body(*refs, cap):
    *got_refs, skey_ref, out_ref, up_ref, down_ref, local_ref = refs
    chunks = len(got_refs)
    rows = out_ref.shape[0]
    targets = []
    for c in range(chunks):
        tail = got_refs[c][cap : cap + TAIL, :].astype(F32)
        place = (tail[0:1] - 1.0) * 32.0 + tail[1:2]
        targets.append(place[:, :cap].astype(I32))
    for m in range(0, rows, 256):
        slot = lax.broadcasted_iota(I32, (256, cap), 0) + m
        total = jnp.zeros((256, C), F32)
        for c in range(chunks):
            total = total + dot(one_hot(slot, targets[c]), got_refs[c][:cap, :])
        out_ref[m : m + 256, :] = total.astype(BF)
    faces_of(lambda g: out_ref[g * 512 : g * 512 + 512, :], skey_ref, up_ref, down_ref, local_ref)


FACE_OUTS = [((192, C), BF), ((192, C), BF), ((128, C), BF)]


def fill_grid(block, x, pieces, ekey, grid_ref):
    wide = x.astype(F32)
    k_of = lax.broadcasted_iota(I32, (512, C), 0) & 7
    row = lax.broadcasted_iota(I32, (800, C), 0)
    cell = (row >> 3) * 10 + (row & 7) + 1
    for ci, c in enumerate((-1, 0, 1)):
        rim = dot(one_hot(cell, ekey - c), pieces)
        if c == 0:
            moved = wide
        elif c < 0:
            moved = jnp.where(k_of == 0, 0.0, pltpu.roll(wide, 1, 0))
        else:
            moved = jnp.where(k_of == 7, 0.0, pltpu.roll(wide, 511, 0))
        for i in range(10):
            stripe = rim[i * 80 : i * 80 + 80]
            if 1 <= i <= 8:
                inner = stripe[8:72] + moved[i * 64 - 64 : i * 64]
                stripe = jnp.concatenate([stripe[:8], inner, stripe[72:]], axis=0)
            grid_ref[block, ci, i * 80 : i * 80 + 80, :] = stripe.astype(BF)


def shifted(grid_ref, block, a, b, c):
    lines = []
    for i in range(8):
        start = (i + a) * 80 + b * 8
        if not isinstance(start, int):
            start = pl.multiple_of(start, 8)
        lines.append(grid_ref[block, c, pl.ds(start, 64), :])
    return jnp.concatenate(lines, axis=0)


def fill_grids(x_ref, up_ref, down_ref, local_ref, ekey_ref, grid_ref, base=0, blocks=(0, 1)):
    def piece(ref, n):
        start = n * 64 + (0 if ref is local_ref else base)
        return ref[start : start + 64, :]

    for at, g in enumerate(blocks):
        if g == 0:
            source = ((up_ref, 0), (up_ref, 1), (local_ref, 1), (down_ref, 1))
        else:
            source = ((up_ref, 2), (local_ref, 0), (down_ref, 0), (down_ref, 2))
        fill_grid(
            at,
            x_ref[g * 512 : g * 512 + 512, :],
            jnp.concatenate([piece(*p) for p in source], axis=0),
            ekey_ref[g : g + 1, :],
            grid_ref,
        )


def convolve(x_ref, grid_ref, weight_ref, out_ref, acc_ref, flip, blocks=(0, 1)):
    for at, g in enumerate(blocks):
        acc_ref[at * 512 : at * 512 + 512, :] = x_ref[g * 512 : g * 512 + 512, :].astype(F32)
    for ab in range(9):
        a, b = ab // 3, ab % 3
        for at, g in enumerate(blocks):
            total = acc_ref[at * 512 : at * 512 + 512, :]
            for c in range(3):
                rows = shifted(grid_ref, at, a, b, c)
                if flip:
                    total = total + dot_nt(rows, weight_ref[26 - (ab * 3 + c)])
                else:
                    total = total + dot(rows, weight_ref[ab * 3 + c])
            acc_ref[at * 512 : at * 512 + 512, :] = total
    for at, g in enumerate(blocks):
        out_ref[g * 512 : g * 512 + 512, :] = acc_ref[at * 512 : at * 512 + 512, :].astype(BF)


def turn_body(x_ref, out_ref):
    out_ref[...] = x_ref[...].astype(F32).T.astype(BF)


def backward_first_body(x, up, down, local, ekey, weight_ref, out_ref, grid_ref, acc_ref, *, base):
    fill_grids(x, up, down, local, ekey, grid_ref, base, (0,))
    convolve(x, grid_ref, weight_ref, out_ref, acc_ref, True, (0,))


def backward_body(x, up, down, local, ekey, weight_ref, first_ref, out_ref, grid_ref, acc_ref, *, base):
    fill_grids(x, up, down, local, ekey, grid_ref, base, (1,))
    out_ref[:512, :] = first_ref[...]
    convolve(x, grid_ref, weight_ref, out_ref, acc_ref, True, (1,))


def forward_body(x_ref, grid_ref, weight_ref, out_ref, acc_ref):
    convolve(x_ref, grid_ref, weight_ref, out_ref, acc_ref, False)


GRID = (2, 3, 800, C)


def scale_code(peak):
    peak = jnp.maximum(peak, 1e-30)
    power = jnp.floor(jnp.log2(peak))
    part = jnp.clip(jnp.ceil(peak * jnp.exp2(-power) * 64.0), 1.0, 200.0)
    return power * 256.0 + part


def scale_of(code):
    power = jnp.floor(code * (1.0 / 256.0))
    return jnp.exp2(power) * (code - power * 256.0) * (1.0 / 64.0)


def encode(values):
    code = scale_code(jnp.max(jnp.abs(values), axis=0, keepdims=True))
    return code, jnp.round(values * (TOP / scale_of(code))).astype(I32).astype(I16)


def decode(values, code):
    return values.astype(I32).astype(F32) * (scale_of(code) * (1.0 / TOP))


def tail_of(codes):
    lines = list(codes) + [jnp.zeros((1, C), F32)] * (TAIL - len(codes))
    return jnp.concatenate(lines, axis=0).astype(I32).astype(I16)


def tail_codes(ref, start):
    return ref[start : start + TAIL, :].astype(I32).astype(F32)


def term(grid_ref, turned_ref, offset):
    at = jnp.minimum(offset, 26)
    a, b, c = at // 9, (at // 3) % 3, at % 3
    total = dot(turned_ref[:, :512], shifted(grid_ref, 0, a, b, c))
    total = total + dot(turned_ref[:, 512:], shifted(grid_ref, 1, a, b, c))
    return jnp.where(offset < 27, total, 0.0)


def send_terms(bits_ref, grid_ref, turned_ref, send_ref, first):
    codes = []
    for i in range(PART):
        offset = (1 - bits_ref[0]) * HALF + first + i
        code, values = encode(term(grid_ref, turned_ref, offset))
        codes.append(code)
        send_ref[i * 256 : i * 256 + 256, :] = values
    send_ref[PART * 256 :, :] = tail_of(codes)


def first_terms_body(bits_ref, x, up, down, local, ekey, turned_ref, grid_ref, send_ref):
    fill_grids(x, up, down, local, ekey, grid_ref)
    send_terms(bits_ref, grid_ref, turned_ref, send_ref, 0)


def more_terms_body(bits_ref, grid_ref, turned_ref, send_ref):
    send_terms(bits_ref, grid_ref, turned_ref, send_ref, PART)


def own_terms_body(bits_ref, grid_ref, turned_ref, got_ref, keep_ref, send_ref, *, first, which):
    tail = tail_codes(got_ref, PART * 256)
    upper = bits_ref[which] > 0
    codes = []
    for i in range(PART):
        total = term(grid_ref, turned_ref, bits_ref[0] * HALF + first + i)
        total = total + decode(got_ref[i * 256 : i * 256 + 256, :], tail[i : i + 1])
        keep_ref[i] = jnp.where(upper, total[128:], total[:128])
        code, values = encode(jnp.where(upper, total[:128], total[128:]))
        codes.append(code)
        send_ref[i * 128 : i * 128 + 128, :] = values
    send_ref[PART * 128 :, :] = tail_of(codes)


def reduce_body(*refs, which, parts, rows):
    bits_ref, keep_ref, send_ref = refs[0], refs[-2], refs[-1]
    half = rows // 2
    mine = bits_ref[which]
    keep_at = pl.multiple_of(mine * half, half)
    send_at = pl.multiple_of((1 - mine) * half, half)
    codes = []
    for n, (first, many, total) in enumerate(parts):
        acc_ref, got_ref = refs[1 + 2 * n], refs[2 + 2 * n]
        tail = tail_codes(got_ref, total * rows)
        for i in range(first, first + many):
            at = len(codes)
            code = tail[i : i + 1]
            wide = acc_ref[i, pl.ds(send_at, half), :] + decode(
                got_ref[pl.ds(i * rows + send_at, half), :], code
            )
            new, values = encode(wide)
            codes.append(new)
            send_ref[at * half : at * half + half, :] = values
            keep_ref[at] = acc_ref[i, pl.ds(keep_at, half), :] + decode(
                got_ref[pl.ds(i * rows + keep_at, half), :], code
            )
    send_ref[len(codes) * half :, :] = tail_of(codes)


def reduce_step(bits, which, operands, parts, rows):
    many = sum(p[1] for p in parts)
    half = rows // 2
    outs = [((many, half, C), F32), ((many * half + TAIL, C), I16)]
    body = functools.partial(reduce_body, which=which, parts=parts, rows=rows)
    return call(body, outs, [bits, *operands], smem=(0,), moved=many * rows * C * 8)


def total_body(acc_ref, got_ref, out_ref):
    tail = tail_codes(got_ref, HALF * 16)
    for i in range(HALF):
        out_ref[i] = acc_ref[i] + decode(got_ref[i * 16 : i * 16 + 16, :], tail[i : i + 1])


def unit_body(total_ref, a_ref, b_ref):
    for p, out_ref in enumerate((a_ref, b_ref)):
        codes = []
        squares = jnp.zeros((1, C), F32)
        for i in range(PART):
            value = total_ref[p * PART + i]
            squares = squares + jnp.sum(value * value, axis=0, keepdims=True)
            code, coded = encode(value)
            codes.append(code)
            out_ref[i * 16 : i * 16 + 16, :] = coded
        squares = jnp.maximum(squares, 1e-30)
        power = jnp.floor(jnp.log2(squares))
        codes.append(power)
        codes.append(jnp.round(jnp.minimum(squares * jnp.exp2(-power) * 15000.0, 32000.0)))
        out_ref[PART * 16 :, :] = tail_of(codes)


def finish_body(bits_ref, *refs):
    out_ref, wide_ref, square_ref = refs[8:]
    mine = bits_ref[0]
    halves = (mine, 1 - mine)

    def place_of(p, u):
        place = 0
        for n, which in enumerate(((1, 2, 3, 4), (2, 1, 3, 4))[p]):
            place = place * 2 + (bits_ref[which] ^ ((u >> (3 - n)) & 1))
        return place

    def ref_of(side, p, u):
        return refs[side * 4 + p * 2 + u // 8], (u % 8) * UNIT

    for side in range(2):
        for p in range(2):
            for u in range(16):
                ref, at = ref_of(side, p, u)
                tail = tail_codes(ref, at + PART * 16)
                square_ref[pl.ds(halves[side] * 32 + p * 16 + place_of(p, u), 1), :] = (
                    jnp.exp2(tail[PART : PART + 1]) * tail[PART + 1 : PART + 2]
                )
    squares = jnp.sum(square_ref[...], axis=0, keepdims=True)
    mean = jnp.sum(squares, axis=1, keepdims=True) * (1.0 / (15000.0 * 27 * C * C))
    gain = 1.0 / jnp.sqrt(mean + 1e-06)
    for side in range(2):
        for p in range(2):
            places, scales = [], []
            for u in range(16):
                ref, at = ref_of(side, p, u)
                places.append(pl.multiple_of(place_of(p, u) * 16, 16))
                scales.append(scale_of(tail_codes(ref, at + PART * 16)[:8]) * gain * (1.0 / TOP))
            for i in range(PART):
                for u in range(16):
                    ref, at = ref_of(side, p, u)
                    coded = ref[at + i * 16 : at + i * 16 + 16, :]
                    wide_ref[i % 2, pl.ds(places[u], 16), :] = (
                        coded.astype(I32).astype(F32) * scales[u][i : i + 1]
                    ).astype(BF)
                offset = halves[side] * HALF + p * PART + i

                @pl.when(offset < 27)
                def _():
                    out_ref[offset] = wide_ref[i % 2].T


def swap(x, bit):
    axis, place = bit
    count = lax.axis_size(axis)
    return lax.ppermute(x, axis, [(i, i ^ (1 << place)) for i in range(count)])


def shift(x, step):
    count = lax.axis_size("pts")
    return lax.ppermute(
        x, "pts", [(i, i + step) for i in range(count) if 0 <= i + step < count]
    )


def device_bits():
    dp = lax.axis_size("dp").bit_length() - 1
    pts = lax.axis_size("pts").bit_length() - 1
    order = [("dp", n) for n in range(dp)] + [("pts", n) for n in range(pts)]
    return order[:5], order[5:]


def bit_value(bit):
    return (lax.axis_index(bit[0]) >> bit[1]) & 1


def on_device(features, hilbert_pos, weight, neighbours, grad_out):
    rows = features.shape[1]
    count = lax.axis_size("pts")
    me = lax.axis_index("pts").astype(I32)
    window = min(16, count)
    cap = 2 * rows // window
    split, extra = device_bits()
    bits = jnp.stack([bit_value(b) for b in split]).astype(I32)
    s0, s1, s2, s3, s4 = split

    dy = grad_out[0]
    lines = [cap + TAIL + (192 if abs(w - window // 2) == 1 else 0) for w in range(window)]
    *packed, skey, ekey, dy_local = call(
        functools.partial(pack_body, count=count, window=window, cap=cap),
        [*(((n, C), BF) for n in lines), ((8, 512), I32), ((2, C), I32), ((128, C), BF)],
        [me.reshape(1), neighbours[0], hilbert_pos, features[0], dy],
        smem=(0, 1),
        flops=4 * rows * rows * C,
        moved=4 * rows * C * 2,
    )
    got = [None] * window
    for w in sorted(range(window), key=lambda w: (-abs(w - window // 2), w)):
        step = w - window // 2
        turn = [(i, (i + step) % count) for i in range(count)]
        got[w] = packed[w] if step == 0 else lax.ppermute(packed[w], "pts", turn)

    conv_flops = 2 * 27 * rows * C * C
    part_flops = conv_flops // 4
    (turned,) = call(turn_body, [((C, rows), BF)], [dy])

    x, up, down, x_local = call(
        functools.partial(order_body, cap=cap),
        [((rows, C), BF), *FACE_OUTS],
        [*got, skey],
        flops=4 * rows * rows * C,
        moved=4 * rows * C * 2,
    )
    x_up, x_down = shift(up, 1), shift(down, -1)
    grid, send_a = call(
        first_terms_body,
        [(GRID, BF), ((PART * C + TAIL, C), I16)],
        [bits, x, x_up, x_down, x_local, ekey, turned],
        smem=(0,),
        flops=part_flops,
        moved=5 * MIB,
    )
    came_a = swap(send_a, s0)
    (send_b,) = call(
        more_terms_body,
        [((PART * C + TAIL, C), I16)],
        [bits, grid, turned],
        smem=(0,),
        flops=part_flops,
        moved=5 * MIB,
    )
    came_b = swap(send_b, s0)
    own_outs = [((PART, 128, C), F32), ((PART * 128 + TAIL, C), I16)]
    keep_a, send_a = call(
        functools.partial(own_terms_body, first=0, which=1),
        own_outs,
        [bits, grid, turned, came_a],
        smem=(0,),
        flops=part_flops,
        moved=5 * MIB,
    )
    came_a = swap(send_a, s1)
    keep_b, send_b = call(
        functools.partial(own_terms_body, first=PART, which=2),
        own_outs,
        [bits, grid, turned, came_b],
        smem=(0,),
        flops=part_flops,
        moved=5 * MIB,
    )
    came_b = swap(send_b, s2)
    x, grid, keep_b = lax.optimization_barrier((x, grid, keep_b))
    (forward,) = call(
        forward_body,
        [((rows, C), BF)],
        [x, grid, weight],
        scratch=[pltpu.VMEM((rows, C), F32)],
        flops=conv_flops,
        moved=6 * MIB,
    )
    forward, came_a, came_b = lax.optimization_barrier((forward, came_a, came_b))

    keep_a, send_a = reduce_step(bits, 2, [keep_a, came_a], ((0, PART, PART),), 128)
    keep_b, send_b = reduce_step(bits, 1, [keep_b, came_b], ((0, PART, PART),), 128)
    came_a, came_b = swap(send_a, s2), swap(send_b, s1)
    keep, send = reduce_step(
        bits, 3, [keep_a, came_a, keep_b, came_b], ((0, PART, PART), (0, PART, PART)), 64
    )
    came = swap(send, s3)
    keep, send = reduce_step(bits, 4, [keep, came], ((0, HALF, HALF),), 32)
    came = swap(send, s4)
    (total,) = call(total_body, [((HALF, 16, C), F32)], [keep, came])
    for b in extra:
        total = total + swap(total, b)
    unit_a, unit_b = call(unit_body, [((UNIT, C), I16), ((UNIT, C), I16)], [total])

    unit_a, unit_b, dy = lax.optimization_barrier((unit_a, unit_b, dy))
    back_args = [got[window // 2 + 1], got[window // 2 - 1], dy_local, ekey, weight]
    back_scratch = [pltpu.VMEM((1, 3, 800, C), BF), pltpu.VMEM((512, C), F32)]
    far = swap(jnp.concatenate([unit_a, unit_b], axis=0), s4)
    (backward,) = call(
        functools.partial(backward_first_body, base=cap + TAIL),
        [((512, C), BF)],
        [dy, *back_args],
        scratch=back_scratch,
        flops=conv_flops // 2,
        moved=5 * MIB,
    )
    far, backward, dy = lax.optimization_barrier((far, backward, dy))
    unit_a = jnp.concatenate([unit_a, far[:UNIT]], axis=0)
    unit_b = jnp.concatenate([unit_b, far[UNIT:]], axis=0)
    far = swap(jnp.concatenate([unit_a, unit_b], axis=0), s3)
    (backward,) = call(
        functools.partial(backward_body, base=cap + TAIL),
        [((rows, C), BF)],
        [dy, *back_args, backward],
        scratch=back_scratch,
        flops=conv_flops // 2,
        moved=5 * MIB,
    )
    far, backward = lax.optimization_barrier((far, backward))
    unit_a = jnp.concatenate([unit_a, far[: 2 * UNIT]], axis=0)
    unit_b = jnp.concatenate([unit_b, far[2 * UNIT :]], axis=0)
    far_a, far_b = swap(unit_a, s2), swap(unit_b, s1)
    unit_a = jnp.concatenate([unit_a, far_a], axis=0)
    unit_b = jnp.concatenate([unit_b, far_b], axis=0)
    far_a, far_b = swap(unit_a, s1), swap(unit_b, s2)
    other_a, other_b = swap(unit_a, s0), swap(unit_b, s0)
    other_far_a, other_far_b = swap(far_a, s0), swap(far_b, s0)
    (weight_grad,) = call(
        finish_body,
        [((27, C, C), BF)],
        [bits, unit_a, far_a, unit_b, far_b, other_a, other_far_a, other_b, other_far_b],
        smem=(0,),
        scratch=[pltpu.VMEM((2, C, C), BF), pltpu.VMEM((64, C), F32)],
    )
    return forward[None], backward[None], weight_grad


def solution(mesh):
    placed = (P("dp", "pts", None), P("dp", "pts"), P(), P("dp", "pts", None), P("dp", "pts", None))
    return jax.shard_map(
        on_device,
        mesh=mesh,
        in_specs=placed,
        out_specs=(P("dp", "pts", None), P("dp", "pts", None), P()),
        check_vma=False,
    )
```

time: 165 us -> 145 us (0.88)
  waiting for transfers between devices: 76.2 us -> 54.6 us
  starting transfers between devices: 31.5 us -> 48.4 us
  Pallas kernels: 48.8 us -> 37.1 us
  local copies, waits for them, and re-layouts: 6.03 us -> 3.56 us
    ppermute x15 -> x18, waiting for transfers between devices: 58.4 us -> 38.9 us  [swap(): return lax.ppermute(x, axis, [(i, i ^ 1 << place) for i in range(count)])]
    ppermute x0 -> x7, starting transfers between devices: none -> 19 us  [on_device(): got[w] = packed[w] if step == 0 else lax.ppermute(packed[w], 'pts', turn)]
    all_to_all x1 -> x0, waiting for transfers between devices: 17.8 us -> none  [on_device(): got = lax.all_to_all(packed, 'pts', 0, 0, tiled=True)]
    pallas_call x15 -> x17, Pallas kernels: 48.8 us -> 37.1 us  [call(): pl.pallas_call(body, out_shape=shapes, in_specs=specs, out_specs=[pl.Bloc...]
    ppermute x0 -> x7, waiting for transfers between devices: none -> 11 us  [on_device(): got[w] = packed[w] if step == 0 else lax.ppermute(packed[w], 'pts', turn)]
    all_to_all x1 -> x0, starting transfers between devices: 7.41 us -> none  [on_device(): got = lax.all_to_all(packed, 'pts', 0, 0, tiled=True)]
    ppermute x15 -> x18, starting transfers between devices: 15.1 us -> 22.3 us  [swap(): return lax.ppermute(x, axis, [(i, i ^ 1 << place) for i in range(count)])]
    ppermute x4 -> x2, waiting for transfers between devices: 0.01 us -> 4.71 us  [shift(): lax.ppermute(x, 'pts', [(i, i + step) for i in range(count) if 0 <= i + s...]
  transfers between devices with their start and end apart: 20 -> 27, of which waited for: 14 -> 17; matrix products, arithmetic and copies ran while one was open for 3% -> 0% of each run, Pallas kernels for 13% -> 13%
where the time goes in v1:
time: 145 us
  waiting for transfers between devices  54.6 us (38%)
  starting transfers between devices  48.4 us (33%)
  Pallas kernels  37.1 us (26%)
  local copies, waits for them, and re-layouts  3.56 us (2%)
    ppermute x18, waiting for transfers between devices, swap(): return lax.ppermute(x, axis, [(i, i ^ 1 << place) for i in range(count)])  38.9 us
    pallas_call x17, Pallas kernels, call(): pl.pallas_call(body, out_shape=shapes, in_specs=specs, out_specs=[pl.Bloc...  37.1 us
    ppermute x18, starting transfers between devices, swap(): return lax.ppermute(x, axis, [(i, i ^ 1 << place) for i in range(count)])  22.3 us
    ppermute x7, starting transfers between devices, on_device(): got[w] = packed[w] if step == 0 else lax.ppermute(packed[w], 'pts', turn)  19 us
    ppermute x7, waiting for transfers between devices, on_device(): got[w] = packed[w] if step == 0 else lax.ppermute(packed[w], 'pts', turn)  11 us
    ppermute x2, starting transfers between devices, shift(): lax.ppermute(x, 'pts', [(i, i + step) for i in range(count) if 0 <= i + s...  7.04 us
    ppermute x2, waiting for transfers between devices, shift(): lax.ppermute(x, 'pts', [(i, i + step) for i in range(count) if 0 <= i + s...  4.71 us
    unnamed x12, local copies, waits for them, and re-layouts  3.45 us
  transfers between devices with their start and end apart: 27, of which 17 were waited for; matrix products, arithmetic and copies ran while one was open for 0% of the time, Pallas kernels for 13%

profile of v1, /device:TPU:0, one launch (start us, length us, event | category | flops | bytes accessed | tf_op | source)
XLA Modules:
  0.0 144.7 jit_solution(3281280336094173378)
XLA Ops:
  0.6 1.0 copy-done
  1.7 1.0 copy-done.3
  2.7 0.7 copy-done.4
  3.4 0.7 copy-done.5
  4.1 3.6 %shard_map.76 = (bf16[272,256]{1,0:T(8,128)(2,1)S(1)}, bf16[272,256]{1,0:T(8,128)(2,1)S(1)}, bf16[272,256]{1,0:T(8,128)(2,1)S(1)}, bf16[464,256]{1,0:T(8,128)(2,...) custom-call(s32[1]{0:T(128)} %bitcast.me_ref, ...), custom_call_target="tpu_custom_call" | custom-call | flops 1073741824 | bytes 2097152 | tf_op jit(solution)/shard_map/pallas_call | solution.py:42
  7.7 4.1 %collective-permute-start = (bf16[272,256]{1,0:T(8,128)(2,1)S(1)}, bf16[272,256]{1,0:T(8,128)(2,1)S(1)}, u32[]{:S(2)}, u32[]{:S(2)}) collective-permute-start(bf16[272,256]{1,0:T(8,128)(2,1)S(1)} %get-tuple-element.48), channel_id=1, source_target_pairs={{0,16},{4,20},{8,24},{12,28},{16,0},{20,4},{24,8},{28,12},{1,17},{... | collective-permute-start | bytes 417800 | tf_op jit(solution)/shard_map/ppermute | solution.py:489
  11.8 1.3 collective-permute-start.1
  13.0 1.1 collective-permute-start.3
  14.2 0.9 collective-permute-start.4
  15.1 3.6 %collective-permute-start.2 = (bf16[272,256]{1,0:T(8,128)(2,1)S(1)}, bf16[272,256]{1,0:T(8,128)(2,1)S(1)}, u32[]{:S(2)}, u32[]{:S(2)}) collective-permute-start(bf16[272,256]{1,0:T(8,128)(2,1)S(1)} %get-tuple-element.50), channel_id=1, source_target_pairs={{0,24},{4,28},{8,0},{12,4},{16,8},{20,12},{24,16},{28,20},{1,25},{... | collective-permute-start | bytes 417800 | tf_op jit(solution)/shard_map/ppermute | solution.py:489
  18.7 3.7 %collective-permute-done.refs_0_ = bf16[272,256]{1,0:T(8,128)(2,1)S(1)} collective-permute-done((bf16[272,256]{1,0:T(8,128)(2,1)S(1)}, bf16[272,256]{1,0:T(8,128)(2,1)S(1)}, u32[]{:S(2)}, u32[]{:S(2)}) %collective-permute-start) | collective-permute-done | bytes 139296 | tf_op jit(solution)/shard_map/ppermute | solution.py:489
  22.3 8.0 %collective-permute-start.5 = (bf16[272,256]{1,0:T(8,128)(2,1)S(1)}, bf16[272,256]{1,0:T(8,128)(2,1)S(1)}, u32[]{:S(2)}, u32[]{:S(2)}) collective-permute-start(bf16[272,256]{1,0:T(8,128)(2,1)S(1)} %get-tuple-element.54), channel_id=1, source_target_pairs={{0,8},{4,12},{8,16},{12,20},{16,24},{20,28},{24,0},{28,4},{1,9},{5... | collective-permute-start | bytes 417800 | tf_op jit(solution)/shard_map/ppermute | solution.py:489
  30.3 0.0 collective-permute-done.1.refs_1_
  30.3 0.0 collective-permute-start.6
  30.3 0.0 collective-permute-done.2.refs_2_
  30.3 7.3 %collective-permute-done.5.refs_6_ = bf16[272,256]{1,0:T(8,128)(2,1)S(1)} collective-permute-done((bf16[272,256]{1,0:T(8,128)(2,1)S(1)}, bf16[272,256]{1,0:T(8,128)(2,1)S(1)}, u32[]{:S(2)}, u32[]{:S(2)}) %collective-permute-start.5) | collective-permute-done | bytes 139296 | tf_op jit(solution)/shard_map/ppermute | solution.py:489
  37.7 1.5 %shard_map.77 = (bf16[1024,256]{1,0:T(8,128)(2,1)S(1)}, bf16[192,256]{1,0:T(8,128)(2,1)S(1)}, bf16[192,256]{1,0:T(8,128)(2,1)S(1)}, bf16[128,256]{1,0:T(8,128)(2,1)S(1)}) custom-call(bf16[272,256]{1,0:T(8,128)(2,1)S(1)} %collective-permute-done.refs_0_, bf16[272,256]{1,0:T(8,128)(2,1)S(1)} %collective-permute-done.1.refs_1_, ...), custom_call_target="tpu_custom_call" | custom-call | flops 1073741824 | bytes 2097152 | tf_op jit(solution)/shard_map/pallas_call | solution.py:42
  39.2 5.6 %collective-permute-start.7 = (bf16[192,256]{1,0:T(8,128)(2,1)S(1)}, bf16[192,256]{1,0:T(8,128)(2,1)S(1)}, u32[]{:S(2)}, u32[]{:S(2)}) collective-permute-start(bf16[192,256]{1,0:T(8,128)(2,1)S(1)} %get-tuple-element.58), channel_id=1, source_target_pairs={{0,4},{4,8},{8,12},{12,16},{16,20},{20,24},{24,28},{1,5},{5,9},{9,... | collective-permute-start | bytes 294920 | tf_op jit(solution)/shard_map/ppermute | solution.py:449
  44.7 1.5 %collective-permute-start.8 = (bf16[192,256]{1,0:T(8,128)(2,1)S(1)}, bf16[192,256]{1,0:T(8,128)(2,1)S(1)}, u32[]{:S(2)}, u32[]{:S(2)}) collective-permute-start(bf16[192,256]{1,0:T(8,128)(2,1)S(1)} %get-tuple-element.59), channel_id=1, source_target_pairs={{4,0},{8,4},{12,8},{16,12},{20,16},{24,20},{28,24},{5,1},{9,5},{13... | collective-permute-start | bytes 294920 | tf_op jit(solution)/shard_map/ppermute | solution.py:449
  46.2 0.2 shard_map.78.turned_ref
  46.5 0.1 stack.23.bits_ref.refs_0_
  46.5 0.4 collective-permute-done.7.up
  46.9 4.3 %collective-permute-done.8.down = bf16[192,256]{1,0:T(8,128)(2,1)S(1)} collective-permute-done((bf16[192,256]{1,0:T(8,128)(2,1)S(1)}, bf16[192,256]{1,0:T(8,128)(2,1)S(1)}, u32[]{:S(2)}, u32[]{:S(2)}) %collective-permute-start.8) | collective-permute-done | bytes 98336 | tf_op jit(solution)/shard_map/ppermute | solution.py:449
  51.3 3.1 %shard_map.79 = (bf16[2,3,800,256]{3,2,1,0:T(8,128)(2,1)S(1)}, s16[1808,256]{1,0:T(8,128)(2,1)S(1)}) custom-call(s32[5]{0:T(128)S(1)} %stack.23.bits_ref.refs_0_, bf16[1024,256]{1,0:T(8,128)(2,1)S(1)} %get-tuple-element.64.x.x_ref, bf16[192,256]{1,0:T(8,128)(2,1)S(1)} %collective-permute-done.7.up, bf16[192,256]{1,0:T(8,128)(2,1)S(1)} %collective-permute-done.8.down, ...), custom_call_target="tpu_custom_call" | custom-call | flops 905969664 | bytes 5242880 | tf_op jit(solution)/shard_map/pallas_call | solution.py:42
  54.3 1.9 %shard_map.80 = s16[1808,256]{1,0:T(8,128)(2,1)S(1)} custom-call(s32[5]{0:T(128)S(1)} %stack.23.bits_ref.refs_0_, bf16[2,3,800,256]{3,2,1,0:T(8,128)(2,1)S(1)} %get-tuple-element.65.grid_ref, bf16[256,1024]{1,0:T(8,128)(2,1)S(1)} %shard_map.78.turned_ref), custom_call_target="tpu_custom_call" | custom-call | flops 905969664 | bytes 5242880 | tf_op jit(solution)/shard_map/pallas_call | solution.py:42
  56.2 0.1 collective-permute-start.9
  56.3 0.5 collective-permute-start.10
  56.8 2.0 %collective-permute-done.9.got_ref = s16[1808,256]{1,0:T(8,128)(2,1)S(1)} collective-permute-done((s16[1808,256]{1,0:T(8,128)(2,1)S(1)}, s16[1808,256]{1,0:T(8,128)(2,1)S(1)}, u32[]{:S(2)}, u32[]{:S(2)}) %collective-permute-start.9) | collective-permute-done | bytes 925728 | tf_op jit(solution)/shard_map/ppermute | solution.py:444
  58.8 1.9 %shard_map.81 = (f32[7,128,256]{2,1,0:T(8,128)S(1)}, s16[912,256]{1,0:T(8,128)(2,1)S(1)}) custom-call(s32[5]{0:T(128)S(1)} %stack.23.bits_ref.refs_0_, bf16[2,3,800,256]{3,2,1,0:T(8,128)(2,1)S(1)} %get-tuple-element.65.grid_ref, bf16[256,1024]{1,0:T(8,128)(2,1)S(1)} %shard_map.78.turned_ref, s16[1808,256]{1,0:T(8,128)(2,1)S(1)} %collective-permute-done.9.got_ref), custom_call_target="tpu_custom_call" | custom-call | flops 905969664 | bytes 5242880 | tf_op jit(solution)/shard_map/pallas_call | solution.py:42
  60.6 2.4 %collective-permute-start.12 = (s16[912,256]{1,0:T(8,128)(2,1)S(1)}, s16[912,256]{1,0:T(8,128)(2,1)S(1)}, u32[]{:S(2)}, u32[]{:S(2)}) collective-permute-start(s16[912,256]{1,0:T(8,128)(2,1)S(1)} %get-tuple-element.68), channel_id=1, source_target_pairs={{0,4},{4,0},{8,12},{12,8},{16,20},{20,16},{24,28},{28,24},{1,5},{5... | collective-permute-start | bytes 1400840 | tf_op jit(solution)/shard_map/ppermute | solution.py:444
  63.1 1.9 %shard_map.83 = (f32[7,128,256]{2,1,0:T(8,128)S(1)}, s16[912,256]{1,0:T(8,128)(2,1)S(1)}) custom-call(s32[5]{0:T(128)S(1)} %stack.23.bits_ref.refs_0_, bf16[2,3,800,256]{3,2,1,0:T(8,128)(2,1)S(1)} %get-tuple-element.65.grid_ref, bf16[256,1024]{1,0:T(8,128)(2,1)S(1)} %shard_map.78.turned_ref, s16[1808,256]{1,0:T(8,128)(2,1)S(1)} %collective-permute-done.10.got_ref), custom_call_target="tpu_custom_call" | custom-call | flops 905969664 | bytes 5242880 | tf_op jit(solution)/shard_map/pallas_call | solution.py:42
  65.0 1.6 %collective-permute-start.11 = (s16[912,256]{1,0:T(8,128)(2,1)S(1)}, s16[912,256]{1,0:T(8,128)(2,1)S(1)}, u32[]{:S(2)}, u32[]{:S(2)}) collective-permute-start(s16[912,256]{1,0:T(8,128)(2,1)S(1)} %get-tuple-element.67), channel_id=1, source_target_pairs={{0,2},{1,3},{2,0},{3,1},{4,6},{5,7},{6,4},{7,5},{8,10},{9,11},{10,... | collective-permute-start | bytes 1400840 | tf_op jit(solution)/shard_map/ppermute | solution.py:444
  66.5 6.6 %shard_map.82 = bf16[1024,256]{1,0:T(8,128)(2,1)} custom-call(bf16[1024,256]{1,0:T(8,128)(2,1)S(1)} %get-tuple-element.64.x.x_ref, bf16[2,3,800,256]{3,2,1,0:T(8,128)(2,1)S(1)} %get-tuple-element.65.grid_ref, bf16[27,256,256]{2,1,0:T(8,128)(2,1)} %weight_ref.5), custom_call_target="tpu_custom_call" | custom-call | flops 3623878656 | bytes 6291456 | tf_op jit(solution)/shard_map/pallas_call | solution.py:42
  73.1 0.9 collective-permute-done.12.refs_2_
  74.1 3.4 %collective-permute-done.11.refs_2_ = s16[912,256]{1,0:T(8,128)(2,1)S(1)} collective-permute-done((s16[912,256]{1,0:T(8,128)(2,1)S(1)}, s16[912,256]{1,0:T(8,128)(2,1)S(1)}, u32[]{:S(2)}, u32[]{:S(2)}) %collective-permute-start.11) | collective-permute-done | bytes 466976 | tf_op jit(solution)/shard_map/ppermute | solution.py:444
  77.5 0.8 shard_map.84
  78.3 0.4 collective-permute-start.13
  78.7 0.8 shard_map.85
  79.5 1.6 %collective-permute-start.14 = (s16[464,256]{1,0:T(8,128)(2,1)S(1)}, s16[464,256]{1,0:T(8,128)(2,1)S(1)}, u32[]{:S(2)}, u32[]{:S(2)}) collective-permute-start(s16[464,256]{1,0:T(8,128)(2,1)S(1)} %get-tuple-element.77), channel_id=1, source_target_pairs={{0,2},{1,3},{2,0},{3,1},{4,6},{5,7},{6,4},{7,5},{8,10},{9,11},{10,... | collective-permute-start | bytes 712712 | tf_op jit(solution)/shard_map/ppermute | solution.py:444
  81.0 4.0 %collective-permute-done.13.refs_2_ = s16[464,256]{1,0:T(8,128)(2,1)S(1)} collective-permute-done((s16[464,256]{1,0:T(8,128)(2,1)S(1)}, s16[464,256]{1,0:T(8,128)(2,1)S(1)}, u32[]{:S(2)}, u32[]{:S(2)}) %collective-permute-start.13) | collective-permute-done | bytes 237600 | tf_op jit(solution)/shard_map/ppermute | solution.py:444
  85.1 1.2 collective-permute-done.14.refs_4_
  86.2 0.9 shard_map.86
  87.1 0.1 collective-permute-start.15
  87.2 6.1 %collective-permute-done.15.refs_2_ = s16[464,256]{1,0:T(8,128)(2,1)S(1)} collective-permute-done((s16[464,256]{1,0:T(8,128)(2,1)S(1)}, s16[464,256]{1,0:T(8,128)(2,1)S(1)}, u32[]{:S(2)}, u32[]{:S(2)}) %collective-permute-start.15) | collective-permute-done | bytes 237600 | tf_op jit(solution)/shard_map/ppermute | solution.py:444
  93.3 0.8 shard_map.87
  94.0 3.7 %collective-permute-start.16 = (s16[240,256]{1,0:T(8,128)(2,1)S(1)}, s16[240,256]{1,0:T(8,128)(2,1)S(1)}, u32[]{:S(2)}, u32[]{:S(2)}) collective-permute-start(s16[240,256]{1,0:T(8,128)(2,1)S(1)} %get-tuple-element.81), channel_id=1, source_target_pairs={{0,16},{4,20},{8,24},{12,28},{16,0},{20,4},{24,8},{28,12},{1,17},{... | collective-permute-start | bytes 368648 | tf_op jit(solution)/shard_map/ppermute | solution.py:444
  97.7 4.7 %collective-permute-done.16.got_ref = s16[240,256]{1,0:T(8,128)(2,1)S(1)} collective-permute-done((s16[240,256]{1,0:T(8,128)(2,1)S(1)}, s16[240,256]{1,0:T(8,128)(2,1)S(1)}, u32[]{:S(2)}, u32[]{:S(2)}) %collective-permute-start.16) | collective-permute-done | bytes 122912 | tf_op jit(solution)/shard_map/ppermute | solution.py:444
  102.5 0.2 shard_map.89
  102.8 2.5 %collective-permute-start.17 = (s16[256,256]{1,0:T(8,128)(2,1)S(1)}, s16[256,256]{1,0:T(8,128)(2,1)S(1)}, u32[]{:S(2)}, u32[]{:S(2)}) collective-permute-start(s16[256,256]{1,0:T(8,128)(2,1)S(1)} %pad_add_fusion.6), channel_id=1, source_target_pairs={{0,16},{4,20},{8,24},{12,28},{16,0},{20,4},{24,8},{28,12},{1,17},{... | collective-permute-start | bytes 393224 | tf_op jit(solution)/shard_map/ppermute | solution.py:444
  105.2 2.9 %shard_map.90.first_ref = bf16[512,256]{1,0:T(8,128)(2,1)S(1)} custom-call(bf16[1024,256]{1,0:T(8,128)(2,1)S(1)} %bitcast.13, bf16[464,256]{1,0:T(8,128)(2,1)S(1)} %collective-permute-done.4.refs_5_.up, bf16[464,256]{1,0:T(8,128)(2,1)S(1)} %collective-permute-done.3.refs_3_.down, bf16[128,256]{1,0:T(8,128)(2,1)S(1)} %get-tuple-element.87.local, ...), custom_call_target="tpu_custom_call" | custom-call | flops 1811939328 | bytes 5242880 | tf_op jit(solution)/shard_map/pallas_call | solution.py:42
  108.1 0.8 collective-permute-done.17
  109.0 0.1 collective-permute-start.18
  109.1 3.9 %shard_map.91 = bf16[1024,256]{1,0:T(8,128)(2,1)} custom-call(bf16[1024,256]{1,0:T(8,128)(2,1)S(1)} %bitcast.14, bf16[464,256]{1,0:T(8,128)(2,1)S(1)} %collective-permute-done.4.refs_5_.up, bf16[464,256]{1,0:T(8,128)(2,1)S(1)} %collective-permute-done.3.refs_3_.down, bf16[128,256]{1,0:T(8,128)(2,1)S(1)} %get-tuple-element.87.local, ...), custom_call_target="tpu_custom_call" | custom-call | flops 1811939328 | bytes 5242880 | tf_op jit(solution)/shard_map/pallas_call | solution.py:42
  113.0 2.4 %collective-permute-done.18 = s16[512,256]{1,0:T(8,128)(2,1)S(1)} collective-permute-done((s16[512,256]{1,0:T(8,128)(2,1)S(1)}, s16[512,256]{1,0:T(8,128)(2,1)S(1)}, u32[]{:S(2)}, u32[]{:S(2)}) %collective-permute-start.18) | collective-permute-done | bytes 262176 | tf_op jit(solution)/shard_map/ppermute | solution.py:444
  115.5 1.6 %collective-permute-start.21 = (s16[512,256]{1,0:T(8,128)(2,1)S(1)}, s16[512,256]{1,0:T(8,128)(2,1)S(1)}, u32[]{:S(2)}, u32[]{:S(2)}) collective-permute-start(s16[512,256]{1,0:T(8,128)(2,1)S(1)} %pad_add_fusion.5), channel_id=1, source_target_pairs={{0,2},{1,3},{2,0},{3,1},{4,6},{5,7},{6,4},{7,5},{8,10},{9,11},{10,... | collective-permute-start | bytes 786440 | tf_op jit(solution)/shard_map/ppermute | solution.py:444
  117.1 2.4 %collective-permute-start.19 = (s16[512,256]{1,0:T(8,128)(2,1)S(1)}, s16[512,256]{1,0:T(8,128)(2,1)S(1)}, u32[]{:S(2)}, u32[]{:S(2)}) collective-permute-start(s16[512,256]{1,0:T(8,128)(2,1)S(1)} %pad_add_fusion.4), channel_id=1, source_target_pairs={{0,4},{4,0},{8,12},{12,8},{16,20},{20,16},{24,28},{28,24},{1,5},{5... | collective-permute-start | bytes 786440 | tf_op jit(solution)/shard_map/ppermute | solution.py:444
  119.5 4.2 %collective-permute-done.21 = s16[512,256]{1,0:T(8,128)(2,1)S(1)} collective-permute-done((s16[512,256]{1,0:T(8,128)(2,1)S(1)}, s16[512,256]{1,0:T(8,128)(2,1)S(1)}, u32[]{:S(2)}, u32[]{:S(2)}) %collective-permute-start.21) | collective-permute-done | bytes 262176 | tf_op jit(solution)/shard_map/ppermute | solution.py:444
  123.7 3.5 %collective-permute-start.22 = (s16[1024,256]{1,0:T(8,128)(2,1)S(1)}, s16[1024,256]{1,0:T(8,128)(2,1)S(1)}, u32[]{:S(2)}, u32[]{:S(2)}) collective-permute-start(s16[1024,256]{1,0:T(8,128)(2,1)S(1)} %pad_add_fusion.1.refs_2_), channel_id=1, source_target_pairs={{0,4},{4,0},{8,12},{12,8},{16,20},{20,16},{24,28},{28,24},{1,5},{5... | collective-permute-start | bytes 1572872 | tf_op jit(solution)/shard_map/ppermute | solution.py:444
  127.3 1.5 %collective-permute-start.20 = (s16[1024,256]{1,0:T(8,128)(2,1)S(1)}, s16[1024,256]{1,0:T(8,128)(2,1)S(1)}, u32[]{:S(2)}, u32[]{:S(2)}) collective-permute-start(s16[1024,256]{1,0:T(8,128)(2,1)S(1)} %pad_add_fusion.refs_0_), channel_id=1, source_target_pairs={{0,2},{1,3},{2,0},{3,1},{4,6},{5,7},{6,4},{7,5},{8,10},{9,11},{10,... | collective-permute-start | bytes 1572872 | tf_op jit(solution)/shard_map/ppermute | solution.py:444
  128.8 0.5 collective-permute-start.23
  129.3 5.1 %collective-permute-done.22.refs_3_ = s16[1024,256]{1,0:T(8,128)(2,1)S(1)} collective-permute-done((s16[1024,256]{1,0:T(8,128)(2,1)S(1)}, s16[1024,256]{1,0:T(8,128)(2,1)S(1)}, u32[]{:S(2)}, u32[]{:S(2)}) %collective-permute-start.22) | collective-permute-done | bytes 524320 | tf_op jit(solution)/shard_map/ppermute | solution.py:444
  134.4 2.1 %collective-permute-done.20.refs_1_ = s16[1024,256]{1,0:T(8,128)(2,1)S(1)} collective-permute-done((s16[1024,256]{1,0:T(8,128)(2,1)S(1)}, s16[1024,256]{1,0:T(8,128)(2,1)S(1)}, u32[]{:S(2)}, u32[]{:S(2)}) %collective-permute-start.20) | collective-permute-done | bytes 524320 | tf_op jit(solution)/shard_map/ppermute | solution.py:444
  136.5 1.9 %collective-permute-done.24.refs_5_ = s16[1024,256]{1,0:T(8,128)(2,1)S(1)} collective-permute-done((s16[1024,256]{1,0:T(8,128)(2,1)S(1)}, s16[1024,256]{1,0:T(8,128)(2,1)S(1)}, u32[]{:S(2)}, u32[]{:S(2)}) %collective-permute-start.24) | collective-permute-done | bytes 524320 | tf_op jit(solution)/shard_map/ppermute | solution.py:444
  138.4 6.3 %shard_map.92 = bf16[27,256,256]{2,1,0:T(8,128)(2,1)} custom-call(s32[5]{0:T(128)S(1)} %stack.23.bits_ref.refs_0_, s16[1024,256]{1,0:T(8,128)(2,1)S(1)} %pad_add_fusion.refs_0_, s16[1024,256]{1,0:T(8,128)(2,1)S(1)} %collective-permute-done.20.refs_1_, s16[1024,256]{1,0:T(8,128)(2,1)S(1)} %pad_add_fusion.1.refs_2_, ...), custom_call_target="tpu_custom_call" | custom-call | tf_op jit(solution)/shard_map/pallas_call | solution.py:42
  (28 shorter events, 0.3 us)
Async XLA Ops:
  0.6 1.0 copy-start
  1.7 1.0 copy-start.3
  2.7 0.7 copy-start.4
  3.4 0.7 copy-start.5
  4.1 42.1 %copy-start.1 = (bf16[1,1024,256]{2,1,0:T(8,128)(2,1)S(1)}, bf16[1,1024,256]{2,1,0:T(8,128)(2,1)}, u32[]{:S(2)}) copy-start(bf16[1,1024,256]{2,1,0:T(8,128)(2,1)} %param.9) | copy-start | bytes 1572868
  7.7 14.7 %collective-permute-start = (bf16[272,256]{1,0:T(8,128)(2,1)S(1)}, bf16[272,256]{1,0:T(8,128)(2,1)S(1)}, u32[]{:S(2)}, u32[]{:S(2)}) collective-permute-start(bf16[272,256]{1,0:T(8,128)(2,1)S(1)} %get-tuple-element.48), channel_id=1, source_target_pairs={{0,16},{4,20},{8,24},{12,28},{16,0},{20,4},{24,8},{28,12},{1,17},{... | collective-permute-start | bytes 417800 | tf_op jit(solution)/shard_map/ppermute | solution.py:489
  11.8 18.5 %collective-permute-start.1 = (bf16[272,256]{1,0:T(8,128)(2,1)S(1)}, bf16[272,256]{1,0:T(8,128)(2,1)S(1)}, u32[]{:S(2)}, u32[]{:S(2)}) collective-permute-start(bf16[272,256]{1,0:T(8,128)(2,1)S(1)} %get-tuple-element.49), channel_id=1, source_target_pairs={{0,20},{4,24},{8,28},{12,0},{16,4},{20,8},{24,12},{28,16},{1,21},{... | collective-permute-start | bytes 417800 | tf_op jit(solution)/shard_map/ppermute | solution.py:489
  13.0 24.6 %collective-permute-start.3 = (bf16[464,256]{1,0:T(8,128)(2,1)S(1)}, bf16[464,256]{1,0:T(8,128)(2,1)S(1)}, u32[]{:S(2)}, u32[]{:S(2)}) collective-permute-start(bf16[464,256]{1,0:T(8,128)(2,1)S(1)} %get-tuple-element.51), channel_id=1, source_target_pairs={{0,28},{4,0},{8,4},{12,8},{16,12},{20,16},{24,20},{28,24},{1,29},{... | collective-permute-start | bytes 712712 | tf_op jit(solution)/shard_map/ppermute | solution.py:489
  14.2 23.5 %collective-permute-start.4 = (bf16[464,256]{1,0:T(8,128)(2,1)S(1)}, bf16[464,256]{1,0:T(8,128)(2,1)S(1)}, u32[]{:S(2)}, u32[]{:S(2)}) collective-permute-start(bf16[464,256]{1,0:T(8,128)(2,1)S(1)} %get-tuple-element.53), channel_id=1, source_target_pairs={{0,4},{4,8},{8,12},{12,16},{16,20},{20,24},{24,28},{28,0},{1,5},{5... | collective-permute-start | bytes 712712 | tf_op jit(solution)/shard_map/ppermute | solution.py:489
  15.1 15.2 %collective-permute-start.2 = (bf16[272,256]{1,0:T(8,128)(2,1)S(1)}, bf16[272,256]{1,0:T(8,128)(2,1)S(1)}, u32[]{:S(2)}, u32[]{:S(2)}) collective-permute-start(bf16[272,256]{1,0:T(8,128)(2,1)S(1)} %get-tuple-element.50), channel_id=1, source_target_pairs={{0,24},{4,28},{8,0},{12,4},{16,8},{20,12},{24,16},{28,20},{1,25},{... | collective-permute-start | bytes 417800 | tf_op jit(solution)/shard_map/ppermute | solution.py:489
  22.3 15.3 %collective-permute-start.5 = (bf16[272,256]{1,0:T(8,128)(2,1)S(1)}, bf16[272,256]{1,0:T(8,128)(2,1)S(1)}, u32[]{:S(2)}, u32[]{:S(2)}) collective-permute-start(bf16[272,256]{1,0:T(8,128)(2,1)S(1)} %get-tuple-element.54), channel_id=1, source_target_pairs={{0,8},{4,12},{8,16},{12,20},{16,24},{20,28},{24,0},{28,4},{1,9},{5... | collective-permute-start | bytes 417800 | tf_op jit(solution)/shard_map/ppermute | solution.py:489
  30.3 7.4 %collective-permute-start.6 = (bf16[272,256]{1,0:T(8,128)(2,1)S(1)}, bf16[272,256]{1,0:T(8,128)(2,1)S(1)}, u32[]{:S(2)}, u32[]{:S(2)}) collective-permute-start(bf16[272,256]{1,0:T(8,128)(2,1)S(1)} %get-tuple-element.55), channel_id=1, source_target_pairs={{0,12},{4,16},{8,20},{12,24},{16,28},{20,0},{24,4},{28,8},{1,13},{... | collective-permute-start | bytes 417800 | tf_op jit(solution)/shard_map/ppermute | solution.py:489
  39.2 7.8 %collective-permute-start.7 = (bf16[192,256]{1,0:T(8,128)(2,1)S(1)}, bf16[192,256]{1,0:T(8,128)(2,1)S(1)}, u32[]{:S(2)}, u32[]{:S(2)}) collective-permute-start(bf16[192,256]{1,0:T(8,128)(2,1)S(1)} %get-tuple-element.58), channel_id=1, source_target_pairs={{0,4},{4,8},{8,12},{12,16},{16,20},{20,24},{24,28},{1,5},{5,9},{9,... | collective-permute-start | bytes 294920 | tf_op jit(solution)/shard_map/ppermute | solution.py:449
  44.7 6.5 %collective-permute-start.8 = (bf16[192,256]{1,0:T(8,128)(2,1)S(1)}, bf16[192,256]{1,0:T(8,128)(2,1)S(1)}, u32[]{:S(2)}, u32[]{:S(2)}) collective-permute-start(bf16[192,256]{1,0:T(8,128)(2,1)S(1)} %get-tuple-element.59), channel_id=1, source_target_pairs={{4,0},{8,4},{12,8},{16,12},{20,16},{24,20},{28,24},{5,1},{9,5},{13... | collective-permute-start | bytes 294920 | tf_op jit(solution)/shard_map/ppermute | solution.py:449
  56.2 2.5 %collective-permute-start.9 = (s16[1808,256]{1,0:T(8,128)(2,1)S(1)}, s16[1808,256]{1,0:T(8,128)(2,1)S(1)}, u32[]{:S(2)}, u32[]{:S(2)}) collective-permute-start(s16[1808,256]{1,0:T(8,128)(2,1)S(1)} %shard_map.80), channel_id=1, source_target_pairs={{0,1},{1,0},{2,3},{3,2},{4,5},{5,4},{6,7},{7,6},{8,9},{9,8},{10,11... | collective-permute-start | bytes 2777096 | tf_op jit(solution)/shard_map/ppermute | solution.py:444
  56.3 6.8 %collective-permute-start.10 = (s16[1808,256]{1,0:T(8,128)(2,1)S(1)}, s16[1808,256]{1,0:T(8,128)(2,1)S(1)}, u32[]{:S(2)}, u32[]{:S(2)}) collective-permute-start(s16[1808,256]{1,0:T(8,128)(2,1)S(1)} %get-tuple-element.66), channel_id=1, source_target_pairs={{0,1},{1,0},{2,3},{3,2},{4,5},{5,4},{6,7},{7,6},{8,9},{9,8},{10,11... | collective-permute-start | bytes 2777096 | tf_op jit(solution)/shard_map/ppermute | solution.py:444
  60.6 13.4 %collective-permute-start.12 = (s16[912,256]{1,0:T(8,128)(2,1)S(1)}, s16[912,256]{1,0:T(8,128)(2,1)S(1)}, u32[]{:S(2)}, u32[]{:S(2)}) collective-permute-start(s16[912,256]{1,0:T(8,128)(2,1)S(1)} %get-tuple-element.68), channel_id=1, source_target_pairs={{0,4},{4,0},{8,12},{12,8},{16,20},{20,16},{24,28},{28,24},{1,5},{5... | collective-permute-start | bytes 1400840 | tf_op jit(solution)/shard_map/ppermute | solution.py:444
  65.0 12.5 %collective-permute-start.11 = (s16[912,256]{1,0:T(8,128)(2,1)S(1)}, s16[912,256]{1,0:T(8,128)(2,1)S(1)}, u32[]{:S(2)}, u32[]{:S(2)}) collective-permute-start(s16[912,256]{1,0:T(8,128)(2,1)S(1)} %get-tuple-element.67), channel_id=1, source_target_pairs={{0,2},{1,3},{2,0},{3,1},{4,6},{5,7},{6,4},{7,5},{8,10},{9,11},{10,... | collective-permute-start | bytes 1400840 | tf_op jit(solution)/shard_map/ppermute | solution.py:444
  73.1 32.1 %copy-start.2 = (bf16[27,256,256]{2,1,0:T(8,128)(2,1)S(1)}, bf16[27,256,256]{2,1,0:T(8,128)(2,1)}, u32[]{:S(2)}) copy-start(bf16[27,256,256]{2,1,0:T(8,128)(2,1)} %weight_ref.5) | copy-start | bytes 10616836
  78.3 6.8 %collective-permute-start.13 = (s16[464,256]{1,0:T(8,128)(2,1)S(1)}, s16[464,256]{1,0:T(8,128)(2,1)S(1)}, u32[]{:S(2)}, u32[]{:S(2)}) collective-permute-start(s16[464,256]{1,0:T(8,128)(2,1)S(1)} %get-tuple-element.73), channel_id=1, source_target_pairs={{0,4},{4,0},{8,12},{12,8},{16,20},{20,16},{24,28},{28,24},{1,5},{5... | collective-permute-start | bytes 712712 | tf_op jit(solution)/shard_map/ppermute | solution.py:444
  79.5 6.8 %collective-permute-start.14 = (s16[464,256]{1,0:T(8,128)(2,1)S(1)}, s16[464,256]{1,0:T(8,128)(2,1)S(1)}, u32[]{:S(2)}, u32[]{:S(2)}) collective-permute-start(s16[464,256]{1,0:T(8,128)(2,1)S(1)} %get-tuple-element.77), channel_id=1, source_target_pairs={{0,2},{1,3},{2,0},{3,1},{4,6},{5,7},{6,4},{7,5},{8,10},{9,11},{10,... | collective-permute-start | bytes 712712 | tf_op jit(solution)/shard_map/ppermute | solution.py:444
  87.1 6.2 %collective-permute-start.15 = (s16[464,256]{1,0:T(8,128)(2,1)S(1)}, s16[464,256]{1,0:T(8,128)(2,1)S(1)}, u32[]{:S(2)}, u32[]{:S(2)}) collective-permute-start(s16[464,256]{1,0:T(8,128)(2,1)S(1)} %get-tuple-element.79), channel_id=1, source_target_pairs={{0,8},{4,12},{8,0},{12,4},{16,24},{20,28},{24,16},{28,20},{1,9},{5... | collective-permute-start | bytes 712712 | tf_op jit(solution)/shard_map/ppermute | solution.py:444
  94.0 8.5 %collective-permute-start.16 = (s16[240,256]{1,0:T(8,128)(2,1)S(1)}, s16[240,256]{1,0:T(8,128)(2,1)S(1)}, u32[]{:S(2)}, u32[]{:S(2)}) collective-permute-start(s16[240,256]{1,0:T(8,128)(2,1)S(1)} %get-tuple-element.81), channel_id=1, source_target_pairs={{0,16},{4,20},{8,24},{12,28},{16,0},{20,4},{24,8},{28,12},{1,17},{... | collective-permute-start | bytes 368648 | tf_op jit(solution)/shard_map/ppermute | solution.py:444
  102.8 6.2 %collective-permute-start.17 = (s16[256,256]{1,0:T(8,128)(2,1)S(1)}, s16[256,256]{1,0:T(8,128)(2,1)S(1)}, u32[]{:S(2)}, u32[]{:S(2)}) collective-permute-start(s16[256,256]{1,0:T(8,128)(2,1)S(1)} %pad_add_fusion.6), channel_id=1, source_target_pairs={{0,16},{4,20},{8,24},{12,28},{16,0},{20,4},{24,8},{28,12},{1,17},{... | collective-permute-start | bytes 393224 | tf_op jit(solution)/shard_map/ppermute | solution.py:444
  109.0 6.4 %collective-permute-start.18 = (s16[512,256]{1,0:T(8,128)(2,1)S(1)}, s16[512,256]{1,0:T(8,128)(2,1)S(1)}, u32[]{:S(2)}, u32[]{:S(2)}) collective-permute-start(s16[512,256]{1,0:T(8,128)(2,1)S(1)} %pad_add_fusion.2), channel_id=1, source_target_pairs={{0,8},{4,12},{8,0},{12,4},{16,24},{20,28},{24,16},{28,20},{1,9},{5... | collective-permute-start | bytes 786440 | tf_op jit(solution)/shard_map/ppermute | solution.py:444
  115.5 8.2 %collective-permute-start.21 = (s16[512,256]{1,0:T(8,128)(2,1)S(1)}, s16[512,256]{1,0:T(8,128)(2,1)S(1)}, u32[]{:S(2)}, u32[]{:S(2)}) collective-permute-start(s16[512,256]{1,0:T(8,128)(2,1)S(1)} %pad_add_fusion.5), channel_id=1, source_target_pairs={{0,2},{1,3},{2,0},{3,1},{4,6},{5,7},{6,4},{7,5},{8,10},{9,11},{10,... | collective-permute-start | bytes 786440 | tf_op jit(solution)/shard_map/ppermute | solution.py:444
  117.1 10.2 %collective-permute-start.19 = (s16[512,256]{1,0:T(8,128)(2,1)S(1)}, s16[512,256]{1,0:T(8,128)(2,1)S(1)}, u32[]{:S(2)}, u32[]{:S(2)}) collective-permute-start(s16[512,256]{1,0:T(8,128)(2,1)S(1)} %pad_add_fusion.4), channel_id=1, source_target_pairs={{0,4},{4,0},{8,12},{12,8},{16,20},{20,16},{24,28},{28,24},{1,5},{5... | collective-permute-start | bytes 786440 | tf_op jit(solution)/shard_map/ppermute | solution.py:444
  123.7 10.7 %collective-permute-start.22 = (s16[1024,256]{1,0:T(8,128)(2,1)S(1)}, s16[1024,256]{1,0:T(8,128)(2,1)S(1)}, u32[]{:S(2)}, u32[]{:S(2)}) collective-permute-start(s16[1024,256]{1,0:T(8,128)(2,1)S(1)} %pad_add_fusion.1.refs_2_), channel_id=1, source_target_pairs={{0,4},{4,0},{8,12},{12,8},{16,20},{20,16},{24,28},{28,24},{1,5},{5... | collective-permute-start | bytes 1572872 | tf_op jit(solution)/shard_map/ppermute | solution.py:444
  127.3 9.2 %collective-permute-start.20 = (s16[1024,256]{1,0:T(8,128)(2,1)S(1)}, s16[1024,256]{1,0:T(8,128)(2,1)S(1)}, u32[]{:S(2)}, u32[]{:S(2)}) collective-permute-start(s16[1024,256]{1,0:T(8,128)(2,1)S(1)} %pad_add_fusion.refs_0_), channel_id=1, source_target_pairs={{0,2},{1,3},{2,0},{3,1},{4,6},{5,7},{6,4},{7,5},{8,10},{9,11},{10,... | collective-permute-start | bytes 1572872 | tf_op jit(solution)/shard_map/ppermute | solution.py:444
  128.8 7.7 %collective-permute-start.25 = (s16[1024,256]{1,0:T(8,128)(2,1)S(1)}, s16[1024,256]{1,0:T(8,128)(2,1)S(1)}, u32[]{:S(2)}, u32[]{:S(2)}) collective-permute-start(s16[1024,256]{1,0:T(8,128)(2,1)S(1)} %pad_add_fusion.1.refs_2_), channel_id=1, source_target_pairs={{0,1},{1,0},{2,3},{3,2},{4,5},{5,4},{6,7},{7,6},{8,9},{9,8},{10,11... | collective-permute-start | bytes 1572872 | tf_op jit(solution)/shard_map/ppermute | solution.py:444
  128.8 7.7 %collective-permute-start.23 = (s16[1024,256]{1,0:T(8,128)(2,1)S(1)}, s16[1024,256]{1,0:T(8,128)(2,1)S(1)}, u32[]{:S(2)}, u32[]{:S(2)}) collective-permute-start(s16[1024,256]{1,0:T(8,128)(2,1)S(1)} %pad_add_fusion.refs_0_), channel_id=1, source_target_pairs={{0,1},{1,0},{2,3},{3,2},{4,5},{5,4},{6,7},{7,6},{8,9},{9,8},{10,11... | collective-permute-start | bytes 1572872 | tf_op jit(solution)/shard_map/ppermute | solution.py:444
  134.4 2.1 %collective-permute-start.26 = (s16[1024,256]{1,0:T(8,128)(2,1)S(1)}, s16[1024,256]{1,0:T(8,128)(2,1)S(1)}, u32[]{:S(2)}, u32[]{:S(2)}) collective-permute-start(s16[1024,256]{1,0:T(8,128)(2,1)S(1)} %collective-permute-done.22.refs_3_), channel_id=1, source_target_pairs={{0,1},{1,0},{2,3},{3,2},{4,5},{5,4},{6,7},{7,6},{8,9},{9,8},{10,11... | collective-permute-start | bytes 1572872 | tf_op jit(solution)/shard_map/ppermute | solution.py:444
  136.5 1.9 %collective-permute-start.24 = (s16[1024,256]{1,0:T(8,128)(2,1)S(1)}, s16[1024,256]{1,0:T(8,128)(2,1)S(1)}, u32[]{:S(2)}, u32[]{:S(2)}) collective-permute-start(s16[1024,256]{1,0:T(8,128)(2,1)S(1)} %collective-permute-done.20.refs_1_), channel_id=1, source_target_pairs={{0,1},{1,0},{2,3},{3,2},{4,5},{5,4},{6,7},{7,6},{8,9},{9,8},{10,11... | collective-permute-start | bytes 1572872 | tf_op jit(solution)/shard_map/ppermute | solution.py:444

commit v2 on v1

--- a/solution.py
+++ b/solution.py
@@ -33,9 +33,11 @@
     return jnp.where(index == key, 1.0, 0.0).astype(BF)
 
 
-def call(body, outs, args, smem=(), scratch=(), vmem=48, flops=0, moved=0):
+def call(body, outs, args, smem=(), scratch=(), vmem=48, flops=0, moved=0, far=(), far_out=False):
     specs = [
-        pl.BlockSpec(memory_space=pltpu.SMEM if i in smem else pltpu.VMEM)
+        pl.BlockSpec(
+            memory_space=pltpu.HBM if i in far else pltpu.SMEM if i in smem else pltpu.VMEM
+        )
         for i in range(len(args))
     ]
     shapes = [jax.ShapeDtypeStruct(s, d) for s, d in outs]
@@ -43,7 +45,9 @@
         body,
         out_shape=shapes,
         in_specs=specs,
-        out_specs=[pl.BlockSpec(memory_space=pltpu.VMEM) for _ in shapes],
+        out_specs=[
+            pl.BlockSpec(memory_space=pltpu.HBM if far_out else pltpu.VMEM) for _ in shapes
+        ],
         scratch_shapes=list(scratch),
         compiler_params=pltpu.CompilerParams(vmem_limit_bytes=vmem * MIB),
         cost_estimate=pl.CostEstimate(flops=flops, bytes_accessed=moved, transcendentals=0),
@@ -93,14 +97,26 @@
     return sends, cells
 
 
-def pack_body(me_ref, near_ref, pos_ref, x_ref, dy_ref, *refs, count, window, cap):
-    *out_refs, skey_ref, ekey_ref, local_ref = refs
+def pack_body(me_ref, *refs, count, window, cap):
+    sources, refs = refs[:4], refs[4:]
+    *out_refs, skey_ref, ekey_ref, local_ref = refs[: window + 3]
+    *landed, sem = refs[window + 3 :]
+    copies = [
+        pltpu.make_async_copy(source, to, sem.at[n])
+        for n, (source, to) in enumerate(zip(sources, landed, strict=True))
+    ]
+    for copy in copies:
+        copy.start()
+    near_ref, pos_ref, dy_ref, x_ref = landed
     rows = x_ref.shape[0]
+    copies[0].wait()
     for g in range(2):
         sends, cells = key_rows(near_ref, me_ref[0] * 2 + g, g)
         for n in range(4):
             skey_ref[g * 4 + n : g * 4 + n + 1, :] = sends[n]
         ekey_ref[g : g + 1, :] = cells
+    copies[1].wait()
+    copies[2].wait()
     base = cap + TAIL
     faces_of(
         lambda g: dy_ref[g * 512 : g * 512 + 512, :],
@@ -124,6 +140,7 @@
     line = lax.broadcasted_iota(I32, (TAIL, rows), 0)
     digits = jnp.where(line == 0, (local >> 5) + 1, jnp.where(line == 1, local & 31, 0))
     digits = digits.astype(F32).astype(BF)
+    copies[3].wait()
     x = x_ref[...]
     slot = lax.broadcasted_iota(I32, (cap, rows), 0)
     for c in range(window):
@@ -243,8 +260,10 @@
         out_ref[g * 512 : g * 512 + 512, :] = acc_ref[at * 512 : at * 512 + 512, :].astype(BF)
 
 
-def turn_body(x_ref, out_ref):
+def turn_body(x_ref, chunk_ref, skey_ref, out_ref, near_chunk_ref, near_skey_ref):
     out_ref[...] = x_ref[...].astype(F32).T.astype(BF)
+    near_chunk_ref[...] = chunk_ref[...]
+    near_skey_ref[...] = skey_ref[...]
 
 
 def backward_first_body(x, up, down, local, ekey, weight_ref, out_ref, grid_ref, acc_ref, *, base):
@@ -393,15 +412,20 @@
 
 
 def finish_body(bits_ref, *refs):
-    out_ref, wide_ref, square_ref = refs[8:]
+    out_ref, stage_ref, wide_ref, square_ref, sem = refs[8:]
     mine = bits_ref[0]
     halves = (mine, 1 - mine)
 
-    def place_of(p, u):
-        place = 0
-        for n, which in enumerate(((1, 2, 3, 4), (2, 1, 3, 4))[p]):
-            place = place * 2 + (bits_ref[which] ^ ((u >> (3 - n)) & 1))
-        return place
+    def place_of(side, p, u):
+        x = bits_ref[1] ^ ((u >> (3 - p)) & 1)
+        y = bits_ref[2] ^ ((u >> (2 + p)) & 1)
+        low = (bits_ref[3] ^ ((u >> 1) & 1)) * 2 + (bits_ref[4] ^ (u & 1))
+        return jnp.where(halves[side] > 0, y * 8 + x * 4, x * 8 + y * 4) + low
+
+    def leave(side, i):
+        offset = halves[side] * HALF + i
+        n = side * HALF + i
+        return offset, pltpu.make_async_copy(stage_ref.at[n], out_ref.at[offset], sem.at[n])
 
     def ref_of(side, p, u):
         return refs[side * 4 + p * 2 + u // 8], (u % 8) * UNIT
@@ -411,7 +435,7 @@
             for u in range(16):
                 ref, at = ref_of(side, p, u)
                 tail = tail_codes(ref, at + PART * 16)
-                square_ref[pl.ds(halves[side] * 32 + p * 16 + place_of(p, u), 1), :] = (
+                square_ref[pl.ds(halves[side] * 32 + p * 16 + place_of(side, p, u), 1), :] = (
                     jnp.exp2(tail[PART : PART + 1]) * tail[PART + 1 : PART + 2]
                 )
     squares = jnp.sum(square_ref[...], axis=0, keepdims=True)
@@ -422,7 +446,7 @@
             places, scales = [], []
             for u in range(16):
                 ref, at = ref_of(side, p, u)
-                places.append(pl.multiple_of(place_of(p, u) * 16, 16))
+                places.append(pl.multiple_of(place_of(side, p, u) * 16, 16))
                 scales.append(scale_of(tail_codes(ref, at + PART * 16)[:8]) * gain * (1.0 / TOP))
             for i in range(PART):
                 for u in range(16):
@@ -431,17 +455,30 @@
                     wide_ref[i % 2, pl.ds(places[u], 16), :] = (
                         coded.astype(I32).astype(F32) * scales[u][i : i + 1]
                     ).astype(BF)
-                offset = halves[side] * HALF + p * PART + i
-
-                @pl.when(offset < 27)
-                def _():
-                    out_ref[offset] = wide_ref[i % 2].T
+                stage_ref[side * HALF + p * PART + i] = wide_ref[i % 2].T
+                offset, copy = leave(side, p * PART + i)
+                pl.when(offset < 27)(copy.start)
+    for side in range(2):
+        for i in range(HALF):
+            offset, copy = leave(side, i)
+            pl.when(offset < 27)(copy.wait)
 
 
 def swap(x, bit):
     axis, place = bit
     count = lax.axis_size(axis)
     return lax.ppermute(x, axis, [(i, i ^ (1 << place)) for i in range(count)])
+
+
+def swap_either(x, parity, bits):
+    count, width = lax.axis_size("pts"), lax.axis_size("dp")
+    turn = []
+    for i in range(count * width):
+        place = {"pts": i // width, "dp": i % width}
+        axis, at = bits[(place[parity[0]] >> parity[1]) & 1]
+        place[axis] ^= 1 << at
+        turn.append((i, place["pts"] * width + place["dp"]))
+    return lax.ppermute(x, ("pts", "dp"), turn)
 
 
 def shift(x, step):
@@ -469,16 +506,28 @@
     window = min(16, count)
     cap = 2 * rows // window
     split, extra = device_bits()
-    bits = jnp.stack([bit_value(b) for b in split]).astype(I32)
     s0, s1, s2, s3, s4 = split
+    odd = bit_value(s0) > 0
+    first = jnp.where(odd, bit_value(s2), bit_value(s1))
+    second = jnp.where(odd, bit_value(s1), bit_value(s2))
+    bits = jnp.stack([*(bit_value(b) for b in split), first, second]).astype(I32)
 
     dy = grad_out[0]
     lines = [cap + TAIL + (192 if abs(w - window // 2) == 1 else 0) for w in range(window)]
     *packed, skey, ekey, dy_local = call(
         functools.partial(pack_body, count=count, window=window, cap=cap),
         [*(((n, C), BF) for n in lines), ((8, 512), I32), ((2, C), I32), ((128, C), BF)],
-        [me.reshape(1), neighbours[0], hilbert_pos, features[0], dy],
-        smem=(0, 1),
+        [me.reshape(1), neighbours[0], hilbert_pos, dy, features[0]],
+        smem=(0,),
+        far=(1, 2, 3, 4),
+        vmem=60,
+        scratch=[
+            pltpu.SMEM(neighbours.shape[1:], I32),
+            pltpu.VMEM(hilbert_pos.shape, I32),
+            pltpu.VMEM((rows, C), BF),
+            pltpu.VMEM((rows, C), BF),
+            pltpu.SemaphoreType.DMA((4,)),
+        ],
         flops=4 * rows * rows * C,
         moved=4 * rows * C * 2,
     )
@@ -489,8 +538,13 @@
         got[w] = packed[w] if step == 0 else lax.ppermute(packed[w], "pts", turn)
 
     conv_flops = 2 * 27 * rows * C * C
-    part_flops = conv_flops // 4
-    (turned,) = call(turn_body, [((C, rows), BF)], [dy])
+    part_flops = conv_flops
+    stayed = window // 2
+    turned, got[stayed], skey = call(
+        turn_body,
+        [((C, rows), BF), ((cap + TAIL, C), BF), ((8, 512), I32)],
+        [dy, packed[stayed], skey],
+    )
 
     x, up, down, x_local = call(
         functools.partial(order_body, cap=cap),
@@ -520,23 +574,23 @@
     came_b = swap(send_b, s0)
     own_outs = [((PART, 128, C), F32), ((PART * 128 + TAIL, C), I16)]
     keep_a, send_a = call(
-        functools.partial(own_terms_body, first=0, which=1),
+        functools.partial(own_terms_body, first=0, which=5),
         own_outs,
         [bits, grid, turned, came_a],
         smem=(0,),
         flops=part_flops,
         moved=5 * MIB,
     )
-    came_a = swap(send_a, s1)
+    came_a = swap_either(send_a, s0, (s1, s2))
     keep_b, send_b = call(
-        functools.partial(own_terms_body, first=PART, which=2),
+        functools.partial(own_terms_body, first=PART, which=5),
         own_outs,
         [bits, grid, turned, came_b],
         smem=(0,),
         flops=part_flops,
         moved=5 * MIB,
     )
-    came_b = swap(send_b, s2)
+    came_b = swap_either(send_b, s0, (s1, s2))
     x, grid, keep_b = lax.optimization_barrier((x, grid, keep_b))
     (forward,) = call(
         forward_body,
@@ -548,12 +602,11 @@
     )
     forward, came_a, came_b = lax.optimization_barrier((forward, came_a, came_b))
 
-    keep_a, send_a = reduce_step(bits, 2, [keep_a, came_a], ((0, PART, PART),), 128)
-    keep_b, send_b = reduce_step(bits, 1, [keep_b, came_b], ((0, PART, PART),), 128)
-    came_a, came_b = swap(send_a, s2), swap(send_b, s1)
     keep, send = reduce_step(
-        bits, 3, [keep_a, came_a, keep_b, came_b], ((0, PART, PART), (0, PART, PART)), 64
-    )
+        bits, 6, [keep_a, came_a, keep_b, came_b], ((0, PART, PART), (0, PART, PART)), 128
+    )
+    came = swap_either(send, s0, (s2, s1))
+    keep, send = reduce_step(bits, 3, [keep, came], ((0, HALF, HALF),), 64)
     came = swap(send, s3)
     keep, send = reduce_step(bits, 4, [keep, came], ((0, HALF, HALF),), 32)
     came = swap(send, s4)
@@ -600,7 +653,13 @@
         [((27, C, C), BF)],
         [bits, unit_a, far_a, unit_b, far_b, other_a, other_far_a, other_b, other_far_b],
         smem=(0,),
-        scratch=[pltpu.VMEM((2, C, C), BF), pltpu.VMEM((64, C), F32)],
+        scratch=[
+            pltpu.VMEM((2 * HALF, C, C), BF),
+            pltpu.VMEM((2, C, C), BF),
+            pltpu.VMEM((64, C), F32),
+            pltpu.SemaphoreType.DMA((2 * HALF,)),
+        ],
+        far_out=True,
     )
     return forward[None], backward[None], weight_grad
 

time: 145 us -> 139 us (0.959)
  starting transfers between devices: 48.4 us -> 37 us
  waiting for transfers between devices: 54.6 us -> 63.5 us
  local copies, waits for them, and re-layouts: 3.56 us -> 1.75 us
  Pallas kernels: 37.1 us -> 35.3 us
    ppermute x18 -> x14, starting transfers between devices: 22.3 us -> 6.28 us  [swap(): return lax.ppermute(x, axis, [(i, i ^ 1 << place) for i in range(count)])]
    ppermute x0 -> x3, waiting for transfers between devices: none -> 9.51 us  [swap_either(): return lax.ppermute(x, ('pts', 'dp'), turn)]
    ppermute x0 -> x3, starting transfers between devices: none -> 4.59 us  [swap_either(): return lax.ppermute(x, ('pts', 'dp'), turn)]
    unnamed x12, local copies, waits for them, and re-layouts: 3.45 us -> 1.63 us
    pallas_call x17 -> x16, Pallas kernels: 37.1 us -> 35.3 us  [call(): pl.pallas_call(body, out_shape=shapes, in_specs=specs, out_specs=[pl.Bloc...]
    ppermute x7, waiting for transfers between devices: 11 us -> 9.48 us  [on_device(): got[w] = packed[w] if step == 0 else lax.ppermute(packed[w], 'pts', turn)]
    ppermute x18 -> x14, waiting for transfers between devices: 38.9 us -> 39.5 us  [swap(): return lax.ppermute(x, axis, [(i, i ^ 1 << place) for i in range(count)])]
  transfers between devices with their start and end apart: 27 -> 26, of which waited for: 17 -> 17; matrix products, arithmetic and copies ran while one was open for 0% -> 0% of each run, Pallas kernels for 13% -> 13%
where the time goes in v2:
time: 139 us
  waiting for transfers between devices  63.5 us (46%)
  starting transfers between devices  37 us (27%)
  Pallas kernels  35.3 us (25%)
  local copies, waits for them, and re-layouts  1.75 us (1%)
    ppermute x14, waiting for transfers between devices, swap(): return lax.ppermute(x, axis, [(i, i ^ 1 << place) for i in range(count)])  39.5 us
    pallas_call x16, Pallas kernels, call(): pl.pallas_call(body, out_shape=shapes, in_specs=specs, out_specs=[pl.Bloc...  35.3 us
    ppermute x7, starting transfers between devices, on_device(): got[w] = packed[w] if step == 0 else lax.ppermute(packed[w], 'pts', turn)  19.1 us
    ppermute x3, waiting for transfers between devices, swap_either(): return lax.ppermute(x, ('pts', 'dp'), turn)  9.51 us
    ppermute x7, waiting for transfers between devices, on_device(): got[w] = packed[w] if step == 0 else lax.ppermute(packed[w], 'pts', turn)  9.48 us
    ppermute x2, starting transfers between devices, shift(): lax.ppermute(x, 'pts', [(i, i + step) for i in range(count) if 0 <= i + s...  7.04 us
    ppermute x14, starting transfers between devices, swap(): return lax.ppermute(x, axis, [(i, i ^ 1 << place) for i in range(count)])  6.28 us
    ppermute x2, waiting for transfers between devices, shift(): lax.ppermute(x, 'pts', [(i, i + step) for i in range(count) if 0 <= i + s...  4.93 us
  transfers between devices with their start and end apart: 26, of which 17 were waited for; matrix products, arithmetic and copies ran while one was open for 0% of the time, Pallas kernels for 13%

profile of v2, /device:TPU:0, one launch (start us, length us, event | category | flops | bytes accessed | tf_op | source)
XLA Modules:
  0.0 138.8 jit_solution(8403771933716905194)
XLA Ops:
  0.6 5.0 %shard_map.76 = (bf16[272,256]{1,0:T(8,128)(2,1)}, bf16[272,256]{1,0:T(8,128)(2,1)}, bf16[272,256]{1,0:T(8,128)(2,1)}, bf16[464,256]{1,0:T(8,128)(2,1)}, bf16[27...) custom-call(s32[1]{0:T(128)} %bitcast.me_ref, ...), custom_call_target="tpu_custom_call" | custom-call | flops 1073741824 | bytes 2097152 | tf_op jit(solution)/shard_map/pallas_call | solution.py:44
  5.6 4.1 %collective-permute-start = (bf16[272,256]{1,0:T(8,128)(2,1)}, bf16[272,256]{1,0:T(8,128)(2,1)S(1)}, u32[]{:S(2)}, u32[]{:S(2)}) collective-permute-start(bf16[272,256]{1,0:T(8,128)(2,1)} %get-tuple-element.49), channel_id=1, source_target_pairs={{0,16},{4,20},{8,24},{12,28},{16,0},{20,4},{24,8},{28,12},{1,17},{... | collective-permute-start | bytes 417800 | tf_op jit(solution)/shard_map/ppermute | solution.py:538
  9.7 1.3 collective-permute-start.1
  11.0 1.1 collective-permute-start.3
  12.2 0.9 collective-permute-start.4
  13.1 3.6 %collective-permute-start.2 = (bf16[272,256]{1,0:T(8,128)(2,1)}, bf16[272,256]{1,0:T(8,128)(2,1)S(1)}, u32[]{:S(2)}, u32[]{:S(2)}) collective-permute-start(bf16[272,256]{1,0:T(8,128)(2,1)} %get-tuple-element.51), channel_id=1, source_target_pairs={{0,24},{4,28},{8,0},{12,4},{16,8},{20,12},{24,16},{28,20},{1,25},{... | collective-permute-start | bytes 417800 | tf_op jit(solution)/shard_map/ppermute | solution.py:538
  16.7 3.9 %collective-permute-done.refs_0_ = bf16[272,256]{1,0:T(8,128)(2,1)S(1)} collective-permute-done((bf16[272,256]{1,0:T(8,128)(2,1)}, bf16[272,256]{1,0:T(8,128)(2,1)S(1)}, u32[]{:S(2)}, u32[]{:S(2)}) %collective-permute-start) | collective-permute-done | bytes 139296 | tf_op jit(solution)/shard_map/ppermute | solution.py:538
  20.5 8.1 %collective-permute-start.5 = (bf16[272,256]{1,0:T(8,128)(2,1)}, bf16[272,256]{1,0:T(8,128)(2,1)S(1)}, u32[]{:S(2)}, u32[]{:S(2)}) collective-permute-start(bf16[272,256]{1,0:T(8,128)(2,1)} %get-tuple-element.57), channel_id=1, source_target_pairs={{0,8},{4,12},{8,16},{12,20},{16,24},{20,28},{24,0},{28,4},{1,9},{5... | collective-permute-start | bytes 417800 | tf_op jit(solution)/shard_map/ppermute | solution.py:538
  28.6 0.0 collective-permute-done.1.refs_1_
  28.6 0.0 collective-permute-start.6
  28.6 0.9 copy-done.1
  29.5 0.7 copy-done.2
  30.2 0.2 shard_map.77
  30.4 0.0 collective-permute-done.2.refs_2_
  30.4 5.6 %collective-permute-done.5.refs_6_ = bf16[272,256]{1,0:T(8,128)(2,1)S(1)} collective-permute-done((bf16[272,256]{1,0:T(8,128)(2,1)}, bf16[272,256]{1,0:T(8,128)(2,1)S(1)}, u32[]{:S(2)}, u32[]{:S(2)}) %collective-permute-start.5) | collective-permute-done | bytes 139296 | tf_op jit(solution)/shard_map/ppermute | solution.py:538
  36.1 1.5 %shard_map.78 = (bf16[1024,256]{1,0:T(8,128)(2,1)S(1)}, bf16[192,256]{1,0:T(8,128)(2,1)S(1)}, bf16[192,256]{1,0:T(8,128)(2,1)S(1)}, bf16[128,256]{1,0:T(8,128)(2,1)S(1)}) custom-call(bf16[272,256]{1,0:T(8,128)(2,1)S(1)} %collective-permute-done.refs_0_, bf16[272,256]{1,0:T(8,128)(2,1)S(1)} %collective-permute-done.1.refs_1_, ...), custom_call_target="tpu_custom_call" | custom-call | flops 1073741824 | bytes 2097152 | tf_op jit(solution)/shard_map/pallas_call | solution.py:44
  37.6 5.6 %collective-permute-start.7 = (bf16[192,256]{1,0:T(8,128)(2,1)S(1)}, bf16[192,256]{1,0:T(8,128)(2,1)S(1)}, u32[]{:S(2)}, u32[]{:S(2)}) collective-permute-start(bf16[192,256]{1,0:T(8,128)(2,1)S(1)} %get-tuple-element.61), channel_id=1, source_target_pairs={{0,4},{4,8},{8,12},{12,16},{16,20},{20,24},{24,28},{1,5},{5,9},{9,... | collective-permute-start | bytes 294920 | tf_op jit(solution)/shard_map/ppermute | solution.py:486
  43.1 1.5 %collective-permute-start.8 = (bf16[192,256]{1,0:T(8,128)(2,1)S(1)}, bf16[192,256]{1,0:T(8,128)(2,1)S(1)}, u32[]{:S(2)}, u32[]{:S(2)}) collective-permute-start(bf16[192,256]{1,0:T(8,128)(2,1)S(1)} %get-tuple-element.62), channel_id=1, source_target_pairs={{4,0},{8,4},{12,8},{16,12},{20,16},{24,20},{28,24},{5,1},{9,5},{13... | collective-permute-start | bytes 294920 | tf_op jit(solution)/shard_map/ppermute | solution.py:486
  44.6 0.1 stack.31.bits_ref.refs_0_
  44.7 0.6 collective-permute-done.7.up
  45.3 4.3 %collective-permute-done.8.down = bf16[192,256]{1,0:T(8,128)(2,1)S(1)} collective-permute-done((bf16[192,256]{1,0:T(8,128)(2,1)S(1)}, bf16[192,256]{1,0:T(8,128)(2,1)S(1)}, u32[]{:S(2)}, u32[]{:S(2)}) %collective-permute-start.8) | collective-permute-done | bytes 98336 | tf_op jit(solution)/shard_map/ppermute | solution.py:486
  49.6 3.0 %shard_map.79 = (bf16[2,3,800,256]{3,2,1,0:T(8,128)(2,1)S(1)}, s16[1808,256]{1,0:T(8,128)(2,1)S(1)}) custom-call(s32[7]{0:T(128)S(1)} %stack.31.bits_ref.refs_0_, bf16[1024,256]{1,0:T(8,128)(2,1)S(1)} %get-tuple-element.68.x.x_ref, bf16[192,256]{1,0:T(8,128)(2,1)S(1)} %collective-permute-done.7.up, bf16[192,256]{1,0:T(8,128)(2,1)S(1)} %collective-permute-done.8.down, ...), custom_call_target="tpu_custom_call" | custom-call | flops 3623878656 | bytes 5242880 | tf_op jit(solution)/shard_map/pallas_call | solution.py:44
  52.7 1.9 %shard_map.80 = s16[1808,256]{1,0:T(8,128)(2,1)S(1)} custom-call(s32[7]{0:T(128)S(1)} %stack.31.bits_ref.refs_0_, bf16[2,3,800,256]{3,2,1,0:T(8,128)(2,1)S(1)} %get-tuple-element.69.grid_ref, bf16[256,1024]{1,0:T(8,128)(2,1)S(1)} %get-tuple-element.65.turned_ref), custom_call_target="tpu_custom_call" | custom-call | flops 3623878656 | bytes 5242880 | tf_op jit(solution)/shard_map/pallas_call | solution.py:44
  54.6 0.1 collective-permute-start.9
  54.7 0.5 collective-permute-start.10
  55.2 2.0 %collective-permute-done.9.got_ref = s16[1808,256]{1,0:T(8,128)(2,1)S(1)} collective-permute-done((s16[1808,256]{1,0:T(8,128)(2,1)S(1)}, s16[1808,256]{1,0:T(8,128)(2,1)S(1)}, u32[]{:S(2)}, u32[]{:S(2)}) %collective-permute-start.9) | collective-permute-done | bytes 925728 | tf_op jit(solution)/shard_map/ppermute | solution.py:470
  57.1 1.9 %shard_map.81 = (f32[7,128,256]{2,1,0:T(8,128)S(1)}, s16[912,256]{1,0:T(8,128)(2,1)S(1)}) custom-call(s32[7]{0:T(128)S(1)} %stack.31.bits_ref.refs_0_, bf16[2,3,800,256]{3,2,1,0:T(8,128)(2,1)S(1)} %get-tuple-element.69.grid_ref, bf16[256,1024]{1,0:T(8,128)(2,1)S(1)} %get-tuple-element.65.turned_ref, s16[1808,256]{1,0:T(8,128)(2,1)S(1)} %collective-permute-done.9.got_ref), custom_call_target="tpu_custom_call" | custom-call | flops 3623878656 | bytes 5242880 | tf_op jit(solution)/shard_map/pallas_call | solution.py:44
  59.0 1.6 %collective-permute-start.12 = (s16[912,256]{1,0:T(8,128)(2,1)S(1)}, s16[912,256]{1,0:T(8,128)(2,1)S(1)}, u32[]{:S(2)}, u32[]{:S(2)}) collective-permute-start(s16[912,256]{1,0:T(8,128)(2,1)S(1)} %get-tuple-element.72), channel_id=1, source_target_pairs={{0,2},{1,5},{2,0},{3,7},{4,6},{5,1},{6,4},{7,3},{8,10},{9,13},{10,... | collective-permute-start | bytes 1400840 | tf_op jit(solution)/shard_map/ppermute | solution.py:481
  60.6 0.0 collective-permute-done.10.got_ref
  60.6 1.9 %shard_map.83 = (f32[7,128,256]{2,1,0:T(8,128)S(1)}, s16[912,256]{1,0:T(8,128)(2,1)S(1)}) custom-call(s32[7]{0:T(128)S(1)} %stack.31.bits_ref.refs_0_, bf16[2,3,800,256]{3,2,1,0:T(8,128)(2,1)S(1)} %get-tuple-element.69.grid_ref, bf16[256,1024]{1,0:T(8,128)(2,1)S(1)} %get-tuple-element.65.turned_ref, s16[1808,256]{1,0:T(8,128)(2,1)S(1)} %collective-permute-done.10.got_ref), custom_call_target="tpu_custom_call" | custom-call | flops 3623878656 | bytes 5242880 | tf_op jit(solution)/shard_map/pallas_call | solution.py:44
  62.5 0.6 collective-permute-start.11
  63.1 6.6 %shard_map.82 = bf16[1024,256]{1,0:T(8,128)(2,1)} custom-call(bf16[1024,256]{1,0:T(8,128)(2,1)S(1)} %get-tuple-element.68.x.x_ref, bf16[2,3,800,256]{3,2,1,0:T(8,128)(2,1)S(1)} %get-tuple-element.69.grid_ref, bf16[27,256,256]{2,1,0:T(8,128)(2,1)} %weight_ref.5), custom_call_target="tpu_custom_call" | custom-call | flops 3623878656 | bytes 6291456 | tf_op jit(solution)/shard_map/pallas_call | solution.py:44
  69.7 0.0 collective-permute-done.12.refs_4_
  69.7 3.0 %collective-permute-done.11.refs_2_ = s16[912,256]{1,0:T(8,128)(2,1)S(1)} collective-permute-done((s16[912,256]{1,0:T(8,128)(2,1)S(1)}, s16[912,256]{1,0:T(8,128)(2,1)S(1)}, u32[]{:S(2)}, u32[]{:S(2)}) %collective-permute-start.11) | collective-permute-done | bytes 466976 | tf_op jit(solution)/shard_map/ppermute | solution.py:481
  72.7 1.0 shard_map.84
  73.7 2.4 %collective-permute-start.13 = (s16[912,256]{1,0:T(8,128)(2,1)S(1)}, s16[912,256]{1,0:T(8,128)(2,1)S(1)}, u32[]{:S(2)}, u32[]{:S(2)}) collective-permute-start(s16[912,256]{1,0:T(8,128)(2,1)S(1)} %get-tuple-element.79), channel_id=1, source_target_pairs={{0,4},{1,3},{2,6},{3,1},{4,0},{5,7},{6,2},{7,5},{8,12},{9,11},{10,... | collective-permute-start | bytes 1400840 | tf_op jit(solution)/shard_map/ppermute | solution.py:481
  76.1 6.5 %collective-permute-done.13.refs_2_ = s16[912,256]{1,0:T(8,128)(2,1)S(1)} collective-permute-done((s16[912,256]{1,0:T(8,128)(2,1)S(1)}, s16[912,256]{1,0:T(8,128)(2,1)S(1)}, u32[]{:S(2)}, u32[]{:S(2)}) %collective-permute-start.13) | collective-permute-done | bytes 466976 | tf_op jit(solution)/shard_map/ppermute | solution.py:481
  82.7 0.9 shard_map.85
  83.5 0.3 collective-permute-start.14
  83.8 6.2 %collective-permute-done.14.refs_2_ = s16[464,256]{1,0:T(8,128)(2,1)S(1)} collective-permute-done((s16[464,256]{1,0:T(8,128)(2,1)S(1)}, s16[464,256]{1,0:T(8,128)(2,1)S(1)}, u32[]{:S(2)}, u32[]{:S(2)}) %collective-permute-start.14) | collective-permute-done | bytes 237600 | tf_op jit(solution)/shard_map/ppermute | solution.py:470
  90.0 0.8 shard_map.86
  90.8 2.4 %collective-permute-start.15 = (s16[240,256]{1,0:T(8,128)(2,1)S(1)}, s16[240,256]{1,0:T(8,128)(2,1)S(1)}, u32[]{:S(2)}, u32[]{:S(2)}) collective-permute-start(s16[240,256]{1,0:T(8,128)(2,1)S(1)} %get-tuple-element.83), channel_id=1, source_target_pairs={{0,16},{4,20},{8,24},{12,28},{16,0},{20,4},{24,8},{28,12},{1,17},{... | collective-permute-start | bytes 368648 | tf_op jit(solution)/shard_map/ppermute | solution.py:470
  93.2 6.0 %collective-permute-done.15.got_ref = s16[240,256]{1,0:T(8,128)(2,1)S(1)} collective-permute-done((s16[240,256]{1,0:T(8,128)(2,1)S(1)}, s16[240,256]{1,0:T(8,128)(2,1)S(1)}, u32[]{:S(2)}, u32[]{:S(2)}) %collective-permute-start.15) | collective-permute-done | bytes 122912 | tf_op jit(solution)/shard_map/ppermute | solution.py:470
  99.3 0.2 shard_map.88
  99.5 0.1 collective-permute-start.16
  99.6 2.9 %shard_map.89.first_ref = bf16[512,256]{1,0:T(8,128)(2,1)S(1)} custom-call(bf16[1024,256]{1,0:T(8,128)(2,1)S(1)} %bitcast.15, bf16[464,256]{1,0:T(8,128)(2,1)S(1)} %collective-permute-done.4.refs_5_.up, bf16[464,256]{1,0:T(8,128)(2,1)S(1)} %collective-permute-done.3.refs_3_.down, bf16[128,256]{1,0:T(8,128)(2,1)S(1)} %copy-done.4, s32[2,256]{1,0:T(2,128)S(1)} %copy-done.5, ...), custom_call_target="tpu_custom_call" | custom-call | flops 1811939328 | bytes 5242880 | tf_op jit(solution)/shard_map/pallas_call | solution.py:44
  102.5 3.9 %collective-permute-done.16 = s16[256,256]{1,0:T(8,128)(2,1)S(1)} collective-permute-done((s16[256,256]{1,0:T(8,128)(2,1)S(1)}, s16[256,256]{1,0:T(8,128)(2,1)S(1)}, u32[]{:S(2)}, u32[]{:S(2)}) %collective-permute-start.16) | collective-permute-done | bytes 131104 | tf_op jit(solution)/shard_map/ppermute | solution.py:470
  106.4 0.1 collective-permute-start.17
  106.5 3.9 %shard_map.90 = bf16[1024,256]{1,0:T(8,128)(2,1)} custom-call(bf16[1024,256]{1,0:T(8,128)(2,1)S(1)} %bitcast.16, bf16[464,256]{1,0:T(8,128)(2,1)S(1)} %collective-permute-done.4.refs_5_.up, bf16[464,256]{1,0:T(8,128)(2,1)S(1)} %collective-permute-done.3.refs_3_.down, bf16[128,256]{1,0:T(8,128)(2,1)S(1)} %copy-done.4, s32[2,256]{1,0:T(2,128)S(1)} %copy-done.5, ...), custom_call_target="tpu_custom_call" | custom-call | flops 1811939328 | bytes 5242880 | tf_op jit(solution)/shard_map/pallas_call | solution.py:44
  110.5 2.4 %collective-permute-done.17 = s16[512,256]{1,0:T(8,128)(2,1)S(1)} collective-permute-done((s16[512,256]{1,0:T(8,128)(2,1)S(1)}, s16[512,256]{1,0:T(8,128)(2,1)S(1)}, u32[]{:S(2)}, u32[]{:S(2)}) %collective-permute-start.17) | collective-permute-done | bytes 262176 | tf_op jit(solution)/shard_map/ppermute | solution.py:470
  112.9 1.6 %collective-permute-start.20 = (s16[512,256]{1,0:T(8,128)(2,1)S(1)}, s16[512,256]{1,0:T(8,128)(2,1)S(1)}, u32[]{:S(2)}, u32[]{:S(2)}) collective-permute-start(s16[512,256]{1,0:T(8,128)(2,1)S(1)} %pad_add_fusion.5), channel_id=1, source_target_pairs={{0,2},{1,3},{2,0},{3,1},{4,6},{5,7},{6,4},{7,5},{8,10},{9,11},{10,... | collective-permute-start | bytes 786440 | tf_op jit(solution)/shard_map/ppermute | solution.py:470
  114.5 0.1 collective-permute-start.18
  114.6 7.6 %collective-permute-done.20 = s16[512,256]{1,0:T(8,128)(2,1)S(1)} collective-permute-done((s16[512,256]{1,0:T(8,128)(2,1)S(1)}, s16[512,256]{1,0:T(8,128)(2,1)S(1)}, u32[]{:S(2)}, u32[]{:S(2)}) %collective-permute-start.20) | collective-permute-done | bytes 262176 | tf_op jit(solution)/shard_map/ppermute | solution.py:470
  122.2 0.1 collective-permute-start.21
  122.3 1.5 %collective-permute-done.18 = s16[512,256]{1,0:T(8,128)(2,1)S(1)} collective-permute-done((s16[512,256]{1,0:T(8,128)(2,1)S(1)}, s16[512,256]{1,0:T(8,128)(2,1)S(1)}, u32[]{:S(2)}, u32[]{:S(2)}) %collective-permute-start.18) | collective-permute-done | bytes 262176 | tf_op jit(solution)/shard_map/ppermute | solution.py:470
  123.8 0.7 collective-permute-start.19
  124.5 0.0 collective-permute-start.24
  124.5 0.5 collective-permute-start.22
  125.0 6.5 %collective-permute-done.21.refs_3_ = s16[1024,256]{1,0:T(8,128)(2,1)S(1)} collective-permute-done((s16[1024,256]{1,0:T(8,128)(2,1)S(1)}, s16[1024,256]{1,0:T(8,128)(2,1)S(1)}, u32[]{:S(2)}, u32[]{:S(2)}) %collective-permute-start.21) | collective-permute-done | bytes 524320 | tf_op jit(solution)/shard_map/ppermute | solution.py:470
  131.5 1.6 %collective-permute-done.19.refs_1_ = s16[1024,256]{1,0:T(8,128)(2,1)S(1)} collective-permute-done((s16[1024,256]{1,0:T(8,128)(2,1)S(1)}, s16[1024,256]{1,0:T(8,128)(2,1)S(1)}, u32[]{:S(2)}, u32[]{:S(2)}) %collective-permute-start.19) | collective-permute-done | bytes 524320 | tf_op jit(solution)/shard_map/ppermute | solution.py:470
  133.0 0.0 collective-permute-done.22.refs_4_
  133.1 0.3 collective-permute-done.25.refs_7_
  133.4 1.6 %collective-permute-done.23.refs_5_ = s16[1024,256]{1,0:T(8,128)(2,1)S(1)} collective-permute-done((s16[1024,256]{1,0:T(8,128)(2,1)S(1)}, s16[1024,256]{1,0:T(8,128)(2,1)S(1)}, u32[]{:S(2)}, u32[]{:S(2)}) %collective-permute-start.23) | collective-permute-done | bytes 524320 | tf_op jit(solution)/shard_map/ppermute | solution.py:470
  135.0 3.6 %shard_map.91 = bf16[27,256,256]{2,1,0:T(8,128)(2,1)} custom-call(s32[7]{0:T(128)S(1)} %stack.31.bits_ref.refs_0_, s16[1024,256]{1,0:T(8,128)(2,1)S(1)} %pad_add_fusion.refs_0_, s16[1024,256]{1,0:T(8,128)(2,1)S(1)} %collective-permute-done.19.refs_1_, s16[1024,256]{1,0:T(8,128)(2,1)S(1)} %pad_add_fusion.1.refs_2_, ...), custom_call_target="tpu_custom_call" | custom-call | tf_op jit(solution)/shard_map/pallas_call | solution.py:44
  (25 shorter events, 0.2 us)
Async XLA Ops:
  0.6 28.0 %copy-start = (bf16[1,1024,256]{2,1,0:T(8,128)(2,1)S(1)}, bf16[1,1024,256]{2,1,0:T(8,128)(2,1)}, u32[]{:S(2)}) copy-start(bf16[1,1024,256]{2,1,0:T(8,128)(2,1)} %param.9) | copy-start | bytes 1572868
  5.6 44.0 %copy-start.5 = (s32[2,256]{1,0:T(2,128)S(1)}, s32[2,256]{1,0:T(2,128)}, u32[]{:S(2)}) copy-start(s32[2,256]{1,0:T(2,128)} %get-tuple-element.64.ekey) | copy-start | bytes 6148
  5.6 14.9 %collective-permute-start = (bf16[272,256]{1,0:T(8,128)(2,1)}, bf16[272,256]{1,0:T(8,128)(2,1)S(1)}, u32[]{:S(2)}, u32[]{:S(2)}) collective-permute-start(bf16[272,256]{1,0:T(8,128)(2,1)} %get-tuple-element.49), channel_id=1, source_target_pairs={{0,16},{4,20},{8,24},{12,28},{16,0},{20,4},{24,8},{28,12},{1,17},{... | collective-permute-start | bytes 417800 | tf_op jit(solution)/shard_map/ppermute | solution.py:538
  9.7 18.9 %collective-permute-start.1 = (bf16[272,256]{1,0:T(8,128)(2,1)}, bf16[272,256]{1,0:T(8,128)(2,1)S(1)}, u32[]{:S(2)}, u32[]{:S(2)}) collective-permute-start(bf16[272,256]{1,0:T(8,128)(2,1)} %get-tuple-element.50), channel_id=1, source_target_pairs={{0,20},{4,24},{8,28},{12,0},{16,4},{20,8},{24,12},{28,16},{1,21},{... | collective-permute-start | bytes 417800 | tf_op jit(solution)/shard_map/ppermute | solution.py:538
  11.0 25.0 %collective-permute-start.3 = (bf16[464,256]{1,0:T(8,128)(2,1)}, bf16[464,256]{1,0:T(8,128)(2,1)S(1)}, u32[]{:S(2)}, u32[]{:S(2)}) collective-permute-start(bf16[464,256]{1,0:T(8,128)(2,1)} %get-tuple-element.52), channel_id=1, source_target_pairs={{0,28},{4,0},{8,4},{12,8},{16,12},{20,16},{24,20},{28,24},{1,29},{... | collective-permute-start | bytes 712712 | tf_op jit(solution)/shard_map/ppermute | solution.py:538
  12.2 23.9 %collective-permute-start.4 = (bf16[464,256]{1,0:T(8,128)(2,1)}, bf16[464,256]{1,0:T(8,128)(2,1)S(1)}, u32[]{:S(2)}, u32[]{:S(2)}) collective-permute-start(bf16[464,256]{1,0:T(8,128)(2,1)} %get-tuple-element.56), channel_id=1, source_target_pairs={{0,4},{4,8},{8,12},{12,16},{16,20},{20,24},{24,28},{28,0},{1,5},{5... | collective-permute-start | bytes 712712 | tf_op jit(solution)/shard_map/ppermute | solution.py:538
  13.1 17.4 %collective-permute-start.2 = (bf16[272,256]{1,0:T(8,128)(2,1)}, bf16[272,256]{1,0:T(8,128)(2,1)S(1)}, u32[]{:S(2)}, u32[]{:S(2)}) collective-permute-start(bf16[272,256]{1,0:T(8,128)(2,1)} %get-tuple-element.51), channel_id=1, source_target_pairs={{0,24},{4,28},{8,0},{12,4},{16,8},{20,12},{24,16},{28,20},{1,25},{... | collective-permute-start | bytes 417800 | tf_op jit(solution)/shard_map/ppermute | solution.py:538
  20.5 15.5 %collective-permute-start.5 = (bf16[272,256]{1,0:T(8,128)(2,1)}, bf16[272,256]{1,0:T(8,128)(2,1)S(1)}, u32[]{:S(2)}, u32[]{:S(2)}) collective-permute-start(bf16[272,256]{1,0:T(8,128)(2,1)} %get-tuple-element.57), channel_id=1, source_target_pairs={{0,8},{4,12},{8,16},{12,20},{16,24},{20,28},{24,0},{28,4},{1,9},{5... | collective-permute-start | bytes 417800 | tf_op jit(solution)/shard_map/ppermute | solution.py:538
  28.6 7.5 %collective-permute-start.6 = (bf16[272,256]{1,0:T(8,128)(2,1)}, bf16[272,256]{1,0:T(8,128)(2,1)S(1)}, u32[]{:S(2)}, u32[]{:S(2)}) collective-permute-start(bf16[272,256]{1,0:T(8,128)(2,1)} %get-tuple-element.58), channel_id=1, source_target_pairs={{0,12},{4,16},{8,20},{12,24},{16,28},{20,0},{24,4},{28,8},{1,13},{... | collective-permute-start | bytes 417800 | tf_op jit(solution)/shard_map/ppermute | solution.py:538
  28.6 0.9 copy-start.1
  29.5 0.7 copy-start.2
  37.6 7.8 %collective-permute-start.7 = (bf16[192,256]{1,0:T(8,128)(2,1)S(1)}, bf16[192,256]{1,0:T(8,128)(2,1)S(1)}, u32[]{:S(2)}, u32[]{:S(2)}) collective-permute-start(bf16[192,256]{1,0:T(8,128)(2,1)S(1)} %get-tuple-element.61), channel_id=1, source_target_pairs={{0,4},{4,8},{8,12},{12,16},{16,20},{20,24},{24,28},{1,5},{5,9},{9,... | collective-permute-start | bytes 294920 | tf_op jit(solution)/shard_map/ppermute | solution.py:486
  43.1 6.5 %collective-permute-start.8 = (bf16[192,256]{1,0:T(8,128)(2,1)S(1)}, bf16[192,256]{1,0:T(8,128)(2,1)S(1)}, u32[]{:S(2)}, u32[]{:S(2)}) collective-permute-start(bf16[192,256]{1,0:T(8,128)(2,1)S(1)} %get-tuple-element.62), channel_id=1, source_target_pairs={{4,0},{8,4},{12,8},{16,12},{20,16},{24,20},{28,24},{5,1},{9,5},{13... | collective-permute-start | bytes 294920 | tf_op jit(solution)/shard_map/ppermute | solution.py:486
  54.6 2.5 %collective-permute-start.9 = (s16[1808,256]{1,0:T(8,128)(2,1)S(1)}, s16[1808,256]{1,0:T(8,128)(2,1)S(1)}, u32[]{:S(2)}, u32[]{:S(2)}) collective-permute-start(s16[1808,256]{1,0:T(8,128)(2,1)S(1)} %shard_map.80), channel_id=1, source_target_pairs={{0,1},{1,0},{2,3},{3,2},{4,5},{5,4},{6,7},{7,6},{8,9},{9,8},{10,11... | collective-permute-start | bytes 2777096 | tf_op jit(solution)/shard_map/ppermute | solution.py:470
  54.7 5.9 %collective-permute-start.10 = (s16[1808,256]{1,0:T(8,128)(2,1)S(1)}, s16[1808,256]{1,0:T(8,128)(2,1)S(1)}, u32[]{:S(2)}, u32[]{:S(2)}) collective-permute-start(s16[1808,256]{1,0:T(8,128)(2,1)S(1)} %get-tuple-element.70), channel_id=1, source_target_pairs={{0,1},{1,0},{2,3},{3,2},{4,5},{5,4},{6,7},{7,6},{8,9},{9,8},{10,11... | collective-permute-start | bytes 2777096 | tf_op jit(solution)/shard_map/ppermute | solution.py:470
  59.0 10.7 %collective-permute-start.12 = (s16[912,256]{1,0:T(8,128)(2,1)S(1)}, s16[912,256]{1,0:T(8,128)(2,1)S(1)}, u32[]{:S(2)}, u32[]{:S(2)}) collective-permute-start(s16[912,256]{1,0:T(8,128)(2,1)S(1)} %get-tuple-element.72), channel_id=1, source_target_pairs={{0,2},{1,5},{2,0},{3,7},{4,6},{5,1},{6,4},{7,3},{8,10},{9,13},{10,... | collective-permute-start | bytes 1400840 | tf_op jit(solution)/shard_map/ppermute | solution.py:481
  62.5 10.2 %collective-permute-start.11 = (s16[912,256]{1,0:T(8,128)(2,1)S(1)}, s16[912,256]{1,0:T(8,128)(2,1)S(1)}, u32[]{:S(2)}, u32[]{:S(2)}) collective-permute-start(s16[912,256]{1,0:T(8,128)(2,1)S(1)} %get-tuple-element.71), channel_id=1, source_target_pairs={{0,2},{1,5},{2,0},{3,7},{4,6},{5,1},{6,4},{7,3},{8,10},{9,13},{10,... | collective-permute-start | bytes 1400840 | tf_op jit(solution)/shard_map/ppermute | solution.py:481
  69.7 29.9 %copy-start.3 = (bf16[27,256,256]{2,1,0:T(8,128)(2,1)S(1)}, bf16[27,256,256]{2,1,0:T(8,128)(2,1)}, u32[]{:S(2)}) copy-start(bf16[27,256,256]{2,1,0:T(8,128)(2,1)} %weight_ref.5) | copy-start | bytes 10616836
  69.7 29.9 %copy-start.4 = (bf16[128,256]{1,0:T(8,128)(2,1)S(1)}, bf16[128,256]{1,0:T(8,128)(2,1)}, u32[]{:S(2)}) copy-start(bf16[128,256]{1,0:T(8,128)(2,1)} %get-tuple-element.89.local) | copy-start | bytes 196612
  73.7 9.0 %collective-permute-start.13 = (s16[912,256]{1,0:T(8,128)(2,1)S(1)}, s16[912,256]{1,0:T(8,128)(2,1)S(1)}, u32[]{:S(2)}, u32[]{:S(2)}) collective-permute-start(s16[912,256]{1,0:T(8,128)(2,1)S(1)} %get-tuple-element.79), channel_id=1, source_target_pairs={{0,4},{1,3},{2,6},{3,1},{4,0},{5,7},{6,2},{7,5},{8,12},{9,11},{10,... | collective-permute-start | bytes 1400840 | tf_op jit(solution)/shard_map/ppermute | solution.py:481
  83.5 6.5 %collective-permute-start.14 = (s16[464,256]{1,0:T(8,128)(2,1)S(1)}, s16[464,256]{1,0:T(8,128)(2,1)S(1)}, u32[]{:S(2)}, u32[]{:S(2)}) collective-permute-start(s16[464,256]{1,0:T(8,128)(2,1)S(1)} %get-tuple-element.81), channel_id=1, source_target_pairs={{0,8},{4,12},{8,0},{12,4},{16,24},{20,28},{24,16},{28,20},{1,9},{5... | collective-permute-start | bytes 712712 | tf_op jit(solution)/shard_map/ppermute | solution.py:470
  90.8 8.5 %collective-permute-start.15 = (s16[240,256]{1,0:T(8,128)(2,1)S(1)}, s16[240,256]{1,0:T(8,128)(2,1)S(1)}, u32[]{:S(2)}, u32[]{:S(2)}) collective-permute-start(s16[240,256]{1,0:T(8,128)(2,1)S(1)} %get-tuple-element.83), channel_id=1, source_target_pairs={{0,16},{4,20},{8,24},{12,28},{16,0},{20,4},{24,8},{28,12},{1,17},{... | collective-permute-start | bytes 368648 | tf_op jit(solution)/shard_map/ppermute | solution.py:470
  99.5 6.9 %collective-permute-start.16 = (s16[256,256]{1,0:T(8,128)(2,1)S(1)}, s16[256,256]{1,0:T(8,128)(2,1)S(1)}, u32[]{:S(2)}, u32[]{:S(2)}) collective-permute-start(s16[256,256]{1,0:T(8,128)(2,1)S(1)} %pad_add_fusion.6), channel_id=1, source_target_pairs={{0,16},{4,20},{8,24},{12,28},{16,0},{20,4},{24,8},{28,12},{1,17},{... | collective-permute-start | bytes 393224 | tf_op jit(solution)/shard_map/ppermute | solution.py:470
  106.4 6.4 %collective-permute-start.17 = (s16[512,256]{1,0:T(8,128)(2,1)S(1)}, s16[512,256]{1,0:T(8,128)(2,1)S(1)}, u32[]{:S(2)}, u32[]{:S(2)}) collective-permute-start(s16[512,256]{1,0:T(8,128)(2,1)S(1)} %pad_add_fusion.2), channel_id=1, source_target_pairs={{0,8},{4,12},{8,0},{12,4},{16,24},{20,28},{24,16},{28,20},{1,9},{5... | collective-permute-start | bytes 786440 | tf_op jit(solution)/shard_map/ppermute | solution.py:470
  112.9 9.2 %collective-permute-start.20 = (s16[512,256]{1,0:T(8,128)(2,1)S(1)}, s16[512,256]{1,0:T(8,128)(2,1)S(1)}, u32[]{:S(2)}, u32[]{:S(2)}) collective-permute-start(s16[512,256]{1,0:T(8,128)(2,1)S(1)} %pad_add_fusion.5), channel_id=1, source_target_pairs={{0,2},{1,3},{2,0},{3,1},{4,6},{5,7},{6,4},{7,5},{8,10},{9,11},{10,... | collective-permute-start | bytes 786440 | tf_op jit(solution)/shard_map/ppermute | solution.py:470
  114.5 9.3 %collective-permute-start.18 = (s16[512,256]{1,0:T(8,128)(2,1)S(1)}, s16[512,256]{1,0:T(8,128)(2,1)S(1)}, u32[]{:S(2)}, u32[]{:S(2)}) collective-permute-start(s16[512,256]{1,0:T(8,128)(2,1)S(1)} %pad_add_fusion.4), channel_id=1, source_target_pairs={{0,4},{4,0},{8,12},{12,8},{16,20},{20,16},{24,28},{28,24},{1,5},{5... | collective-permute-start | bytes 786440 | tf_op jit(solution)/shard_map/ppermute | solution.py:470
  122.2 9.2 %collective-permute-start.21 = (s16[1024,256]{1,0:T(8,128)(2,1)S(1)}, s16[1024,256]{1,0:T(8,128)(2,1)S(1)}, u32[]{:S(2)}, u32[]{:S(2)}) collective-permute-start(s16[1024,256]{1,0:T(8,128)(2,1)S(1)} %pad_add_fusion.1.refs_2_), channel_id=1, source_target_pairs={{0,4},{4,0},{8,12},{12,8},{16,20},{20,16},{24,28},{28,24},{1,5},{5... | collective-permute-start | bytes 1572872 | tf_op jit(solution)/shard_map/ppermute | solution.py:470
  123.8 9.2 %collective-permute-start.19 = (s16[1024,256]{1,0:T(8,128)(2,1)S(1)}, s16[1024,256]{1,0:T(8,128)(2,1)S(1)}, u32[]{:S(2)}, u32[]{:S(2)}) collective-permute-start(s16[1024,256]{1,0:T(8,128)(2,1)S(1)} %pad_add_fusion.refs_0_), channel_id=1, source_target_pairs={{0,2},{1,3},{2,0},{3,1},{4,6},{5,7},{6,4},{7,5},{8,10},{9,11},{10,... | collective-permute-start | bytes 1572872 | tf_op jit(solution)/shard_map/ppermute | solution.py:470
  124.5 8.6 %collective-permute-start.24 = (s16[1024,256]{1,0:T(8,128)(2,1)S(1)}, s16[1024,256]{1,0:T(8,128)(2,1)S(1)}, u32[]{:S(2)}, u32[]{:S(2)}) collective-permute-start(s16[1024,256]{1,0:T(8,128)(2,1)S(1)} %pad_add_fusion.1.refs_2_), channel_id=1, source_target_pairs={{0,1},{1,0},{2,3},{3,2},{4,5},{5,4},{6,7},{7,6},{8,9},{9,8},{10,11... | collective-permute-start | bytes 1572872 | tf_op jit(solution)/shard_map/ppermute | solution.py:470
  124.5 8.6 %collective-permute-start.22 = (s16[1024,256]{1,0:T(8,128)(2,1)S(1)}, s16[1024,256]{1,0:T(8,128)(2,1)S(1)}, u32[]{:S(2)}, u32[]{:S(2)}) collective-permute-start(s16[1024,256]{1,0:T(8,128)(2,1)S(1)} %pad_add_fusion.refs_0_), channel_id=1, source_target_pairs={{0,1},{1,0},{2,3},{3,2},{4,5},{5,4},{6,7},{7,6},{8,9},{9,8},{10,11... | collective-permute-start | bytes 1572872 | tf_op jit(solution)/shard_map/ppermute | solution.py:470
  131.5 1.9 %collective-permute-start.25 = (s16[1024,256]{1,0:T(8,128)(2,1)S(1)}, s16[1024,256]{1,0:T(8,128)(2,1)S(1)}, u32[]{:S(2)}, u32[]{:S(2)}) collective-permute-start(s16[1024,256]{1,0:T(8,128)(2,1)S(1)} %collective-permute-done.21.refs_3_), channel_id=1, source_target_pairs={{0,1},{1,0},{2,3},{3,2},{4,5},{5,4},{6,7},{7,6},{8,9},{9,8},{10,11... | collective-permute-start | bytes 1572872 | tf_op jit(solution)/shard_map/ppermute | solution.py:470
  133.0 1.9 %collective-permute-start.23 = (s16[1024,256]{1,0:T(8,128)(2,1)S(1)}, s16[1024,256]{1,0:T(8,128)(2,1)S(1)}, u32[]{:S(2)}, u32[]{:S(2)}) collective-permute-start(s16[1024,256]{1,0:T(8,128)(2,1)S(1)} %collective-permute-done.19.refs_1_), channel_id=1, source_target_pairs={{0,1},{1,0},{2,3},{3,2},{4,5},{5,4},{6,7},{7,6},{8,9},{9,8},{10,11... | collective-permute-start | bytes 1572872 | tf_op jit(solution)/shard_map/ppermute | solution.py:470

commit v3 on v2

--- a/solution.py
+++ b/solution.py
@@ -392,6 +392,11 @@
     tail = tail_codes(got_ref, HALF * 16)
     for i in range(HALF):
         out_ref[i] = acc_ref[i] + decode(got_ref[i * 16 : i * 16 + 16, :], tail[i : i + 1])
+
+
+def total_unit_body(acc_ref, got_ref, a_ref, b_ref, total_ref):
+    total_body(acc_ref, got_ref, total_ref)
+    unit_body(total_ref, a_ref, b_ref)
 
 
 def unit_body(total_ref, a_ref, b_ref):
@@ -610,10 +615,16 @@
     came = swap(send, s3)
     keep, send = reduce_step(bits, 4, [keep, came], ((0, HALF, HALF),), 32)
     came = swap(send, s4)
-    (total,) = call(total_body, [((HALF, 16, C), F32)], [keep, came])
-    for b in extra:
-        total = total + swap(total, b)
-    unit_a, unit_b = call(unit_body, [((UNIT, C), I16), ((UNIT, C), I16)], [total])
+    units = [((UNIT, C), I16), ((UNIT, C), I16)]
+    if extra:
+        (total,) = call(total_body, [((HALF, 16, C), F32)], [keep, came])
+        for b in extra:
+            total = total + swap(total, b)
+        unit_a, unit_b = call(unit_body, units, [total])
+    else:
+        unit_a, unit_b = call(
+            total_unit_body, units, [keep, came], scratch=[pltpu.VMEM((HALF, 16, C), F32)]
+        )
 
     unit_a, unit_b, dy = lax.optimization_barrier((unit_a, unit_b, dy))
     back_args = [got[window // 2 + 1], got[window // 2 - 1], dy_local, ekey, weight]

time: 139 us -> 139 us (level)
    pallas_call x16 -> x15, Pallas kernels: 35.3 us -> 35.4 us  [call(): pl.pallas_call(body, out_shape=shapes, in_specs=specs, out_specs=[pl.Bloc...]
where the time goes in v3:
time: 139 us
  waiting for transfers between devices  63.5 us (46%)
  starting transfers between devices  37 us (27%)
  Pallas kernels  35.4 us (25%)
  local copies, waits for them, and re-layouts  1.75 us (1%)
    ppermute x14, waiting for transfers between devices, swap(): return lax.ppermute(x, axis, [(i, i ^ 1 << place) for i in range(count)])  39.5 us
    pallas_call x15, Pallas kernels, call(): pl.pallas_call(body, out_shape=shapes, in_specs=specs, out_specs=[pl.Bloc...  35.4 us
    ppermute x7, starting transfers between devices, on_device(): got[w] = packed[w] if step == 0 else lax.ppermute(packed[w], 'pts', turn)  19.1 us
    ppermute x3, waiting for transfers between devices, swap_either(): return lax.ppermute(x, ('pts', 'dp'), turn)  9.51 us
    ppermute x7, waiting for transfers between devices, on_device(): got[w] = packed[w] if step == 0 else lax.ppermute(packed[w], 'pts', turn)  9.48 us
    ppermute x2, starting transfers between devices, shift(): lax.ppermute(x, 'pts', [(i, i + step) for i in range(count) if 0 <= i + s...  7.04 us
    ppermute x14, starting transfers between devices, swap(): return lax.ppermute(x, axis, [(i, i ^ 1 << place) for i in range(count)])  6.27 us
    ppermute x2, waiting for transfers between devices, shift(): lax.ppermute(x, 'pts', [(i, i + step) for i in range(count) if 0 <= i + s...  4.93 us
  transfers between devices with their start and end apart: 26, of which 17 were waited for; matrix products, arithmetic and copies ran while one was open for 0% of the time, Pallas kernels for 13%

profile of v3, /device:TPU:0, one launch (start us, length us, event | category | flops | bytes accessed | tf_op | source)
XLA Modules:
  0.0 138.8 jit_solution(3249137598121100070)
XLA Ops:
  0.6 5.0 %shard_map.76 = (bf16[272,256]{1,0:T(8,128)(2,1)}, bf16[272,256]{1,0:T(8,128)(2,1)}, bf16[272,256]{1,0:T(8,128)(2,1)}, bf16[464,256]{1,0:T(8,128)(2,1)}, bf16[27...) custom-call(s32[1]{0:T(128)} %bitcast.me_ref, ...), custom_call_target="tpu_custom_call" | custom-call | flops 1073741824 | bytes 2097152 | tf_op jit(solution)/shard_map/pallas_call | solution.py:44
  5.6 4.1 %collective-permute-start = (bf16[272,256]{1,0:T(8,128)(2,1)}, bf16[272,256]{1,0:T(8,128)(2,1)S(1)}, u32[]{:S(2)}, u32[]{:S(2)}) collective-permute-start(bf16[272,256]{1,0:T(8,128)(2,1)} %get-tuple-element.49), channel_id=1, source_target_pairs={{0,16},{4,20},{8,24},{12,28},{16,0},{20,4},{24,8},{28,12},{1,17},{... | collective-permute-start | bytes 417800 | tf_op jit(solution)/shard_map/ppermute | solution.py:543
  9.7 1.3 collective-permute-start.1
  11.0 1.1 collective-permute-start.3
  12.2 0.9 collective-permute-start.4
  13.1 3.6 %collective-permute-start.2 = (bf16[272,256]{1,0:T(8,128)(2,1)}, bf16[272,256]{1,0:T(8,128)(2,1)S(1)}, u32[]{:S(2)}, u32[]{:S(2)}) collective-permute-start(bf16[272,256]{1,0:T(8,128)(2,1)} %get-tuple-element.51), channel_id=1, source_target_pairs={{0,24},{4,28},{8,0},{12,4},{16,8},{20,12},{24,16},{28,20},{1,25},{... | collective-permute-start | bytes 417800 | tf_op jit(solution)/shard_map/ppermute | solution.py:543
  16.7 3.9 %collective-permute-done.refs_0_ = bf16[272,256]{1,0:T(8,128)(2,1)S(1)} collective-permute-done((bf16[272,256]{1,0:T(8,128)(2,1)}, bf16[272,256]{1,0:T(8,128)(2,1)S(1)}, u32[]{:S(2)}, u32[]{:S(2)}) %collective-permute-start) | collective-permute-done | bytes 139296 | tf_op jit(solution)/shard_map/ppermute | solution.py:543
  20.5 8.1 %collective-permute-start.5 = (bf16[272,256]{1,0:T(8,128)(2,1)}, bf16[272,256]{1,0:T(8,128)(2,1)S(1)}, u32[]{:S(2)}, u32[]{:S(2)}) collective-permute-start(bf16[272,256]{1,0:T(8,128)(2,1)} %get-tuple-element.57), channel_id=1, source_target_pairs={{0,8},{4,12},{8,16},{12,20},{16,24},{20,28},{24,0},{28,4},{1,9},{5... | collective-permute-start | bytes 417800 | tf_op jit(solution)/shard_map/ppermute | solution.py:543
  28.6 0.0 collective-permute-done.1.refs_1_
  28.6 0.0 collective-permute-start.6
  28.6 0.9 copy-done.1
  29.5 0.7 copy-done.2
  30.2 0.2 shard_map.77
  30.4 0.0 collective-permute-done.2.refs_2_
  30.4 5.6 %collective-permute-done.5.refs_6_ = bf16[272,256]{1,0:T(8,128)(2,1)S(1)} collective-permute-done((bf16[272,256]{1,0:T(8,128)(2,1)}, bf16[272,256]{1,0:T(8,128)(2,1)S(1)}, u32[]{:S(2)}, u32[]{:S(2)}) %collective-permute-start.5) | collective-permute-done | bytes 139296 | tf_op jit(solution)/shard_map/ppermute | solution.py:543
  36.0 0.0 collective-permute-done.4.refs_5_.up
  36.1 1.5 %shard_map.78 = (bf16[1024,256]{1,0:T(8,128)(2,1)S(1)}, bf16[192,256]{1,0:T(8,128)(2,1)S(1)}, bf16[192,256]{1,0:T(8,128)(2,1)S(1)}, bf16[128,256]{1,0:T(8,128)(2,1)S(1)}) custom-call(bf16[272,256]{1,0:T(8,128)(2,1)S(1)} %collective-permute-done.refs_0_, bf16[272,256]{1,0:T(8,128)(2,1)S(1)} %collective-permute-done.1.refs_1_, ...), custom_call_target="tpu_custom_call" | custom-call | flops 1073741824 | bytes 2097152 | tf_op jit(solution)/shard_map/pallas_call | solution.py:44
  37.6 5.6 %collective-permute-start.7 = (bf16[192,256]{1,0:T(8,128)(2,1)S(1)}, bf16[192,256]{1,0:T(8,128)(2,1)S(1)}, u32[]{:S(2)}, u32[]{:S(2)}) collective-permute-start(bf16[192,256]{1,0:T(8,128)(2,1)S(1)} %get-tuple-element.61), channel_id=1, source_target_pairs={{0,4},{4,8},{8,12},{12,16},{16,20},{20,24},{24,28},{1,5},{5,9},{9,... | collective-permute-start | bytes 294920 | tf_op jit(solution)/shard_map/ppermute | solution.py:491
  43.1 1.5 %collective-permute-start.8 = (bf16[192,256]{1,0:T(8,128)(2,1)S(1)}, bf16[192,256]{1,0:T(8,128)(2,1)S(1)}, u32[]{:S(2)}, u32[]{:S(2)}) collective-permute-start(bf16[192,256]{1,0:T(8,128)(2,1)S(1)} %get-tuple-element.62), channel_id=1, source_target_pairs={{4,0},{8,4},{12,8},{16,12},{20,16},{24,20},{28,24},{5,1},{9,5},{13... | collective-permute-start | bytes 294920 | tf_op jit(solution)/shard_map/ppermute | solution.py:491
  44.6 0.1 stack.31.bits_ref.refs_0_
  44.7 0.6 collective-permute-done.7.up
  45.3 4.3 %collective-permute-done.8.down = bf16[192,256]{1,0:T(8,128)(2,1)S(1)} collective-permute-done((bf16[192,256]{1,0:T(8,128)(2,1)S(1)}, bf16[192,256]{1,0:T(8,128)(2,1)S(1)}, u32[]{:S(2)}, u32[]{:S(2)}) %collective-permute-start.8) | collective-permute-done | bytes 98336 | tf_op jit(solution)/shard_map/ppermute | solution.py:491
  49.6 3.0 %shard_map.79 = (bf16[2,3,800,256]{3,2,1,0:T(8,128)(2,1)S(1)}, s16[1808,256]{1,0:T(8,128)(2,1)S(1)}) custom-call(s32[7]{0:T(128)S(1)} %stack.31.bits_ref.refs_0_, bf16[1024,256]{1,0:T(8,128)(2,1)S(1)} %get-tuple-element.68.x.x_ref, bf16[192,256]{1,0:T(8,128)(2,1)S(1)} %collective-permute-done.7.up, bf16[192,256]{1,0:T(8,128)(2,1)S(1)} %collective-permute-done.8.down, ...), custom_call_target="tpu_custom_call" | custom-call | flops 3623878656 | bytes 5242880 | tf_op jit(solution)/shard_map/pallas_call | solution.py:44
  52.7 1.9 %shard_map.80 = s16[1808,256]{1,0:T(8,128)(2,1)S(1)} custom-call(s32[7]{0:T(128)S(1)} %stack.31.bits_ref.refs_0_, bf16[2,3,800,256]{3,2,1,0:T(8,128)(2,1)S(1)} %get-tuple-element.69.grid_ref, bf16[256,1024]{1,0:T(8,128)(2,1)S(1)} %get-tuple-element.65.turned_ref), custom_call_target="tpu_custom_call" | custom-call | flops 3623878656 | bytes 5242880 | tf_op jit(solution)/shard_map/pallas_call | solution.py:44
  54.6 0.1 collective-permute-start.9
  54.7 0.5 collective-permute-start.10
  55.2 2.0 %collective-permute-done.9.got_ref = s16[1808,256]{1,0:T(8,128)(2,1)S(1)} collective-permute-done((s16[1808,256]{1,0:T(8,128)(2,1)S(1)}, s16[1808,256]{1,0:T(8,128)(2,1)S(1)}, u32[]{:S(2)}, u32[]{:S(2)}) %collective-permute-start.9) | collective-permute-done | bytes 925728 | tf_op jit(solution)/shard_map/ppermute | solution.py:475
  57.1 1.9 %shard_map.81 = (f32[7,128,256]{2,1,0:T(8,128)S(1)}, s16[912,256]{1,0:T(8,128)(2,1)S(1)}) custom-call(s32[7]{0:T(128)S(1)} %stack.31.bits_ref.refs_0_, bf16[2,3,800,256]{3,2,1,0:T(8,128)(2,1)S(1)} %get-tuple-element.69.grid_ref, bf16[256,1024]{1,0:T(8,128)(2,1)S(1)} %get-tuple-element.65.turned_ref, s16[1808,256]{1,0:T(8,128)(2,1)S(1)} %collective-permute-done.9.got_ref), custom_call_target="tpu_custom_call" | custom-call | flops 3623878656 | bytes 5242880 | tf_op jit(solution)/shard_map/pallas_call | solution.py:44
  59.0 1.6 %collective-permute-start.12 = (s16[912,256]{1,0:T(8,128)(2,1)S(1)}, s16[912,256]{1,0:T(8,128)(2,1)S(1)}, u32[]{:S(2)}, u32[]{:S(2)}) collective-permute-start(s16[912,256]{1,0:T(8,128)(2,1)S(1)} %get-tuple-element.72), channel_id=1, source_target_pairs={{0,2},{1,5},{2,0},{3,7},{4,6},{5,1},{6,4},{7,3},{8,10},{9,13},{10,... | collective-permute-start | bytes 1400840 | tf_op jit(solution)/shard_map/ppermute | solution.py:486
  60.6 0.0 collective-permute-done.10.got_ref
  60.6 1.9 %shard_map.83 = (f32[7,128,256]{2,1,0:T(8,128)S(1)}, s16[912,256]{1,0:T(8,128)(2,1)S(1)}) custom-call(s32[7]{0:T(128)S(1)} %stack.31.bits_ref.refs_0_, bf16[2,3,800,256]{3,2,1,0:T(8,128)(2,1)S(1)} %get-tuple-element.69.grid_ref, bf16[256,1024]{1,0:T(8,128)(2,1)S(1)} %get-tuple-element.65.turned_ref, s16[1808,256]{1,0:T(8,128)(2,1)S(1)} %collective-permute-done.10.got_ref), custom_call_target="tpu_custom_call" | custom-call | flops 3623878656 | bytes 5242880 | tf_op jit(solution)/shard_map/pallas_call | solution.py:44
  62.5 0.6 collective-permute-start.11
  63.1 6.6 %shard_map.82 = bf16[1024,256]{1,0:T(8,128)(2,1)} custom-call(bf16[1024,256]{1,0:T(8,128)(2,1)S(1)} %get-tuple-element.68.x.x_ref, bf16[2,3,800,256]{3,2,1,0:T(8,128)(2,1)S(1)} %get-tuple-element.69.grid_ref, bf16[27,256,256]{2,1,0:T(8,128)(2,1)} %weight_ref.5), custom_call_target="tpu_custom_call" | custom-call | flops 3623878656 | bytes 6291456 | tf_op jit(solution)/shard_map/pallas_call | solution.py:44
  69.7 0.0 collective-permute-done.12.refs_4_
  69.7 3.0 %collective-permute-done.11.refs_2_ = s16[912,256]{1,0:T(8,128)(2,1)S(1)} collective-permute-done((s16[912,256]{1,0:T(8,128)(2,1)S(1)}, s16[912,256]{1,0:T(8,128)(2,1)S(1)}, u32[]{:S(2)}, u32[]{:S(2)}) %collective-permute-start.11) | collective-permute-done | bytes 466976 | tf_op jit(solution)/shard_map/ppermute | solution.py:486
  72.7 1.0 shard_map.84
  73.7 2.4 %collective-permute-start.13 = (s16[912,256]{1,0:T(8,128)(2,1)S(1)}, s16[912,256]{1,0:T(8,128)(2,1)S(1)}, u32[]{:S(2)}, u32[]{:S(2)}) collective-permute-start(s16[912,256]{1,0:T(8,128)(2,1)S(1)} %get-tuple-element.79), channel_id=1, source_target_pairs={{0,4},{1,3},{2,6},{3,1},{4,0},{5,7},{6,2},{7,5},{8,12},{9,11},{10,... | collective-permute-start | bytes 1400840 | tf_op jit(solution)/shard_map/ppermute | solution.py:486
  76.1 6.5 %collective-permute-done.13.refs_2_ = s16[912,256]{1,0:T(8,128)(2,1)S(1)} collective-permute-done((s16[912,256]{1,0:T(8,128)(2,1)S(1)}, s16[912,256]{1,0:T(8,128)(2,1)S(1)}, u32[]{:S(2)}, u32[]{:S(2)}) %collective-permute-start.13) | collective-permute-done | bytes 466976 | tf_op jit(solution)/shard_map/ppermute | solution.py:486
  82.7 0.9 shard_map.85
  83.5 0.3 collective-permute-start.14
  83.8 6.2 %collective-permute-done.14.refs_2_ = s16[464,256]{1,0:T(8,128)(2,1)S(1)} collective-permute-done((s16[464,256]{1,0:T(8,128)(2,1)S(1)}, s16[464,256]{1,0:T(8,128)(2,1)S(1)}, u32[]{:S(2)}, u32[]{:S(2)}) %collective-permute-start.14) | collective-permute-done | bytes 237600 | tf_op jit(solution)/shard_map/ppermute | solution.py:475
  90.0 0.8 shard_map.86
  90.8 2.4 %collective-permute-start.15 = (s16[240,256]{1,0:T(8,128)(2,1)S(1)}, s16[240,256]{1,0:T(8,128)(2,1)S(1)}, u32[]{:S(2)}, u32[]{:S(2)}) collective-permute-start(s16[240,256]{1,0:T(8,128)(2,1)S(1)} %get-tuple-element.83), channel_id=1, source_target_pairs={{0,16},{4,20},{8,24},{12,28},{16,0},{20,4},{24,8},{28,12},{1,17},{... | collective-permute-start | bytes 368648 | tf_op jit(solution)/shard_map/ppermute | solution.py:475
  93.2 6.0 %collective-permute-done.15.got_ref = s16[240,256]{1,0:T(8,128)(2,1)S(1)} collective-permute-done((s16[240,256]{1,0:T(8,128)(2,1)S(1)}, s16[240,256]{1,0:T(8,128)(2,1)S(1)}, u32[]{:S(2)}, u32[]{:S(2)}) %collective-permute-start.15) | collective-permute-done | bytes 122912 | tf_op jit(solution)/shard_map/ppermute | solution.py:475
  99.2 0.2 shard_map.87
  99.5 0.1 collective-permute-start.16
  99.6 2.9 %shard_map.88.first_ref = bf16[512,256]{1,0:T(8,128)(2,1)S(1)} custom-call(bf16[1024,256]{1,0:T(8,128)(2,1)S(1)} %bitcast.15, bf16[464,256]{1,0:T(8,128)(2,1)S(1)} %collective-permute-done.4.refs_5_.up, bf16[464,256]{1,0:T(8,128)(2,1)S(1)} %collective-permute-done.3.refs_3_.down, bf16[128,256]{1,0:T(8,128)(2,1)S(1)} %copy-done.4, s32[2,256]{1,0:T(2,128)S(1)} %copy-done.5, ...), custom_call_target="tpu_custom_call" | custom-call | flops 1811939328 | bytes 5242880 | tf_op jit(solution)/shard_map/pallas_call | solution.py:44
  102.5 3.9 %collective-permute-done.16 = s16[256,256]{1,0:T(8,128)(2,1)S(1)} collective-permute-done((s16[256,256]{1,0:T(8,128)(2,1)S(1)}, s16[256,256]{1,0:T(8,128)(2,1)S(1)}, u32[]{:S(2)}, u32[]{:S(2)}) %collective-permute-start.16) | collective-permute-done | bytes 131104 | tf_op jit(solution)/shard_map/ppermute | solution.py:475
  106.4 0.1 collective-permute-start.17
  106.5 3.9 %shard_map.89 = bf16[1024,256]{1,0:T(8,128)(2,1)} custom-call(bf16[1024,256]{1,0:T(8,128)(2,1)S(1)} %bitcast.16, bf16[464,256]{1,0:T(8,128)(2,1)S(1)} %collective-permute-done.4.refs_5_.up, bf16[464,256]{1,0:T(8,128)(2,1)S(1)} %collective-permute-done.3.refs_3_.down, bf16[128,256]{1,0:T(8,128)(2,1)S(1)} %copy-done.4, s32[2,256]{1,0:T(2,128)S(1)} %copy-done.5, ...), custom_call_target="tpu_custom_call" | custom-call | flops 1811939328 | bytes 5242880 | tf_op jit(solution)/shard_map/pallas_call | solution.py:44
  110.5 2.4 %collective-permute-done.17 = s16[512,256]{1,0:T(8,128)(2,1)S(1)} collective-permute-done((s16[512,256]{1,0:T(8,128)(2,1)S(1)}, s16[512,256]{1,0:T(8,128)(2,1)S(1)}, u32[]{:S(2)}, u32[]{:S(2)}) %collective-permute-start.17) | collective-permute-done | bytes 262176 | tf_op jit(solution)/shard_map/ppermute | solution.py:475
  112.9 1.5 %collective-permute-start.20 = (s16[512,256]{1,0:T(8,128)(2,1)S(1)}, s16[512,256]{1,0:T(8,128)(2,1)S(1)}, u32[]{:S(2)}, u32[]{:S(2)}) collective-permute-start(s16[512,256]{1,0:T(8,128)(2,1)S(1)} %pad_add_fusion.5), channel_id=1, source_target_pairs={{0,2},{1,3},{2,0},{3,1},{4,6},{5,7},{6,4},{7,5},{8,10},{9,11},{10,... | collective-permute-start | bytes 786440 | tf_op jit(solution)/shard_map/ppermute | solution.py:475
  114.5 0.1 collective-permute-start.18
  114.6 7.6 %collective-permute-done.20 = s16[512,256]{1,0:T(8,128)(2,1)S(1)} collective-permute-done((s16[512,256]{1,0:T(8,128)(2,1)S(1)}, s16[512,256]{1,0:T(8,128)(2,1)S(1)}, u32[]{:S(2)}, u32[]{:S(2)}) %collective-permute-start.20) | collective-permute-done | bytes 262176 | tf_op jit(solution)/shard_map/ppermute | solution.py:475
  122.2 0.1 collective-permute-start.21
  122.3 1.5 %collective-permute-done.18 = s16[512,256]{1,0:T(8,128)(2,1)S(1)} collective-permute-done((s16[512,256]{1,0:T(8,128)(2,1)S(1)}, s16[512,256]{1,0:T(8,128)(2,1)S(1)}, u32[]{:S(2)}, u32[]{:S(2)}) %collective-permute-start.18) | collective-permute-done | bytes 262176 | tf_op jit(solution)/shard_map/ppermute | solution.py:475
  123.8 0.7 collective-permute-start.19
  124.5 0.0 collective-permute-start.24
  124.5 0.5 collective-permute-start.22
  125.0 6.5 %collective-permute-done.21.refs_3_ = s16[1024,256]{1,0:T(8,128)(2,1)S(1)} collective-permute-done((s16[1024,256]{1,0:T(8,128)(2,1)S(1)}, s16[1024,256]{1,0:T(8,128)(2,1)S(1)}, u32[]{:S(2)}, u32[]{:S(2)}) %collective-permute-start.21) | collective-permute-done | bytes 524320 | tf_op jit(solution)/shard_map/ppermute | solution.py:475
  131.5 1.6 %collective-permute-done.19.refs_1_ = s16[1024,256]{1,0:T(8,128)(2,1)S(1)} collective-permute-done((s16[1024,256]{1,0:T(8,128)(2,1)S(1)}, s16[1024,256]{1,0:T(8,128)(2,1)S(1)}, u32[]{:S(2)}, u32[]{:S(2)}) %collective-permute-start.19) | collective-permute-done | bytes 524320 | tf_op jit(solution)/shard_map/ppermute | solution.py:475
  133.1 0.3 collective-permute-done.25.refs_7_
  133.4 1.6 %collective-permute-done.23.refs_5_ = s16[1024,256]{1,0:T(8,128)(2,1)S(1)} collective-permute-done((s16[1024,256]{1,0:T(8,128)(2,1)S(1)}, s16[1024,256]{1,0:T(8,128)(2,1)S(1)}, u32[]{:S(2)}, u32[]{:S(2)}) %collective-permute-start.23) | collective-permute-done | bytes 524320 | tf_op jit(solution)/shard_map/ppermute | solution.py:475
  135.0 3.6 %shard_map.90 = bf16[27,256,256]{2,1,0:T(8,128)(2,1)} custom-call(s32[7]{0:T(128)S(1)} %stack.31.bits_ref.refs_0_, s16[1024,256]{1,0:T(8,128)(2,1)S(1)} %pad_add_fusion.refs_0_, s16[1024,256]{1,0:T(8,128)(2,1)S(1)} %collective-permute-done.19.refs_1_, s16[1024,256]{1,0:T(8,128)(2,1)S(1)} %pad_add_fusion.1.refs_2_, ...), custom_call_target="tpu_custom_call" | custom-call | tf_op jit(solution)/shard_map/pallas_call | solution.py:44
  (24 shorter events, 0.2 us)
Async XLA Ops:
  0.6 28.0 %copy-start = (bf16[1,1024,256]{2,1,0:T(8,128)(2,1)S(1)}, bf16[1,1024,256]{2,1,0:T(8,128)(2,1)}, u32[]{:S(2)}) copy-start(bf16[1,1024,256]{2,1,0:T(8,128)(2,1)} %param.9) | copy-start | bytes 1572868
  5.6 44.0 %copy-start.5 = (s32[2,256]{1,0:T(2,128)S(1)}, s32[2,256]{1,0:T(2,128)}, u32[]{:S(2)}) copy-start(s32[2,256]{1,0:T(2,128)} %get-tuple-element.64.ekey) | copy-start | bytes 6148
  5.6 14.9 %collective-permute-start = (bf16[272,256]{1,0:T(8,128)(2,1)}, bf16[272,256]{1,0:T(8,128)(2,1)S(1)}, u32[]{:S(2)}, u32[]{:S(2)}) collective-permute-start(bf16[272,256]{1,0:T(8,128)(2,1)} %get-tuple-element.49), channel_id=1, source_target_pairs={{0,16},{4,20},{8,24},{12,28},{16,0},{20,4},{24,8},{28,12},{1,17},{... | collective-permute-start | bytes 417800 | tf_op jit(solution)/shard_map/ppermute | solution.py:543
  9.7 18.9 %collective-permute-start.1 = (bf16[272,256]{1,0:T(8,128)(2,1)}, bf16[272,256]{1,0:T(8,128)(2,1)S(1)}, u32[]{:S(2)}, u32[]{:S(2)}) collective-permute-start(bf16[272,256]{1,0:T(8,128)(2,1)} %get-tuple-element.50), channel_id=1, source_target_pairs={{0,20},{4,24},{8,28},{12,0},{16,4},{20,8},{24,12},{28,16},{1,21},{... | collective-permute-start | bytes 417800 | tf_op jit(solution)/shard_map/ppermute | solution.py:543
  11.0 25.0 %collective-permute-start.3 = (bf16[464,256]{1,0:T(8,128)(2,1)}, bf16[464,256]{1,0:T(8,128)(2,1)S(1)}, u32[]{:S(2)}, u32[]{:S(2)}) collective-permute-start(bf16[464,256]{1,0:T(8,128)(2,1)} %get-tuple-element.52), channel_id=1, source_target_pairs={{0,28},{4,0},{8,4},{12,8},{16,12},{20,16},{24,20},{28,24},{1,29},{... | collective-permute-start | bytes 712712 | tf_op jit(solution)/shard_map/ppermute | solution.py:543
  12.2 23.9 %collective-permute-start.4 = (bf16[464,256]{1,0:T(8,128)(2,1)}, bf16[464,256]{1,0:T(8,128)(2,1)S(1)}, u32[]{:S(2)}, u32[]{:S(2)}) collective-permute-start(bf16[464,256]{1,0:T(8,128)(2,1)} %get-tuple-element.56), channel_id=1, source_target_pairs={{0,4},{4,8},{8,12},{12,16},{16,20},{20,24},{24,28},{28,0},{1,5},{5... | collective-permute-start | bytes 712712 | tf_op jit(solution)/shard_map/ppermute | solution.py:543
  13.1 17.4 %collective-permute-start.2 = (bf16[272,256]{1,0:T(8,128)(2,1)}, bf16[272,256]{1,0:T(8,128)(2,1)S(1)}, u32[]{:S(2)}, u32[]{:S(2)}) collective-permute-start(bf16[272,256]{1,0:T(8,128)(2,1)} %get-tuple-element.51), channel_id=1, source_target_pairs={{0,24},{4,28},{8,0},{12,4},{16,8},{20,12},{24,16},{28,20},{1,25},{... | collective-permute-start | bytes 417800 | tf_op jit(solution)/shard_map/ppermute | solution.py:543
  20.5 15.5 %collective-permute-start.5 = (bf16[272,256]{1,0:T(8,128)(2,1)}, bf16[272,256]{1,0:T(8,128)(2,1)S(1)}, u32[]{:S(2)}, u32[]{:S(2)}) collective-permute-start(bf16[272,256]{1,0:T(8,128)(2,1)} %get-tuple-element.57), channel_id=1, source_target_pairs={{0,8},{4,12},{8,16},{12,20},{16,24},{20,28},{24,0},{28,4},{1,9},{5... | collective-permute-start | bytes 417800 | tf_op jit(solution)/shard_map/ppermute | solution.py:543
  28.6 7.5 %collective-permute-start.6 = (bf16[272,256]{1,0:T(8,128)(2,1)}, bf16[272,256]{1,0:T(8,128)(2,1)S(1)}, u32[]{:S(2)}, u32[]{:S(2)}) collective-permute-start(bf16[272,256]{1,0:T(8,128)(2,1)} %get-tuple-element.58), channel_id=1, source_target_pairs={{0,12},{4,16},{8,20},{12,24},{16,28},{20,0},{24,4},{28,8},{1,13},{... | collective-permute-start | bytes 417800 | tf_op jit(solution)/shard_map/ppermute | solution.py:543
  28.6 0.9 copy-start.1
  29.5 0.7 copy-start.2
  37.6 7.8 %collective-permute-start.7 = (bf16[192,256]{1,0:T(8,128)(2,1)S(1)}, bf16[192,256]{1,0:T(8,128)(2,1)S(1)}, u32[]{:S(2)}, u32[]{:S(2)}) collective-permute-start(bf16[192,256]{1,0:T(8,128)(2,1)S(1)} %get-tuple-element.61), channel_id=1, source_target_pairs={{0,4},{4,8},{8,12},{12,16},{16,20},{20,24},{24,28},{1,5},{5,9},{9,... | collective-permute-start | bytes 294920 | tf_op jit(solution)/shard_map/ppermute | solution.py:491
  43.1 6.5 %collective-permute-start.8 = (bf16[192,256]{1,0:T(8,128)(2,1)S(1)}, bf16[192,256]{1,0:T(8,128)(2,1)S(1)}, u32[]{:S(2)}, u32[]{:S(2)}) collective-permute-start(bf16[192,256]{1,0:T(8,128)(2,1)S(1)} %get-tuple-element.62), channel_id=1, source_target_pairs={{4,0},{8,4},{12,8},{16,12},{20,16},{24,20},{28,24},{5,1},{9,5},{13... | collective-permute-start | bytes 294920 | tf_op jit(solution)/shard_map/ppermute | solution.py:491
  54.6 2.5 %collective-permute-start.9 = (s16[1808,256]{1,0:T(8,128)(2,1)S(1)}, s16[1808,256]{1,0:T(8,128)(2,1)S(1)}, u32[]{:S(2)}, u32[]{:S(2)}) collective-permute-start(s16[1808,256]{1,0:T(8,128)(2,1)S(1)} %shard_map.80), channel_id=1, source_target_pairs={{0,1},{1,0},{2,3},{3,2},{4,5},{5,4},{6,7},{7,6},{8,9},{9,8},{10,11... | collective-permute-start | bytes 2777096 | tf_op jit(solution)/shard_map/ppermute | solution.py:475
  54.7 5.9 %collective-permute-start.10 = (s16[1808,256]{1,0:T(8,128)(2,1)S(1)}, s16[1808,256]{1,0:T(8,128)(2,1)S(1)}, u32[]{:S(2)}, u32[]{:S(2)}) collective-permute-start(s16[1808,256]{1,0:T(8,128)(2,1)S(1)} %get-tuple-element.70), channel_id=1, source_target_pairs={{0,1},{1,0},{2,3},{3,2},{4,5},{5,4},{6,7},{7,6},{8,9},{9,8},{10,11... | collective-permute-start | bytes 2777096 | tf_op jit(solution)/shard_map/ppermute | solution.py:475
  59.0 10.7 %collective-permute-start.12 = (s16[912,256]{1,0:T(8,128)(2,1)S(1)}, s16[912,256]{1,0:T(8,128)(2,1)S(1)}, u32[]{:S(2)}, u32[]{:S(2)}) collective-permute-start(s16[912,256]{1,0:T(8,128)(2,1)S(1)} %get-tuple-element.72), channel_id=1, source_target_pairs={{0,2},{1,5},{2,0},{3,7},{4,6},{5,1},{6,4},{7,3},{8,10},{9,13},{10,... | collective-permute-start | bytes 1400840 | tf_op jit(solution)/shard_map/ppermute | solution.py:486
  62.5 10.2 %collective-permute-start.11 = (s16[912,256]{1,0:T(8,128)(2,1)S(1)}, s16[912,256]{1,0:T(8,128)(2,1)S(1)}, u32[]{:S(2)}, u32[]{:S(2)}) collective-permute-start(s16[912,256]{1,0:T(8,128)(2,1)S(1)} %get-tuple-element.71), channel_id=1, source_target_pairs={{0,2},{1,5},{2,0},{3,7},{4,6},{5,1},{6,4},{7,3},{8,10},{9,13},{10,... | collective-permute-start | bytes 1400840 | tf_op jit(solution)/shard_map/ppermute | solution.py:486
  69.7 29.9 %copy-start.3 = (bf16[27,256,256]{2,1,0:T(8,128)(2,1)S(1)}, bf16[27,256,256]{2,1,0:T(8,128)(2,1)}, u32[]{:S(2)}) copy-start(bf16[27,256,256]{2,1,0:T(8,128)(2,1)} %weight_ref.5) | copy-start | bytes 10616836
  69.7 29.9 %copy-start.4 = (bf16[128,256]{1,0:T(8,128)(2,1)S(1)}, bf16[128,256]{1,0:T(8,128)(2,1)}, u32[]{:S(2)}) copy-start(bf16[128,256]{1,0:T(8,128)(2,1)} %get-tuple-element.89.local) | copy-start | bytes 196612
  73.7 9.0 %collective-permute-start.13 = (s16[912,256]{1,0:T(8,128)(2,1)S(1)}, s16[912,256]{1,0:T(8,128)(2,1)S(1)}, u32[]{:S(2)}, u32[]{:S(2)}) collective-permute-start(s16[912,256]{1,0:T(8,128)(2,1)S(1)} %get-tuple-element.79), channel_id=1, source_target_pairs={{0,4},{1,3},{2,6},{3,1},{4,0},{5,7},{6,2},{7,5},{8,12},{9,11},{10,... | collective-permute-start | bytes 1400840 | tf_op jit(solution)/shard_map/ppermute | solution.py:486
  83.5 6.5 %collective-permute-start.14 = (s16[464,256]{1,0:T(8,128)(2,1)S(1)}, s16[464,256]{1,0:T(8,128)(2,1)S(1)}, u32[]{:S(2)}, u32[]{:S(2)}) collective-permute-start(s16[464,256]{1,0:T(8,128)(2,1)S(1)} %get-tuple-element.81), channel_id=1, source_target_pairs={{0,8},{4,12},{8,0},{12,4},{16,24},{20,28},{24,16},{28,20},{1,9},{5... | collective-permute-start | bytes 712712 | tf_op jit(solution)/shard_map/ppermute | solution.py:475
  90.8 8.5 %collective-permute-start.15 = (s16[240,256]{1,0:T(8,128)(2,1)S(1)}, s16[240,256]{1,0:T(8,128)(2,1)S(1)}, u32[]{:S(2)}, u32[]{:S(2)}) collective-permute-start(s16[240,256]{1,0:T(8,128)(2,1)S(1)} %get-tuple-element.83), channel_id=1, source_target_pairs={{0,16},{4,20},{8,24},{12,28},{16,0},{20,4},{24,8},{28,12},{1,17},{... | collective-permute-start | bytes 368648 | tf_op jit(solution)/shard_map/ppermute | solution.py:475
  99.5 6.9 %collective-permute-start.16 = (s16[256,256]{1,0:T(8,128)(2,1)S(1)}, s16[256,256]{1,0:T(8,128)(2,1)S(1)}, u32[]{:S(2)}, u32[]{:S(2)}) collective-permute-start(s16[256,256]{1,0:T(8,128)(2,1)S(1)} %pad_add_fusion.6), channel_id=1, source_target_pairs={{0,16},{4,20},{8,24},{12,28},{16,0},{20,4},{24,8},{28,12},{1,17},{... | collective-permute-start | bytes 393224 | tf_op jit(solution)/shard_map/ppermute | solution.py:475
  106.4 6.4 %collective-permute-start.17 = (s16[512,256]{1,0:T(8,128)(2,1)S(1)}, s16[512,256]{1,0:T(8,128)(2,1)S(1)}, u32[]{:S(2)}, u32[]{:S(2)}) collective-permute-start(s16[512,256]{1,0:T(8,128)(2,1)S(1)} %pad_add_fusion.2), channel_id=1, source_target_pairs={{0,8},{4,12},{8,0},{12,4},{16,24},{20,28},{24,16},{28,20},{1,9},{5... | collective-permute-start | bytes 786440 | tf_op jit(solution)/shard_map/ppermute | solution.py:475
  112.9 9.2 %collective-permute-start.20 = (s16[512,256]{1,0:T(8,128)(2,1)S(1)}, s16[512,256]{1,0:T(8,128)(2,1)S(1)}, u32[]{:S(2)}, u32[]{:S(2)}) collective-permute-start(s16[512,256]{1,0:T(8,128)(2,1)S(1)} %pad_add_fusion.5), channel_id=1, source_target_pairs={{0,2},{1,3},{2,0},{3,1},{4,6},{5,7},{6,4},{7,5},{8,10},{9,11},{10,... | collective-permute-start | bytes 786440 | tf_op jit(solution)/shard_map/ppermute | solution.py:475
  114.5 9.3 %collective-permute-start.18 = (s16[512,256]{1,0:T(8,128)(2,1)S(1)}, s16[512,256]{1,0:T(8,128)(2,1)S(1)}, u32[]{:S(2)}, u32[]{:S(2)}) collective-permute-start(s16[512,256]{1,0:T(8,128)(2,1)S(1)} %pad_add_fusion.4), channel_id=1, source_target_pairs={{0,4},{4,0},{8,12},{12,8},{16,20},{20,16},{24,28},{28,24},{1,5},{5... | collective-permute-start | bytes 786440 | tf_op jit(solution)/shard_map/ppermute | solution.py:475
  122.2 9.2 %collective-permute-start.21 = (s16[1024,256]{1,0:T(8,128)(2,1)S(1)}, s16[1024,256]{1,0:T(8,128)(2,1)S(1)}, u32[]{:S(2)}, u32[]{:S(2)}) collective-permute-start(s16[1024,256]{1,0:T(8,128)(2,1)S(1)} %pad_add_fusion.1.refs_2_), channel_id=1, source_target_pairs={{0,4},{4,0},{8,12},{12,8},{16,20},{20,16},{24,28},{28,24},{1,5},{5... | collective-permute-start | bytes 1572872 | tf_op jit(solution)/shard_map/ppermute | solution.py:475
  123.8 9.2 %collective-permute-start.19 = (s16[1024,256]{1,0:T(8,128)(2,1)S(1)}, s16[1024,256]{1,0:T(8,128)(2,1)S(1)}, u32[]{:S(2)}, u32[]{:S(2)}) collective-permute-start(s16[1024,256]{1,0:T(8,128)(2,1)S(1)} %pad_add_fusion.refs_0_), channel_id=1, source_target_pairs={{0,2},{1,3},{2,0},{3,1},{4,6},{5,7},{6,4},{7,5},{8,10},{9,11},{10,... | collective-permute-start | bytes 1572872 | tf_op jit(solution)/shard_map/ppermute | solution.py:475
  124.5 8.6 %collective-permute-start.24 = (s16[1024,256]{1,0:T(8,128)(2,1)S(1)}, s16[1024,256]{1,0:T(8,128)(2,1)S(1)}, u32[]{:S(2)}, u32[]{:S(2)}) collective-permute-start(s16[1024,256]{1,0:T(8,128)(2,1)S(1)} %pad_add_fusion.1.refs_2_), channel_id=1, source_target_pairs={{0,1},{1,0},{2,3},{3,2},{4,5},{5,4},{6,7},{7,6},{8,9},{9,8},{10,11... | collective-permute-start | bytes 1572872 | tf_op jit(solution)/shard_map/ppermute | solution.py:475
  124.5 8.6 %collective-permute-start.22 = (s16[1024,256]{1,0:T(8,128)(2,1)S(1)}, s16[1024,256]{1,0:T(8,128)(2,1)S(1)}, u32[]{:S(2)}, u32[]{:S(2)}) collective-permute-start(s16[1024,256]{1,0:T(8,128)(2,1)S(1)} %pad_add_fusion.refs_0_), channel_id=1, source_target_pairs={{0,1},{1,0},{2,3},{3,2},{4,5},{5,4},{6,7},{7,6},{8,9},{9,8},{10,11... | collective-permute-start | bytes 1572872 | tf_op jit(solution)/shard_map/ppermute | solution.py:475
  131.5 1.9 %collective-permute-start.25 = (s16[1024,256]{1,0:T(8,128)(2,1)S(1)}, s16[1024,256]{1,0:T(8,128)(2,1)S(1)}, u32[]{:S(2)}, u32[]{:S(2)}) collective-permute-start(s16[1024,256]{1,0:T(8,128)(2,1)S(1)} %collective-permute-done.21.refs_3_), channel_id=1, source_target_pairs={{0,1},{1,0},{2,3},{3,2},{4,5},{5,4},{6,7},{7,6},{8,9},{9,8},{10,11... | collective-permute-start | bytes 1572872 | tf_op jit(solution)/shard_map/ppermute | solution.py:475
  133.0 1.9 %collective-permute-start.23 = (s16[1024,256]{1,0:T(8,128)(2,1)S(1)}, s16[1024,256]{1,0:T(8,128)(2,1)S(1)}, u32[]{:S(2)}, u32[]{:S(2)}) collective-permute-start(s16[1024,256]{1,0:T(8,128)(2,1)S(1)} %collective-permute-done.19.refs_1_), channel_id=1, source_target_pairs={{0,1},{1,0},{2,3},{3,2},{4,5},{5,4},{6,7},{7,6},{8,9},{9,8},{10,11... | collective-permute-start | bytes 1572872 | tf_op jit(solution)/shard_map/ppermute | solution.py:475
